TPU v7x, 32 devices: a whole 2x2x4 slice. The times are simulated.
32 devices in a mesh: groups: 2 (over y), src: 16 (over z, x, core).
Axes of the slice: x: 2, y: 2, z: 4, core: 2. Of those that a mesh axis runs over, the one named last changes fastest.
Arguments:
- src_points: bfloat16 [256, 64, 256], P(('groups', 'src')), parts along dimension 0, may hold values from -1.5 to 1.5
- tgt_points: bfloat16 [256, 64, 256], P(('groups', 'src')), parts along dimension 0, may hold values from -1.5 to 1.5
- g_init: float32 [256, 256], P(('groups', 'src')), parts along dimension 0, may hold values from 2 to 66
- far_src: float32 [256, 256], P(('groups', 'src')), parts along dimension 0, may hold values from 10 to 22
- far_tgt: float32 [256, 256], P(('groups', 'src')), parts along dimension 0, may hold values from -160 to -14
- cand_owner: int32 [256, 8], P(('groups', 'src')), parts along dimension 0, may hold values from 0 to 15, all different within a row; in each aligned block of 8 rows (0 to 7, 8 to 15, ...) at most 4 rows name the same one
- cand_local: int32 [256, 8], P(('groups', 'src')), parts along dimension 0, may hold values from 0 to 7
Outputs:
- src_potential: float32 [256, 256], P(('groups', 'src')), parts along dimension 0
- tgt_potential: float32 [256, 256], P(('groups', 'src')), parts along dimension 0
There are 2 independent parts, one for each index of `groups`. A program takes and returns all parts, laid end to end along the dimension named above; each array names one. Nothing has to cross between parts.
Inputs may be any that keep to these rules, and one draw needn't show every extreme that they name: `cand_owner`: each source cluster names 8 different shards; among the 8 source clusters of one device at most 4 name the same shard, and in every draw some device names some shard exactly 4 times.
All inputs are finite; a program needn't handle non-finite values.
Results may differ from a plain program's by a relative error of at most 0.0003.
Values may be sent and summed in bfloat16 or wider, within the bound.
No kernel may reach another device: no remote copies, remote signals or barrier semaphores. Data moves between devices by JAX's collectives and lax.ppermute only.
A program may use at most 64 MiB of HBM per device.

v0:
```python
import jax
import jax.numpy as jnp
from jax import lax
from jax.sharding import PartitionSpec as P

ITERS = 2


SCALE_EPS = 0.25
KEEP_TAU = 0.8
VERY_LOW = -1e30


def half_norms(blocks):
    wide = blocks.astype(jnp.float32)
    return 0.5 * jnp.sum(wide * wide, axis=-2)


def per_device(src_points, tgt_points, g_init, far_src, far_tgt, cand_owner, cand_local):
    src_count, feature_dim, cluster_size = src_points.shape
    tgt_count = tgt_points.shape[0]
    per_cluster = cand_owner.shape[1]
    shards = lax.axis_size("src")
    capacity = max(2, min(src_count // 2, 2 * src_count * per_cluster // shards))
    requests = src_count * per_cluster
    slot_count = shards * capacity
    group_size = 4
    group_count = src_count // group_size
    owners = cand_owner.reshape(requests)
    wanted = cand_local.reshape(requests)
    onehot = (owners[:, None] == jnp.arange(shards, dtype=jnp.int32)[None, :]).astype(jnp.int32)
    earlier = jnp.cumsum(onehot, axis=0) - onehot
    within = jnp.sum(earlier * onehot, axis=1)
    slot_pos = owners * capacity + within
    request_table = jnp.full((slot_count,), -1, jnp.int32).at[slot_pos].set(wanted)
    asked_ids = lax.all_to_all(
        request_table.reshape(shards, capacity), "src", split_axis=0, concat_axis=0, tiled=True
    ).reshape(slot_count)
    safe_ids = jnp.maximum(asked_ids, 0)
    member = (asked_ids[:, None] == jnp.arange(tgt_count, dtype=jnp.int32)[None, :]).astype(
        jnp.float32
    )
    member_rows = member.T
    send_points = tgt_points[safe_ids].reshape(shards, capacity, feature_dim, cluster_size)
    src_half = half_norms(src_points)
    src_grouped = src_points.reshape(group_count, group_size, feature_dim, cluster_size)
    half_grouped = src_half.reshape(group_count, group_size, cluster_size)
    far_grouped = far_src.reshape(group_count, group_size, cluster_size)

    def tile_cost(src_block, src_norm, tgt_block, tgt_norm):
        inner = jnp.einsum(
            "gdp,gkdq->gpkq", src_block, tgt_block, preferred_element_type=jnp.float32
        )
        return src_norm[:, :, None, None] + tgt_norm[:, None, :, :] - inner

    def row_pass(blocks, block_half, req_pot):

        def row_one_group(pieces):
            src_block, src_norm, tgt_block, tgt_norm, tgt_values, far_term = pieces
            cost = tile_cost(src_block, src_norm, tgt_block, tgt_norm)
            scores = (tgt_values[:, None, :, :] - cost) / SCALE_EPS
            highest = jnp.maximum(jnp.max(scores, axis=(2, 3)), far_term)
            total = jnp.exp(far_term - highest) + jnp.sum(
                jnp.exp(scores - highest[:, :, None, None]), axis=(2, 3)
            )
            return -KEEP_TAU * SCALE_EPS * (highest + jnp.log(total))

        pieces = (
            src_grouped,
            half_grouped,
            blocks.reshape(group_count, group_size, per_cluster, feature_dim, cluster_size),
            block_half.reshape(group_count, group_size, per_cluster, cluster_size),
            req_pot.reshape(group_count, group_size, per_cluster, cluster_size),
            far_grouped,
        )
        return lax.map(row_one_group, pieces).reshape(src_count, cluster_size)

    def column_pass(blocks, block_half, src_pot):

        def column_one_group(pieces):
            src_block, src_norm, tgt_block, tgt_norm, src_values = pieces
            cost = tile_cost(src_block, src_norm, tgt_block, tgt_norm)
            scores = (src_values[:, :, None, None] - cost) / SCALE_EPS
            highest = jnp.max(scores, axis=1)
            total = jnp.sum(jnp.exp(scores - highest[:, None, :, :]), axis=1)
            return (highest, total)

        pieces = (
            src_grouped,
            half_grouped,
            blocks.reshape(group_count, group_size, per_cluster, feature_dim, cluster_size),
            block_half.reshape(group_count, group_size, per_cluster, cluster_size),
            src_pot.reshape(group_count, group_size, cluster_size),
        )
        col_high, col_total = lax.map(column_one_group, pieces)
        col_high = col_high.reshape(requests, cluster_size)
        col_total = col_total.reshape(requests, cluster_size)
        send_high = (
            jnp.full((slot_count, cluster_size), VERY_LOW, jnp.float32).at[slot_pos].set(col_high)
        )
        send_total = jnp.zeros((slot_count, cluster_size), jnp.float32).at[slot_pos].set(col_total)
        back_high, back_total = (
            lax.all_to_all(
                send_high.reshape(shards, capacity, cluster_size),
                "src",
                split_axis=0,
                concat_axis=0,
                tiled=True,
            ),
            lax.all_to_all(
                send_total.reshape(shards, capacity, cluster_size),
                "src",
                split_axis=0,
                concat_axis=0,
                tiled=True,
            ),
        )
        back_high = back_high.reshape(slot_count, cluster_size)
        back_total = back_total.reshape(slot_count, cluster_size)

        def cluster_best(column):
            return jnp.max(jnp.where(column[:, None] > 0.5, back_high, VERY_LOW), axis=0)

        best = jnp.maximum(far_tgt, lax.map(cluster_best, member_rows))
        weights = back_total * jnp.exp(back_high - best[safe_ids])
        summed = jnp.exp(far_tgt - best) + jnp.dot(
            member_rows, weights, precision=lax.Precision.HIGHEST
        )
        return -KEEP_TAU * SCALE_EPS * (best + jnp.log(summed))

    tgt_pot = g_init
    src_pot = jnp.zeros((src_count, cluster_size), jnp.float32)
    for iteration in range(ITERS):
        flattened = lax.all_to_all(
            send_points, "src", split_axis=0, concat_axis=0, tiled=True
        ).reshape(slot_count, feature_dim, cluster_size)
        chosen = flattened[slot_pos]
        blocks = chosen
        block_half = half_norms(chosen)
        send_pot = tgt_pot[safe_ids].reshape(shards, capacity, cluster_size)
        got_pot = lax.all_to_all(send_pot, "src", split_axis=0, concat_axis=0, tiled=True)
        req_pot = got_pot.reshape(slot_count, cluster_size)[slot_pos]
        src_pot = row_pass(blocks, block_half, req_pot)
        tgt_pot = column_pass(blocks, block_half, src_pot)
    return (src_pot, tgt_pot)


def solution(mesh):
    return jax.shard_map(
        per_device,
        mesh=mesh,
        in_specs=(
            P(("groups", "src"), None, None),
            P(("groups", "src"), None, None),
            P(("groups", "src"), None),
            P(("groups", "src"), None),
            P(("groups", "src"), None),
            P(("groups", "src"), None),
            P(("groups", "src"), None),
        ),
        out_specs=(P(("groups", "src"), None), P(("groups", "src"), None)),
        check_vma=False,
    )
```

profile of v0, /device:TPU:0, one launch (start us, length us, event | category | flops | bytes accessed | tf_op | source)
XLA Modules:
  0.0 192.3 jit_solution(4724374246698592759)
XLA Ops:
  4.3 13.6 %all_to_all.45 = s32[16,1,4]{2,1,0:T(1,128)S(1)} all-to-all(s32[16,1,4]{2,1,0:T(1,128)S(1)} %bitcast.212), channel_id=1, replica_groups=mesh['groups'=2,'src'=16] {'src'}, dimensions={0} | all-to-all | bytes 512 | tf_op jit(solution)/shard_map/all_to_all | solution.py:36
  21.1 3.5 %all-to-all-start.1 = ((f32[16,4,256]{2,1,0:T(4,128)}), f32[16,4,256]{2,1,0:T(4,128)S(1)}, u32[]{:S(2)}, u32[]{:S(2)}) async-start(f32[16,4,256]{2,1,0:T(4,128)} %reshape.209), calls=%async_computation.1 | async-start | bytes 131072 | tf_op jit(solution)/shard_map/all_to_all | solution.py:141
  26.7 4.8 %all-to-all-done.1 = f32[16,4,256]{2,1,0:T(4,128)S(1)} async-done(((f32[16,4,256]{2,1,0:T(4,128)}), f32[16,4,256]{2,1,0:T(4,128)S(1)}, u32[]{:S(2)}, u32[]{:S(2)}) %all-to-all-start.1) | async-done | bytes 65568 | tf_op jit(solution)/shard_map/all_to_all | solution.py:141
  31.5 3.7 %all-to-all-start.2 = ((bf16[16,4,64,256]{3,2,1,0:T(8,128)(2,1)}), bf16[16,4,64,256]{3,2,1,0:T(8,128)(2,1)S(1)}, u32[]{:S(2)}, u32[]{:S(2)}) async-start(bf16[16,4,64,256]{3,2,1,0:T(8,128)(2,1)} %bitcast.46), calls=%async_computation.2 | async-start | bytes 4194304 | tf_op jit(solution)/shard_map/all_to_all | solution.py:134
  36.1 40.1 %all-to-all-done.2 = bf16[16,4,64,256]{3,2,1,0:T(8,128)(2,1)S(1)} async-done(((bf16[16,4,64,256]{3,2,1,0:T(8,128)(2,1)}), bf16[16,4,64,256]{3,2,1,0:T(8,128)(2,1)S(1)}, u32[]{:S(2)}, u32[]{:S(2)}) %all-to-all-start.2) | async-done | bytes 2097184 | tf_op jit(solution)/shard_map/all_to_all | solution.py:134
  77.6 2.3 %gather_fusion.3 = bf16[64,64,256]{2,1,0:T(8,128)(2,1)S(1)} fusion(bf16[64,64,256]{2,1,0:T(8,128)(2,1)} %bitcast.201, s32[1024]{0:T(1024)S(1)} %pad_clamp_fusion), kind=kCustom, calls=%fused_computation.3 | custom fusion | bytes 4194560 | tf_op jit(solution)/shard_map/gather | solution.py:137
  80.6 11.7 %while.64 = (s32[]{:T(128)}, f32[2,4,256]{2,1,0:T(4,128)S(1)}, f32[2,4,8,256]{3,2,1,0:T(8,128)S(1)}, f32[2,4,256]{2,1,0:T(4,128)S(1)}, f32[2,4,8,256]{3,2,1,0:T(...) while((s32[]{:T(128)}, f32[2,4,256]{2,1,0:T(4,128)S(1)}, ...), condition=%wide.region_8.9_spmd, body=%wide.region_5.8_spmd.sunk | while | flops 291508224 | bytes 18277484 | solution.py:76
  80.6 3.2 %fusion.69 = (f32[4,256]{1,0:T(4,128)S(1)}, f32[4,256,8,256]{1,3,2,0:T(8,128)S(1)}) fusion(f32[4,8,256]{2,1,0:T(8,128)S(1)} %get-tuple-element.552, f32[4,256]{1,0:T(4,128)S(1)} %dynamic-slice_bitcast_fusion.23, f32[4,8,256]{2,1,0:T(8,128)S(1)} %get-tuple-element.553, bf16[2,4,8,64,256]{4,3,2,1,0:T(8,128)(2,1)S(1)} %get-tuple-element.624, ...), kind=kOutput, calls=%fused_computation.15.clone.1 | convolution fusion | flops 278920192 | bytes 9643008 | tf_op jit(solution)/shard_map/while/body/eval_jaxpr/gdp,gkdq->gpkq/dot_general | solution.py:51
  83.8 2.6 %exponential_reduce_fusion.8 = f32[4,256]{1,0:T(4,128)S(1)} fusion(f32[4,256,8,256]{1,3,2,0:T(8,128)S(1)} %get-tuple-element.554, f32[4,256]{1,0:T(4,128)S(1)} %bitcast_maximum_fusion.6, f32[4,8,256]{2,1,0:T(8,128)S(1)} %get-tuple-element.552, f32[4,256]{1,0:T(4,128)S(1)} %dynamic-slice_bitcast_fusion.23, f32[4,8,256]{2,1,0:T(8,128)S(1)} %get-tuple-element.553), kind=kLoop, calls=%fused_computation.13.clone.1 | loop fusion | flops 12581888 | bytes 8466432 | tf_op jit(solution)/shard_map/while/body/eval_jaxpr/reduce_sum | solution.py:63
  86.5 3.2 %fusion.69 = (f32[4,256]{1,0:T(4,128)S(1)}, f32[4,256,8,256]{1,3,2,0:T(8,128)S(1)}) fusion(f32[4,8,256]{2,1,0:T(8,128)S(1)} %get-tuple-element.552, f32[4,256]{1,0:T(4,128)S(1)} %dynamic-slice_bitcast_fusion.23, f32[4,8,256]{2,1,0:T(8,128)S(1)} %get-tuple-element.553, bf16[2,4,8,64,256]{4,3,2,1,0:T(8,128)(2,1)S(1)} %get-tuple-element.624, ...), kind=kOutput, calls=%fused_computation.15.clone.1 | convolution fusion | flops 278920192 | bytes 9643008 | tf_op jit(solution)/shard_map/while/body/eval_jaxpr/gdp,gkdq->gpkq/dot_general | solution.py:51
  89.6 2.6 %exponential_reduce_fusion.8 = f32[4,256]{1,0:T(4,128)S(1)} fusion(f32[4,256,8,256]{1,3,2,0:T(8,128)S(1)} %get-tuple-element.554, f32[4,256]{1,0:T(4,128)S(1)} %bitcast_maximum_fusion.6, f32[4,8,256]{2,1,0:T(8,128)S(1)} %get-tuple-element.552, f32[4,256]{1,0:T(4,128)S(1)} %dynamic-slice_bitcast_fusion.23, f32[4,8,256]{2,1,0:T(8,128)S(1)} %get-tuple-element.553), kind=kLoop, calls=%fused_computation.13.clone.1 | loop fusion | flops 12581888 | bytes 8466432 | tf_op jit(solution)/shard_map/while/body/eval_jaxpr/reduce_sum | solution.py:63
  92.3 11.3 %while.65 = (s32[]{:T(128)}, f32[2,4,8,256]{3,2,1,0:T(8,128)S(1)}, f32[2,4,8,256]{3,2,1,0:T(8,128)S(1)}, f32[2,4,256]{2,1,0:T(4,128)S(1)}, f32[2,4,256]{2,1,0:T(...) while((s32[]{:T(128)}, f32[2,4,8,256]{3,2,1,0:T(8,128)S(1)}, ...), condition=%wide.region_12.13_spmd, body=%wide.region_9.12_spmd.sunk | while | flops 291487744 | bytes 18351212 | solution.py:95
  94.4 3.6 %exponential_reduce_fusion.9 = f32[4,8,256]{2,1,0:T(8,128)S(1)} fusion(f32[4,256,8,256]{3,1,2,0:T(8,128)S(1)} %get-tuple-element.564, f32[4,8,256]{2,1,0:T(8,128)S(1)} %get-tuple-element.565, f32[4,8,256]{2,1,0:T(8,128)S(1)} %dynamic-slice_bitcast_fusion.24, f32[4,256]{1,0:T(4,128)S(1)} %dynamic-slice_bitcast_fusion.25, ...), kind=kLoop, calls=%fused_computation.32.clone.1 | loop fusion | flops 12574720 | bytes 8495104 | tf_op jit(solution)/shard_map/while/body/eval_jaxpr/reduce_sum | solution.py:85
  100.0 3.6 %exponential_reduce_fusion.9 = f32[4,8,256]{2,1,0:T(8,128)S(1)} fusion(f32[4,256,8,256]{3,1,2,0:T(8,128)S(1)} %get-tuple-element.564, f32[4,8,256]{2,1,0:T(8,128)S(1)} %get-tuple-element.565, f32[4,8,256]{2,1,0:T(8,128)S(1)} %dynamic-slice_bitcast_fusion.24, f32[4,256]{1,0:T(4,128)S(1)} %dynamic-slice_bitcast_fusion.25, ...), kind=kLoop, calls=%fused_computation.32.clone.1 | loop fusion | flops 12574720 | bytes 8495104 | tf_op jit(solution)/shard_map/while/body/eval_jaxpr/reduce_sum | solution.py:85
  105.1 11.2 %all-to-all-start.3 = ((f32[16,4,256]{2,1,0:T(4,128)}), f32[16,4,256]{2,1,0:T(4,128)S(1)}, u32[]{:S(2)}, u32[]{:S(2)}) async-start(f32[16,4,256]{2,1,0:T(4,128)} %reshape.218), calls=%async_computation.3 | async-start | bytes 131072 | tf_op jit(solution)/shard_map/all_to_all | solution.py:103
  117.8 5.4 %all-to-all-done.3 = f32[16,4,256]{2,1,0:T(4,128)S(1)} async-done(((f32[16,4,256]{2,1,0:T(4,128)}), f32[16,4,256]{2,1,0:T(4,128)S(1)}, u32[]{:S(2)}, u32[]{:S(2)}) %all-to-all-start.3) | async-done | bytes 65568 | tf_op jit(solution)/shard_map/all_to_all | solution.py:103
  123.2 3.5 %all-to-all-start.4 = ((f32[16,4,256]{2,1,0:T(4,128)}), f32[16,4,256]{2,1,0:T(4,128)S(1)}, u32[]{:S(2)}, u32[]{:S(2)}) async-start(f32[16,4,256]{2,1,0:T(4,128)} %reshape.221), calls=%async_computation.4 | async-start | bytes 131072 | tf_op jit(solution)/shard_map/all_to_all | solution.py:110
  128.8 4.8 %all-to-all-done.4 = f32[16,4,256]{2,1,0:T(4,128)S(1)} async-done(((f32[16,4,256]{2,1,0:T(4,128)}), f32[16,4,256]{2,1,0:T(4,128)S(1)}, u32[]{:S(2)}, u32[]{:S(2)}) %all-to-all-start.4) | async-done | bytes 65568 | tf_op jit(solution)/shard_map/all_to_all | solution.py:110
  135.2 3.7 %all-to-all-start.5 = ((f32[16,4,256]{2,1,0:T(4,128)}), f32[16,4,256]{2,1,0:T(4,128)S(1)}, u32[]{:S(2)}, u32[]{:S(2)}) async-start(f32[16,4,256]{2,1,0:T(4,128)} %reshape.223), calls=%async_computation.5 | async-start | bytes 131072 | tf_op jit(solution)/shard_map/all_to_all | solution.py:141
  138.8 6.7 %all-to-all-done.5 = f32[16,4,256]{2,1,0:T(4,128)S(1)} async-done(((f32[16,4,256]{2,1,0:T(4,128)}), f32[16,4,256]{2,1,0:T(4,128)S(1)}, u32[]{:S(2)}, u32[]{:S(2)}) %all-to-all-start.5) | async-done | bytes 65568 | tf_op jit(solution)/shard_map/all_to_all | solution.py:141
  146.2 11.7 %while.67 = (s32[]{:T(128)}, f32[2,4,256]{2,1,0:T(4,128)S(1)}, f32[2,4,8,256]{3,2,1,0:T(8,128)S(1)}, f32[2,4,256]{2,1,0:T(4,128)S(1)}, f32[2,4,8,256]{3,2,1,0:T(...) while((s32[]{:T(128)}, f32[2,4,256]{2,1,0:T(4,128)S(1)}, ...), condition=%wide.region_21.22_spmd, body=%wide.region_18.21_spmd.sunk | while | flops 291508224 | bytes 18277484 | solution.py:76
  146.3 3.2 %fusion.72 = (f32[4,256]{1,0:T(4,128)S(1)}, f32[4,256,8,256]{1,3,2,0:T(8,128)S(1)}) fusion(f32[4,8,256]{2,1,0:T(8,128)S(1)} %get-tuple-element.580, f32[4,256]{1,0:T(4,128)S(1)} %dynamic-slice_bitcast_fusion.28, f32[4,8,256]{2,1,0:T(8,128)S(1)} %get-tuple-element.581, bf16[2,4,8,64,256]{4,3,2,1,0:T(8,128)(2,1)S(1)} %get-tuple-element.696, ...), kind=kOutput, calls=%fused_computation.50.clone.1 | convolution fusion | flops 278920192 | bytes 9643008 | tf_op jit(solution)/shard_map/while/body/eval_jaxpr/gdp,gkdq->gpkq/dot_general | solution.py:51
  149.4 2.6 %exponential_reduce_fusion.10 = f32[4,256]{1,0:T(4,128)S(1)} fusion(f32[4,256,8,256]{1,3,2,0:T(8,128)S(1)} %get-tuple-element.582, f32[4,256]{1,0:T(4,128)S(1)} %bitcast_maximum_fusion.7, f32[4,8,256]{2,1,0:T(8,128)S(1)} %get-tuple-element.580, f32[4,256]{1,0:T(4,128)S(1)} %dynamic-slice_bitcast_fusion.28, f32[4,8,256]{2,1,0:T(8,128)S(1)} %get-tuple-element.581), kind=kLoop, calls=%fused_computation.48.clone.1 | loop fusion | flops 12581888 | bytes 8466432 | tf_op jit(solution)/shard_map/while/body/eval_jaxpr/reduce_sum | solution.py:63
  152.1 3.2 %fusion.72 = (f32[4,256]{1,0:T(4,128)S(1)}, f32[4,256,8,256]{1,3,2,0:T(8,128)S(1)}) fusion(f32[4,8,256]{2,1,0:T(8,128)S(1)} %get-tuple-element.580, f32[4,256]{1,0:T(4,128)S(1)} %dynamic-slice_bitcast_fusion.28, f32[4,8,256]{2,1,0:T(8,128)S(1)} %get-tuple-element.581, bf16[2,4,8,64,256]{4,3,2,1,0:T(8,128)(2,1)S(1)} %get-tuple-element.696, ...), kind=kOutput, calls=%fused_computation.50.clone.1 | convolution fusion | flops 278920192 | bytes 9643008 | tf_op jit(solution)/shard_map/while/body/eval_jaxpr/gdp,gkdq->gpkq/dot_general | solution.py:51
  155.3 2.6 %exponential_reduce_fusion.10 = f32[4,256]{1,0:T(4,128)S(1)} fusion(f32[4,256,8,256]{1,3,2,0:T(8,128)S(1)} %get-tuple-element.582, f32[4,256]{1,0:T(4,128)S(1)} %bitcast_maximum_fusion.7, f32[4,8,256]{2,1,0:T(8,128)S(1)} %get-tuple-element.580, f32[4,256]{1,0:T(4,128)S(1)} %dynamic-slice_bitcast_fusion.28, f32[4,8,256]{2,1,0:T(8,128)S(1)} %get-tuple-element.581), kind=kLoop, calls=%fused_computation.48.clone.1 | loop fusion | flops 12581888 | bytes 8466432 | tf_op jit(solution)/shard_map/while/body/eval_jaxpr/reduce_sum | solution.py:63
  157.9 11.3 %while.68 = (s32[]{:T(128)}, f32[2,4,8,256]{3,2,1,0:T(8,128)S(1)}, f32[2,4,8,256]{3,2,1,0:T(8,128)S(1)}, f32[2,4,256]{2,1,0:T(4,128)S(1)}, f32[2,4,256]{2,1,0:T(...) while((s32[]{:T(128)}, f32[2,4,8,256]{3,2,1,0:T(8,128)S(1)}, ...), condition=%wide.region_25.26_spmd, body=%wide.region_22.25_spmd.sunk | while | flops 291487744 | bytes 18351212 | solution.py:95
  160.0 3.6 %exponential_reduce_fusion.11 = f32[4,8,256]{2,1,0:T(8,128)S(1)} fusion(f32[4,256,8,256]{3,1,2,0:T(8,128)S(1)} %get-tuple-element.592, f32[4,8,256]{2,1,0:T(8,128)S(1)} %get-tuple-element.593, f32[4,8,256]{2,1,0:T(8,128)S(1)} %dynamic-slice_bitcast_fusion.29, f32[4,256]{1,0:T(4,128)S(1)} %dynamic-slice_bitcast_fusion.30, ...), kind=kLoop, calls=%fused_computation.67.clone.1 | loop fusion | flops 12574720 | bytes 8495104 | tf_op jit(solution)/shard_map/while/body/eval_jaxpr/reduce_sum | solution.py:85
  165.6 3.6 %exponential_reduce_fusion.11 = f32[4,8,256]{2,1,0:T(8,128)S(1)} fusion(f32[4,256,8,256]{3,1,2,0:T(8,128)S(1)} %get-tuple-element.592, f32[4,8,256]{2,1,0:T(8,128)S(1)} %get-tuple-element.593, f32[4,8,256]{2,1,0:T(8,128)S(1)} %dynamic-slice_bitcast_fusion.29, f32[4,256]{1,0:T(4,128)S(1)} %dynamic-slice_bitcast_fusion.30, ...), kind=kLoop, calls=%fused_computation.67.clone.1 | loop fusion | flops 12574720 | bytes 8495104 | tf_op jit(solution)/shard_map/while/body/eval_jaxpr/reduce_sum | solution.py:85
  170.7 3.5 %all-to-all-start.6 = ((f32[16,4,256]{2,1,0:T(4,128)}), f32[16,4,256]{2,1,0:T(4,128)S(1)}, u32[]{:S(2)}, u32[]{:S(2)}) async-start(f32[16,4,256]{2,1,0:T(4,128)} %reshape.228), calls=%async_computation.6 | async-start | bytes 131072 | tf_op jit(solution)/shard_map/all_to_all | solution.py:103
  176.3 4.8 %all-to-all-done.6 = f32[16,4,256]{2,1,0:T(4,128)S(1)} async-done(((f32[16,4,256]{2,1,0:T(4,128)}), f32[16,4,256]{2,1,0:T(4,128)S(1)}, u32[]{:S(2)}, u32[]{:S(2)}) %all-to-all-start.6) | async-done | bytes 65568 | tf_op jit(solution)/shard_map/all_to_all | solution.py:103
  181.1 3.5 %all-to-all-start.7 = ((f32[16,4,256]{2,1,0:T(4,128)}), f32[16,4,256]{2,1,0:T(4,128)S(1)}, u32[]{:S(2)}, u32[]{:S(2)}) async-start(f32[16,4,256]{2,1,0:T(4,128)} %reshape.231), calls=%async_computation.7 | async-start | bytes 131072 | tf_op jit(solution)/shard_map/all_to_all | solution.py:110
  186.6 4.8 %all-to-all-done.7 = f32[16,4,256]{2,1,0:T(4,128)S(1)} async-done(((f32[16,4,256]{2,1,0:T(4,128)}), f32[16,4,256]{2,1,0:T(4,128)S(1)}, u32[]{:S(2)}, u32[]{:S(2)}) %all-to-all-start.7) | async-done | bytes 65568 | tf_op jit(solution)/shard_map/all_to_all | solution.py:110
  (155 shorter events, 36.2 us)
Async XLA Ops:
  0.6 24.0 %copy-start = (bf16[8,64,256]{2,1,0:T(8,128)(2,1)S(1)}, bf16[8,64,256]{2,1,0:T(8,128)(2,1)}, u32[]{:S(2)}) copy-start(bf16[8,64,256]{2,1,0:T(8,128)(2,1)} %param.20) | copy-start | bytes 786436
  0.6 34.6 %copy-start.2 = (bf16[8,64,256]{2,1,0:T(8,128)(2,1)S(1)}, bf16[8,64,256]{2,1,0:T(8,128)(2,1)}, u32[]{:S(2)}) copy-start(bf16[8,64,256]{2,1,0:T(8,128)(2,1)} %param.19) | copy-start | bytes 786436
  0.7 34.7 %copy-start.4 = (f32[8,256]{1,0:T(8,128)S(1)}, f32[8,256]{1,0:T(8,128)}, u32[]{:S(2)}) copy-start(f32[8,256]{1,0:T(8,128)} %param.22) | copy-start | bytes 24580
  21.1 10.4 %all-to-all-start.1 = ((f32[16,4,256]{2,1,0:T(4,128)}), f32[16,4,256]{2,1,0:T(4,128)S(1)}, u32[]{:S(2)}, u32[]{:S(2)}) async-start(f32[16,4,256]{2,1,0:T(4,128)} %reshape.209), calls=%async_computation.1 | async-start | bytes 131072 | tf_op jit(solution)/shard_map/all_to_all | solution.py:141
  31.5 44.8 %all-to-all-start.2 = ((bf16[16,4,64,256]{3,2,1,0:T(8,128)(2,1)}), bf16[16,4,64,256]{3,2,1,0:T(8,128)(2,1)S(1)}, u32[]{:S(2)}, u32[]{:S(2)}) async-start(bf16[16,4,64,256]{3,2,1,0:T(8,128)(2,1)} %bitcast.46), calls=%async_computation.2 | async-start | bytes 4194304 | tf_op jit(solution)/shard_map/all_to_all | solution.py:134
  76.2 1.4 copy-start.1
  92.3 35.8 %copy-start.3 = (f32[8,256]{1,0:T(8,128)S(1)}, f32[8,256]{1,0:T(8,128)}, u32[]{:S(2)}) copy-start(f32[8,256]{1,0:T(8,128)} %param.23) | copy-start | bytes 24580
  105.1 18.1 %all-to-all-start.3 = ((f32[16,4,256]{2,1,0:T(4,128)}), f32[16,4,256]{2,1,0:T(4,128)S(1)}, u32[]{:S(2)}, u32[]{:S(2)}) async-start(f32[16,4,256]{2,1,0:T(4,128)} %reshape.218), calls=%async_computation.3 | async-start | bytes 131072 | tf_op jit(solution)/shard_map/all_to_all | solution.py:103
  123.2 10.4 %all-to-all-start.4 = ((f32[16,4,256]{2,1,0:T(4,128)}), f32[16,4,256]{2,1,0:T(4,128)S(1)}, u32[]{:S(2)}, u32[]{:S(2)}) async-start(f32[16,4,256]{2,1,0:T(4,128)} %reshape.221), calls=%async_computation.4 | async-start | bytes 131072 | tf_op jit(solution)/shard_map/all_to_all | solution.py:110
  135.2 10.4 %all-to-all-start.5 = ((f32[16,4,256]{2,1,0:T(4,128)}), f32[16,4,256]{2,1,0:T(4,128)S(1)}, u32[]{:S(2)}, u32[]{:S(2)}) async-start(f32[16,4,256]{2,1,0:T(4,128)} %reshape.223), calls=%async_computation.5 | async-start | bytes 131072 | tf_op jit(solution)/shard_map/all_to_all | solution.py:141
  170.7 10.4 %all-to-all-start.6 = ((f32[16,4,256]{2,1,0:T(4,128)}), f32[16,4,256]{2,1,0:T(4,128)S(1)}, u32[]{:S(2)}, u32[]{:S(2)}) async-start(f32[16,4,256]{2,1,0:T(4,128)} %reshape.228), calls=%async_computation.6 | async-start | bytes 131072 | tf_op jit(solution)/shard_map/all_to_all | solution.py:103
  181.1 10.4 %all-to-all-start.7 = ((f32[16,4,256]{2,1,0:T(4,128)}), f32[16,4,256]{2,1,0:T(4,128)S(1)}, u32[]{:S(2)}, u32[]{:S(2)}) async-start(f32[16,4,256]{2,1,0:T(4,128)} %reshape.231), calls=%async_computation.7 | async-start | bytes 131072 | tf_op jit(solution)/shard_map/all_to_all | solution.py:110
where the time goes:
time: 193 us; the launch traced here: 192 us
  waiting for transfers between devices  71.4 us (37%)
  starting transfers between devices  32.6 us (17%)
  other arithmetic  28.7 us (15%)
  local copies, waits for them, and re-layouts  22.3 us (12%)
  matrix products  21.8 us (11%)
  blocking collectives  13.6 us (7%)
    all_to_all x1, waiting for transfers between devices, per_device(): lax.all_to_all(send_points, 'src', split_axis=0, concat_axis=0, tiled=True)  40.1 us
    dot_general x8, matrix products, tile_cost(): jnp.einsum('gdp,gkdq->gpkq', src_block, tgt_block, preferred_element_type...  20.7 us
    all_to_all x2, starting transfers between devices, column_pass(): lax.all_to_all(send_high.reshape(shards, capacity, cluster_size), 'src',...  14.7 us
    reduce_sum x4, other arithmetic, column_one_group(): total = jnp.sum(jnp.exp(scores - highest[:, None, :, :]), axis=1)  14.2 us
    all_to_all x1, blocking collectives, per_device(): lax.all_to_all(request_table.reshape(shards, capacity), 'src', split_axis...  13.6 us
    all_to_all x2, waiting for transfers between devices, per_device(): lax.all_to_all(send_pot, 'src', split_axis=0, concat_axis=0, tiled=True)  11.5 us
    reduce_sum x4, other arithmetic, row_one_group(): jnp.sum(jnp.exp(scores - highest[:, :, None, None]), axis=(2, 3))  10.2 us
    all_to_all x2, waiting for transfers between devices, column_pass(): lax.all_to_all(send_high.reshape(shards, capacity, cluster_size), 'src',...  10.2 us
  transfers between devices with their start and end apart: 7, of which 7 were waited for; matrix products, arithmetic and copies ran while one was open for 5% of the time, Pallas kernels for 0%

commit v1 on v0

v1 whole, which is shorter than its diff:
```python
import functools
import math

import jax
import jax.numpy as jnp
from jax import lax
from jax.experimental import pallas as pl
from jax.experimental.pallas import tpu as pltpu
from jax.sharding import PartitionSpec as P

ITERS = 2
SCALE_EPS = 0.25
KEEP_TAU = 0.8
INV_EPS = 1.0 / SCALE_EPS

LOW_OFFSET = 60.0
LOW_TOP = 130.0
HIGH_OFFSET = 200.0
COLUMN_TOP = -KEEP_TAU * 10.0
LOG_LARGEST = 88.4

DEPTH = 128
VMEM = 24 * 1024 * 1024


def split3(value):
    high = value.astype(jnp.bfloat16).astype(jnp.float32)
    rest = value - high
    mid = rest.astype(jnp.bfloat16).astype(jnp.float32)
    return high, mid, rest - mid


def prepare(points, place, count, state):
    clusters, dims, size = points.shape

    def body(points_ref, *refs):
        lhs_ref, rhs_ref, half_ref = refs[-3:]
        row = lax.broadcasted_iota(jnp.int32, (DEPTH - dims, size), 0)
        ones = jnp.where(row < 3, 1.0, 0.0).astype(jnp.float32)

        def one(c, carry):
            raw = points_ref[c]
            wide = raw.astype(jnp.float32)
            half = 0.5 * jnp.sum(wide * wide, axis=0, keepdims=True)
            half_ref[0, pl.ds(c, 1), :] = half
            high, mid, low = split3(-INV_EPS * half)
            extra = jnp.where(row == 0, high, jnp.where(row == 1, mid, jnp.where(row == 2, low, 0.0)))
            rhs_ref[0, c, :dims, :] = raw
            rhs_ref[0, c, dims:, :] = extra.astype(jnp.bfloat16)
            lhs_ref[0, c] = jnp.concatenate([INV_EPS * wide, ones], axis=0).T.astype(jnp.bfloat16)
            return carry

        lax.fori_loop(0, clusters, one, 0, unroll=2)

    shapes = (
        jax.ShapeDtypeStruct((count, clusters, size, DEPTH), jnp.bfloat16),
        jax.ShapeDtypeStruct((count, clusters, DEPTH, size), jnp.bfloat16),
        jax.ShapeDtypeStruct((count, clusters, size), jnp.float32),
    )
    extra_specs = [] if state is None else [pl.BlockSpec(memory_space=pl.ANY)] * 3
    return pl.pallas_call(
        body,
        grid=(1,),
        out_shape=shapes,
        in_specs=[pl.BlockSpec((clusters, dims, size), lambda i: (0, 0, 0))] + extra_specs,
        out_specs=(
            pl.BlockSpec((1, clusters, size, DEPTH), lambda i: (place, 0, 0, 0)),
            pl.BlockSpec((1, clusters, DEPTH, size), lambda i: (place, 0, 0, 0)),
            pl.BlockSpec((1, clusters, size), lambda i: (place, 0, 0)),
        ),
        input_output_aliases={} if state is None else {1: 0, 2: 1, 3: 2},
        compiler_params=pltpu.CompilerParams(vmem_limit_bytes=VMEM),
        cost_estimate=pl.CostEstimate(
            flops=clusters * dims * size * 4, bytes_accessed=clusters * size * DEPTH * 4, transcendentals=0
        ),
        name="prepare",
    )(points, *(() if state is None else state))


def swap_blocks(array, place, rows):
    blocks = array.shape[-2] // rows
    order = [q ^ (1 << place) for q in range(blocks)]
    return jnp.concatenate([array[..., q * rows:(q + 1) * rows, :] for q in order], axis=-2)


def list_pairs(me, cand, target_bits, tgt_count):
    sources, per_cluster = cand.shape
    group = tgt_count << len(target_bits)
    mask = sum(1 << b for b in target_bits)

    def body(me_ref, cand_ref, out_ref):
        own = me_ref[0]

        def one(s, filled):
            for k in range(per_cluster):
                code = cand_ref[s, k]
                apart = lax.div(code, tgt_count) ^ own
                block = 0
                for place, bit in enumerate(target_bits):
                    block = block | (((apart >> bit) & 1) << place)
                out_ref[filled + 1] = s * group + block * tgt_count + lax.rem(code, tgt_count)
                filled = filled + jnp.where((apart & ~mask) == 0, 1, 0).astype(jnp.int32)
            return filled

        out_ref[0] = lax.fori_loop(0, sources, one, jnp.int32(0))

    return pl.pallas_call(
        body,
        out_shape=jax.ShapeDtypeStruct((sources * per_cluster + 2,), jnp.int32),
        in_specs=[pl.BlockSpec(memory_space=pltpu.SMEM)] * 2,
        out_specs=pl.BlockSpec(memory_space=pltpu.SMEM),
        cost_estimate=pl.CostEstimate(flops=1000000, bytes_accessed=10000, transcendentals=0),
        name="list_pairs",
    )(me, cand)


def spread_columns(rows_value, column_ref):
    turned = rows_value.T
    for r in range(rows_value.shape[0]):
        column_ref[r] = jnp.broadcast_to(turned[:, r:r + 1], column_ref.shape[1:])


def tile_sums(lhs_ref, rhs_ref, column_ref, m, n, keep=None, shift=0.0):
    size = lhs_ref.shape[1]
    step = 64
    right = rhs_ref[n]
    total = None
    for start in range(0, size, step):
        product = jnp.dot(lhs_ref[m, start:start + step, :], right, preferred_element_type=jnp.float32)
        column = column_ref[m, start:start + step, :]
        term = product + jnp.concatenate([column] * (size // column.shape[1]), axis=1)
        value = jnp.exp(term - shift if keep is not None else term)
        if keep is not None:
            value = jnp.where(keep(term), value, 0.0)
        part = jnp.sum(value.reshape(step // 8, 8, size), axis=0)
        total = part if total is None else total + part
    return total


def row_kernel(group, first, place, rows, pairs_ref, lhs_ref, rhs_ref, half_ref, pot_ref, come_ref, far_ref, out_ref, column_ref, acc_ref):
    if first:
        pot = pot_ref[...]
    else:
        sums = pot_ref[...] + swap_blocks(come_ref[...], place, rows)
        pot = -KEEP_TAU * SCALE_EPS * (jnp.log(sums) - column_offset(group))
    spread_columns(INV_EPS * (pot - half_ref[...]) - LOW_OFFSET, column_ref)
    targets = lhs_ref.shape[0]
    count = pairs_ref[0]

    def run(keep, shift):
        acc_ref[...] = jnp.zeros_like(acc_ref)

        def one(p, carry):
            code = pairs_ref[p + 1]
            s, t = lax.div(code, targets), lax.rem(code, targets)
            acc_ref[s] += tile_sums(lhs_ref, rhs_ref, column_ref, t, s, keep, shift)
            return carry

        lax.fori_loop(0, count, one, 0)
        return jnp.sum(acc_ref[...], axis=1)

    def far_added(sums):
        own = far_ref.shape[0]
        return jnp.concatenate([sums[:own] + jnp.exp(far_ref[...] - LOW_OFFSET), sums[own:]], axis=0)

    if not first:
        out_ref[...] = far_added(run(None, 0.0))
        return
    narrow = jnp.max(pot) <= LOW_TOP * SCALE_EPS

    @pl.when(narrow)
    def _():
        out_ref[0] = far_added(run(None, 0.0))
        out_ref[1] = jnp.zeros(out_ref.shape[1:], jnp.float32)

    @pl.when(jnp.logical_not(narrow))
    def _():
        edge = LOW_TOP - LOW_OFFSET
        out_ref[0] = far_added(run(lambda term: term <= edge, 0.0))
        out_ref[1] = run(lambda term: term > edge, HIGH_OFFSET - LOW_OFFSET)


def column_offset(terms):
    return LOG_LARGEST - COLUMN_TOP - math.log(terms)


def column_kernel(terms, first, place, rows, pairs_ref, lhs_ref, rhs_ref, half_ref, sums_ref, come_ref, far_ref, out_ref, pot_ref, column_ref, acc_ref):
    sums = sums_ref[...] + swap_blocks(come_ref[...], place, rows)
    if first:
        low, high = sums[0], sums[1]
        low_log = jnp.log(low) + LOW_OFFSET
        high_log = jnp.where(high > 0.0, jnp.log(jnp.where(high > 0.0, high, 1.0)) + HIGH_OFFSET, -1e30)
        top = jnp.maximum(low_log, high_log)
        log_sum = top + jnp.log(jnp.exp(low_log - top) + jnp.exp(high_log - top))
    else:
        log_sum = jnp.log(sums) + LOW_OFFSET
    pot = -KEEP_TAU * SCALE_EPS * log_sum
    pot_ref[...] = pot[:pot_ref.shape[0]]
    spread_columns(INV_EPS * (pot - half_ref[...]) + column_offset(terms), column_ref)
    targets = rhs_ref.shape[0]
    acc_ref[...] = jnp.zeros_like(acc_ref)

    def one(p, carry):
        code = pairs_ref[p + 1]
        s, t = lax.div(code, targets), lax.rem(code, targets)
        acc_ref[t] += tile_sums(lhs_ref, rhs_ref, column_ref, s, t)
        return carry

    lax.fori_loop(0, pairs_ref[0], one, 0)
    total = jnp.sum(acc_ref[...], axis=1)
    own = far_ref.shape[0]
    out_ref[...] = jnp.concatenate([total[:own] + jnp.exp(far_ref[...] + column_offset(terms)), total[own:]], axis=0)


def run_pass(kernel, out_shapes, lhs, rhs, pairs, tiles, *rest):
    size = lhs.shape[1]
    space = pl.BlockSpec(memory_space=pltpu.VMEM)
    return pl.pallas_call(
        kernel,
        out_shape=out_shapes,
        in_specs=[pl.BlockSpec(memory_space=pltpu.SMEM)] + [space] * (2 + len(rest)),
        out_specs=jax.tree.map(lambda _: space, out_shapes),
        scratch_shapes=[
            pltpu.VMEM((lhs.shape[0], size, 128), jnp.float32),
            pltpu.VMEM((rhs.shape[0], 8, size), jnp.float32),
        ],
        compiler_params=pltpu.CompilerParams(vmem_limit_bytes=VMEM),
        cost_estimate=pl.CostEstimate(
            flops=2 * tiles * size * size * DEPTH, bytes_accessed=8 << 20, transcendentals=tiles * size * size
        ),
        name="tiles",
    )(pairs, lhs, rhs, *rest)


def per_device(src_points, tgt_points, g_init, far_src, far_tgt, cand_owner, cand_local):
    src_count, _, size = src_points.shape
    tgt_count = tgt_points.shape[0]
    per_cluster = cand_owner.shape[1]
    shards = lax.axis_size("src")
    bits = shards.bit_length() - 1
    upper = max(bits // 2 - 1, 0)
    source_bits = [b for b in range(bits - 1, bits - 1 - upper, -1)] + [0]
    target_bits = [b for b in range(bits - 1 - upper, 0, -1)]
    nr, nc = 1 << len(source_bits), 1 << len(target_bits)
    capacity = max(2, min(src_count // 2, 2 * src_count * per_cluster // shards))
    terms = shards * capacity * size

    def across(array, bit):
        return lax.ppermute(array, "src", [(i, i ^ (1 << bit)) for i in range(shards)])

    def gathered(array, which):
        blocks = [array]
        for bit in which:
            blocks = blocks + [across(b, bit) for b in blocks]
        return blocks

    def grown(array, which):
        for bit in which:
            array = jnp.concatenate([array, across(array, bit)], axis=0)
        return array

    def added(array, which, rows):
        for place, bit in enumerate(which[:-1]):
            array = array + swap_blocks(across(array, bit), place, rows)
        return array, across(array, which[-1]), len(which) - 1

    cand = grown(cand_owner * tgt_count + cand_local, source_bits)
    pot = grown(g_init, target_bits)
    src_blocks = gathered(src_points, source_bits)
    tgt_blocks = gathered(tgt_points, target_bits)
    me = lax.axis_index("src").astype(jnp.int32).reshape(1)
    pairs = list_pairs(me, cand, target_bits, tgt_count)

    src_state = tgt_state = None
    for place, block in enumerate(src_blocks):
        src_state = prepare(block, place, nr, src_state)
    for place, block in enumerate(tgt_blocks):
        tgt_state = prepare(block, place, nc, tgt_state)
    src_lhs, src_rhs, src_half = [a.reshape((-1,) + a.shape[2:]) for a in src_state]
    tgt_lhs, tgt_rhs, tgt_half = [a.reshape((-1,) + a.shape[2:]) for a in tgt_state]

    f32 = jnp.float32
    sources, targets = nr * src_count, nc * tgt_count
    tiles = src_count * per_cluster
    come, place = pot, 0
    for iteration in range(ITERS):
        first = iteration == 0
        shape = (2, sources, size) if first else (sources, size)
        sums = run_pass(
            functools.partial(row_kernel, terms, first, place, tgt_count),
            jax.ShapeDtypeStruct(shape, f32),
            tgt_lhs, src_rhs, pairs, tiles, tgt_half, pot, come, far_src,
        )
        sums, come, place = added(sums, source_bits, src_count)
        column, src_pot = run_pass(
            functools.partial(column_kernel, terms, first, place, src_count),
            (jax.ShapeDtypeStruct((targets, size), f32), jax.ShapeDtypeStruct((src_count, size), f32)),
            src_lhs, tgt_rhs, pairs, tiles, src_half, sums, come, far_tgt,
        )
        pot, come, place = added(column, target_bits, tgt_count)
    other = (1 << place) * tgt_count
    total = pot[:tgt_count] + come[other:other + tgt_count]
    tgt_pot = -KEEP_TAU * SCALE_EPS * (jnp.log(total) - column_offset(terms))
    return (src_pot, tgt_pot)


def solution(mesh):
    return jax.shard_map(
        per_device,
        mesh=mesh,
        in_specs=(
            P(("groups", "src"), None, None),
            P(("groups", "src"), None, None),
            P(("groups", "src"), None),
            P(("groups", "src"), None),
            P(("groups", "src"), None),
            P(("groups", "src"), None),
            P(("groups", "src"), None),
        ),
        out_specs=(P(("groups", "src"), None), P(("groups", "src"), None)),
        check_vma=False,
    )
```

time: 193 us -> 147 us (0.76)
  Pallas kernels: 0 us -> 80 us
  waiting for transfers between devices: 71.4 us -> 34.9 us
  other arithmetic: 28.7 us -> 2.2 us
  matrix products: 21.8 us -> 0 us
  starting transfers between devices: 32.6 us -> 12.9 us
  blocking collectives: 13.6 us -> 0 us
  local copies, waits for them, and re-layouts: 22.3 us -> 15.6 us
    pallas_call x0 -> x13, Pallas kernels: none -> 80 us  [the longest x4 72 us: run_pass(): pl.pallas_call(kernel, out_shape=out_shapes, in_specs=[pl.BlockSpec(memor...]
    all_to_all x7 -> x0, waiting for transfers between devices: 71.4 us -> none  [the longest x1 40.1 us: per_device(): lax.all_to_all(send_points, 'src', split_axis=0, concat_axis=0, tiled=True)]
    ppermute x0 -> x18, waiting for transfers between devices: none -> 34.9 us  [across(): lax.ppermute(array, 'src', [(i, i ^ 1 << bit) for i in range(shards)])]
    all_to_all x7 -> x0, starting transfers between devices: 32.6 us -> none  [the longest x2 14.7 us: column_pass(): lax.all_to_all(send_high.reshape(shards, capacity, cluster_size), 'src',...]
    reduce_sum x11 -> x0, other arithmetic: 25.4 us -> none  [the longest x4 14.2 us: column_one_group(): total = jnp.sum(jnp.exp(scores - highest[:, None, :, :]), axis=1)]
    dot_general x10 -> x0, matrix products: 21.8 us -> none  [the longest x8 20.7 us: tile_cost(): jnp.einsum('gdp,gkdq->gpkq', src_block, tgt_block, preferred_element_type...]
    unnamed x10 -> x32, local copies, waits for them, and re-layouts: 1.38 us -> 14.9 us
    all_to_all x1 -> x0, blocking collectives: 13.6 us -> none  [per_device(): lax.all_to_all(request_table.reshape(shards, capacity), 'src', split_axis...]
  transfers between devices with their start and end apart: 7 -> 18, of which waited for: 7 -> 11; matrix products, arithmetic and copies ran while one was open for 5% -> 3% of each run, Pallas kernels for 0% -> 5%
where the time goes in v1:
time: 147 us; the launch traced here: 146 us
  Pallas kernels  80 us (54%)
  waiting for transfers between devices  34.9 us (24%)
  local copies, waits for them, and re-layouts  15.6 us (11%)
  starting transfers between devices  12.9 us (9%)
  other arithmetic  2.2 us (1%)
    pallas_call x4, Pallas kernels, run_pass(): pl.pallas_call(kernel, out_shape=out_shapes, in_specs=[pl.BlockSpec(memor...  72 us
    ppermute x18, waiting for transfers between devices, across(): lax.ppermute(array, 'src', [(i, i ^ 1 << bit) for i in range(shards)])  34.9 us
    unnamed x32, local copies, waits for them, and re-layouts  14.9 us
    ppermute x18, starting transfers between devices, across(): lax.ppermute(array, 'src', [(i, i ^ 1 << bit) for i in range(shards)])  12.9 us
    pallas_call x8, Pallas kernels, prepare(): pl.pallas_call(body, grid=(1,), out_shape=shapes, in_specs=[pl.BlockSpec(...  4.41 us
    pallas_call x1, Pallas kernels, list_pairs(): pl.pallas_call(body, out_shape=jax.ShapeDtypeStruct((sources * per_cluste...  3.58 us
  transfers between devices with their start and end apart: 18, of which 11 were waited for; matrix products, arithmetic and copies ran while one was open for 3% of the time, Pallas kernels for 5%

profile of v1, /device:TPU:0, one launch (start us, length us, event | category | flops | bytes accessed | tf_op | source)
XLA Modules:
  0.0 146.4 jit_solution(13474096878096876895)
XLA Ops:
  0.6 3.1 %collective-permute-start.5 = (bf16[8,64,256]{2,1,0:T(8,128)(2,1)}, bf16[8,64,256]{2,1,0:T(8,128)(2,1)S(1)}, u32[]{:S(2)}, u32[]{:S(2)}) collective-permute-start(bf16[8,64,256]{2,1,0:T(8,128)(2,1)} %points_ref.3), channel_id=1, source_target_pairs={{0,4},{1,5},{2,6},{3,7},{4,0},{5,1},{6,2},{7,3},{8,12},{9,13},{10,... | collective-permute-start | bytes 786440 | tf_op jit(solution)/shard_map/ppermute | solution.py:249
  3.7 1.5 %collective-permute-start.7 = (bf16[8,64,256]{2,1,0:T(8,128)(2,1)}, bf16[8,64,256]{2,1,0:T(8,128)(2,1)S(1)}, u32[]{:S(2)}, u32[]{:S(2)}) collective-permute-start(bf16[8,64,256]{2,1,0:T(8,128)(2,1)} %points_ref.3), channel_id=1, source_target_pairs={{0,2},{1,3},{2,0},{3,1},{4,6},{5,7},{6,4},{7,5},{8,10},{9,11},{10,... | collective-permute-start | bytes 786440 | tf_op jit(solution)/shard_map/ppermute | solution.py:249
  5.2 2.6 %collective-permute-start.2 = (bf16[8,64,256]{2,1,0:T(8,128)(2,1)}, bf16[8,64,256]{2,1,0:T(8,128)(2,1)S(1)}, u32[]{:S(2)}, u32[]{:S(2)}) collective-permute-start(bf16[8,64,256]{2,1,0:T(8,128)(2,1)} %points_ref.2), channel_id=1, source_target_pairs={{0,8},{1,9},{2,10},{3,11},{4,12},{5,13},{6,14},{7,15},{8,0},{9,1},... | collective-permute-start | bytes 786440 | tf_op jit(solution)/shard_map/ppermute | solution.py:249
  9.7 0.9 copy-done.10
  11.1 1.3 copy-done.2
  12.4 1.4 copy-done.6
  13.7 0.9 copy-done.11
  15.1 1.3 copy-done
  16.5 3.2 %collective-permute-done = s32[8,8]{0,1:T(8,128)S(1)} collective-permute-done((s32[8,8]{0,1:T(8,128)S(1)}, s32[8,8]{0,1:T(8,128)S(1)}, u32[]{:S(2)}, u32[]{:S(2)}) %collective-permute-start) | collective-permute-done | bytes 288 | tf_op jit(solution)/shard_map/ppermute | solution.py:249
  19.7 3.8 %collective-permute-done.8 = f32[8,256]{1,0:T(8,128)S(1)} collective-permute-done((f32[8,256]{1,0:T(8,128)}, f32[8,256]{1,0:T(8,128)S(1)}, u32[]{:S(2)}, u32[]{:S(2)}) %collective-permute-start.8) | collective-permute-done | bytes 8224 | tf_op jit(solution)/shard_map/ppermute | solution.py:249
  25.0 1.5 %collective-permute-start.9 = (f32[16,256]{1,0:T(8,128)S(1)}, f32[16,256]{1,0:T(8,128)S(1)}, u32[]{:S(2)}, u32[]{:S(2)}) collective-permute-start(f32[16,256]{1,0:T(8,128)S(1)} %pad_maximum_fusion.1), channel_id=1, source_target_pairs={{0,2},{1,3},{2,0},{3,1},{4,6},{5,7},{6,4},{7,5},{8,10},{9,11},{10,... | collective-permute-start | bytes 49160 | tf_op jit(solution)/shard_map/ppermute | solution.py:249
  27.2 3.6 %list_pairs.1.pairs_ref = s32[258]{0:T(512)} custom-call(s32[1]{0:T(128)} %bitcast.me_ref, s32[32,8]{1,0:T(8,128)} %copy.29.cand_ref), custom_call_target="tpu_custom_call" | custom-call | flops 1000000 | bytes 10000 | tf_op jit(solution)/shard_map/list_pairs/pallas_call | solution.py:107
  30.8 1.8 %collective-permute-done.9 = f32[16,256]{1,0:T(8,128)S(1)} collective-permute-done((f32[16,256]{1,0:T(8,128)S(1)}, f32[16,256]{1,0:T(8,128)S(1)}, u32[]{:S(2)}, u32[]{:S(2)}) %collective-permute-start.9) | collective-permute-done | bytes 16416 | tf_op jit(solution)/shard_map/ppermute | solution.py:249
  33.3 1.6 %copy-done.3 = bf16[4,8,256,128]{3,2,1,0:T(8,128)(2,1)S(1)} copy-done((bf16[4,8,256,128]{3,2,1,0:T(8,128)(2,1)S(1)}, bf16[4,8,256,128]{3,2,1,0:T(8,128)(2,1)}, u32[]{:S(2)}) %copy-start.3) | copy-done | bytes 2097176
  34.9 1.6 %copy-done.7 = bf16[4,8,128,256]{3,2,1,0:T(8,128)(2,1)S(1)} copy-done((bf16[4,8,128,256]{3,2,1,0:T(8,128)(2,1)S(1)}, bf16[4,8,128,256]{3,2,1,0:T(8,128)(2,1)}, u32[]{:S(2)}) %copy-start.7) | copy-done | bytes 2097176
  36.9 1.2 copy-done.1
  39.4 1.4 prepare.15
  41.3 0.8 copy-done.4
  42.8 1.6 %copy-done.5 = bf16[4,8,256,128]{3,2,1,0:T(8,128)(2,1)S(1)} copy-done((bf16[4,8,256,128]{3,2,1,0:T(8,128)(2,1)S(1)}, bf16[4,8,256,128]{3,2,1,0:T(8,128)(2,1)}, u32[]{:S(2)}) %copy-start.5) | copy-done | bytes 2097176
  44.4 28.7 %tiles.4 = f32[2,32,256]{2,1,0:T(8,128)S(1)} custom-call(s32[258]{0:T(512)S(1)} %copy-done.12, bf16[32,256,128]{2,1,0:T(8,128)(2,1)S(1)} %bitcast.11, bf16[32,128,256]{2,1,0:T(8,128)(2,1)S(1)} %bitcast.9, f32[32,256]{1,0:T(8,128)S(1)} %bitcast.17, f32[32,256]{1,0:T(8,128)S(1)} %pad_maximum_fusion.pot_ref.come_ref, ...), custom_call_target="tpu_custom_call" | custom-call | flops 1073741824 | bytes 8388608 | tf_op jit(solution)/shard_map/tiles/pallas_call | solution.py:218
  73.1 1.1 collective-permute-start.10
  74.2 5.0 %collective-permute-done.10 = f32[2,32,256]{2,1,0:T(8,128)S(1)} collective-permute-done((f32[2,32,256]{2,1,0:T(8,128)S(1)}, f32[2,32,256]{2,1,0:T(8,128)S(1)}, u32[]{:S(2)}, u32[]{:S(2)}) %collective-permute-start.10) | collective-permute-done | bytes 65568 | tf_op jit(solution)/shard_map/ppermute | solution.py:249
  79.2 1.2 collective-permute-done.11.come_ref
  80.5 14.6 %tiles.5 = (f32[32,256]{1,0:T(8,128)S(1)}, f32[8,256]{1,0:T(8,128)}) custom-call(s32[258]{0:T(512)S(1)} %copy-done.12, bf16[32,256,128]{2,1,0:T(8,128)(2,1)S(1)} %bitcast.7, bf16[32,128,256]{2,1,0:T(8,128)(2,1)S(1)} %bitcast.13, f32[32,256]{1,0:T(8,128)S(1)} %bitcast.15, f32[2,32,256]{2,1,0:T(8,128)S(1)} %maximum_add_fusion.sums_ref, ...), custom_call_target="tpu_custom_call" | custom-call | flops 1073741824 | bytes 8388608 | tf_op jit(solution)/shard_map/tiles/pallas_call | solution.py:218
  95.1 3.9 %collective-permute-done.12 = f32[32,256]{1,0:T(8,128)S(1)} collective-permute-done((f32[32,256]{1,0:T(8,128)S(1)}, f32[32,256]{1,0:T(8,128)S(1)}, u32[]{:S(2)}, u32[]{:S(2)}) %collective-permute-start.12) | collective-permute-done | bytes 32800 | tf_op jit(solution)/shard_map/ppermute | solution.py:249
  99.7 3.4 %collective-permute-done.13.come_ref = f32[32,256]{1,0:T(8,128)S(1)} collective-permute-done((f32[32,256]{1,0:T(8,128)S(1)}, f32[32,256]{1,0:T(8,128)S(1)}, u32[]{:S(2)}, u32[]{:S(2)}) %collective-permute-start.13) | collective-permute-done | bytes 32800 | tf_op jit(solution)/shard_map/ppermute | solution.py:249
  103.0 14.1 %tiles.6 = f32[32,256]{1,0:T(8,128)S(1)} custom-call(s32[258]{0:T(512)S(1)} %copy-done.12, bf16[32,256,128]{2,1,0:T(8,128)(2,1)S(1)} %bitcast.12, bf16[32,128,256]{2,1,0:T(8,128)(2,1)S(1)} %bitcast.10, f32[32,256]{1,0:T(8,128)S(1)} %bitcast.18, f32[32,256]{1,0:T(8,128)S(1)} %maximum_add_fusion.1.pot_ref, f32[32,256]{1,0:T(8,128)S(1)} %collective-permute-done.13.come_ref, ...), custom_call_target="tpu_custom_call" | custom-call | flops 1073741824 | bytes 8388608 | tf_op jit(solution)/shard_map/tiles/pallas_call | solution.py:218
  117.8 4.2 %collective-permute-done.14 = f32[32,256]{1,0:T(8,128)S(1)} collective-permute-done((f32[32,256]{1,0:T(8,128)S(1)}, f32[32,256]{1,0:T(8,128)S(1)}, u32[]{:S(2)}, u32[]{:S(2)}) %collective-permute-start.14) | collective-permute-done | bytes 32800 | tf_op jit(solution)/shard_map/ppermute | solution.py:249
  122.1 1.2 collective-permute-done.15.come_ref
  123.3 14.6 %tiles.7 = (f32[32,256]{1,0:T(8,128)S(1)}, f32[8,256]{1,0:T(8,128)}) custom-call(s32[258]{0:T(512)S(1)} %copy-done.12, bf16[32,256,128]{2,1,0:T(8,128)(2,1)S(1)} %bitcast.8, bf16[32,128,256]{2,1,0:T(8,128)(2,1)S(1)} %bitcast.14, f32[32,256]{1,0:T(8,128)S(1)} %bitcast.16, f32[32,256]{1,0:T(8,128)S(1)} %maximum_add_fusion.2.sums_ref, ...), custom_call_target="tpu_custom_call" | custom-call | flops 1073741824 | bytes 8388608 | tf_op jit(solution)/shard_map/tiles/pallas_call | solution.py:218
  137.9 3.9 %collective-permute-done.16 = f32[32,256]{1,0:T(8,128)S(1)} collective-permute-done((f32[32,256]{1,0:T(8,128)S(1)}, f32[32,256]{1,0:T(8,128)S(1)}, u32[]{:S(2)}, u32[]{:S(2)}) %collective-permute-start.16) | collective-permute-done | bytes 32800 | tf_op jit(solution)/shard_map/ppermute | solution.py:249
  142.5 3.4 %collective-permute-done.17 = f32[32,256]{1,0:T(8,128)S(1)} collective-permute-done((f32[32,256]{1,0:T(8,128)S(1)}, f32[32,256]{1,0:T(8,128)S(1)}, u32[]{:S(2)}, u32[]{:S(2)}) %collective-permute-start.17) | collective-permute-done | bytes 32800 | tf_op jit(solution)/shard_map/ppermute | solution.py:249
  (64 shorter events, 11.4 us)
Async XLA Ops:
  0.6 22.9 %collective-permute-start.5 = (bf16[8,64,256]{2,1,0:T(8,128)(2,1)}, bf16[8,64,256]{2,1,0:T(8,128)(2,1)S(1)}, u32[]{:S(2)}, u32[]{:S(2)}) collective-permute-start(bf16[8,64,256]{2,1,0:T(8,128)(2,1)} %points_ref.3), channel_id=1, source_target_pairs={{0,4},{1,5},{2,6},{3,7},{4,0},{5,1},{6,2},{7,3},{8,12},{9,13},{10,... | collective-permute-start | bytes 786440 | tf_op jit(solution)/shard_map/ppermute | solution.py:249
  3.7 34.8 %collective-permute-start.7 = (bf16[8,64,256]{2,1,0:T(8,128)(2,1)}, bf16[8,64,256]{2,1,0:T(8,128)(2,1)S(1)}, u32[]{:S(2)}, u32[]{:S(2)}) collective-permute-start(bf16[8,64,256]{2,1,0:T(8,128)(2,1)} %points_ref.3), channel_id=1, source_target_pairs={{0,2},{1,3},{2,0},{3,1},{4,6},{5,7},{6,4},{7,5},{8,10},{9,11},{10,... | collective-permute-start | bytes 786440 | tf_op jit(solution)/shard_map/ppermute | solution.py:249
  5.2 18.8 %collective-permute-start.2 = (bf16[8,64,256]{2,1,0:T(8,128)(2,1)}, bf16[8,64,256]{2,1,0:T(8,128)(2,1)S(1)}, u32[]{:S(2)}, u32[]{:S(2)}) collective-permute-start(bf16[8,64,256]{2,1,0:T(8,128)(2,1)} %points_ref.2), channel_id=1, source_target_pairs={{0,8},{1,9},{2,10},{3,11},{4,12},{5,13},{6,14},{7,15},{8,0},{9,1},... | collective-permute-start | bytes 786440 | tf_op jit(solution)/shard_map/ppermute | solution.py:249
  7.8 31.2 %collective-permute-start.4 = (bf16[8,64,256]{2,1,0:T(8,128)(2,1)}, bf16[8,64,256]{2,1,0:T(8,128)(2,1)S(1)}, u32[]{:S(2)}, u32[]{:S(2)}) collective-permute-start(bf16[8,64,256]{2,1,0:T(8,128)(2,1)} %points_ref.2), channel_id=1, source_target_pairs={{0,1},{1,0},{2,3},{3,2},{4,5},{5,4},{6,7},{7,6},{8,9},{9,8},{10,11... | collective-permute-start | bytes 786440 | tf_op jit(solution)/shard_map/ppermute | solution.py:249
  9.3 10.3 %collective-permute-start = (s32[8,8]{0,1:T(8,128)S(1)}, s32[8,8]{0,1:T(8,128)S(1)}, u32[]{:S(2)}, u32[]{:S(2)}) collective-permute-start(s32[8,8]{0,1:T(8,128)S(1)} %multiply_add_fusion), channel_id=1, source_target_pairs={{0,8},{1,9},{2,10},{3,11},{4,12},{5,13},{6,14},{7,15},{8,0},{9,1},... | collective-permute-start | bytes 776 | tf_op jit(solution)/shard_map/ppermute | solution.py:249
  9.7 0.9 copy-start.10
  11.0 1.3 copy-start.2
  12.4 1.4 copy-start.6
  15.1 1.3 copy-start
  19.7 3.9 %collective-permute-start.8 = (f32[8,256]{1,0:T(8,128)}, f32[8,256]{1,0:T(8,128)S(1)}, u32[]{:S(2)}, u32[]{:S(2)}) collective-permute-start(f32[8,256]{1,0:T(8,128)} %param.9), channel_id=1, source_target_pairs={{0,4},{1,5},{2,6},{3,7},{4,0},{5,1},{6,2},{7,3},{8,12},{9,13},{10,... | collective-permute-start | bytes 24584 | tf_op jit(solution)/shard_map/ppermute | solution.py:249
  23.5 1.5 collective-permute-start.1
  23.5 15.9 %collective-permute-start.6 = (bf16[8,64,256]{2,1,0:T(8,128)(2,1)S(1)}, bf16[8,64,256]{2,1,0:T(8,128)(2,1)}, u32[]{:S(2)}, u32[]{:S(2)}) collective-permute-start(bf16[8,64,256]{2,1,0:T(8,128)(2,1)S(1)} %collective-permute-done.5.points_ref), channel_id=1, source_target_pairs={{0,2},{1,3},{2,0},{3,1},{4,6},{5,7},{6,4},{7,5},{8,10},{9,11},{10,... | collective-permute-start | bytes 786440 | tf_op jit(solution)/shard_map/ppermute | solution.py:249
  24.1 16.8 %collective-permute-start.3 = (bf16[8,64,256]{2,1,0:T(8,128)(2,1)S(1)}, bf16[8,64,256]{2,1,0:T(8,128)(2,1)S(1)}, u32[]{:S(2)}, u32[]{:S(2)}) collective-permute-start(bf16[8,64,256]{2,1,0:T(8,128)(2,1)S(1)} %collective-permute-done.2.points_ref), channel_id=1, source_target_pairs={{0,1},{1,0},{2,3},{3,2},{4,5},{5,4},{6,7},{7,6},{8,9},{9,8},{10,11... | collective-permute-start | bytes 786440 | tf_op jit(solution)/shard_map/ppermute | solution.py:249
  25.0 7.6 %collective-permute-start.9 = (f32[16,256]{1,0:T(8,128)S(1)}, f32[16,256]{1,0:T(8,128)S(1)}, u32[]{:S(2)}, u32[]{:S(2)}) collective-permute-start(f32[16,256]{1,0:T(8,128)S(1)} %pad_maximum_fusion.1), channel_id=1, source_target_pairs={{0,2},{1,3},{2,0},{3,1},{4,6},{5,7},{6,4},{7,5},{8,10},{9,11},{10,... | collective-permute-start | bytes 49160 | tf_op jit(solution)/shard_map/ppermute | solution.py:249
  33.3 1.6 %copy-start.3 = (bf16[4,8,256,128]{3,2,1,0:T(8,128)(2,1)S(1)}, bf16[4,8,256,128]{3,2,1,0:T(8,128)(2,1)}, u32[]{:S(2)}) copy-start(bf16[4,8,256,128]{3,2,1,0:T(8,128)(2,1)} %copy-done.2) | copy-start | bytes 6291460
  34.9 1.6 %copy-start.7 = (bf16[4,8,128,256]{3,2,1,0:T(8,128)(2,1)S(1)}, bf16[4,8,128,256]{3,2,1,0:T(8,128)(2,1)}, u32[]{:S(2)}) copy-start(bf16[4,8,128,256]{3,2,1,0:T(8,128)(2,1)} %copy-done.6) | copy-start | bytes 6291460
  36.5 1.6 %copy-start.1 = (bf16[4,8,128,256]{3,2,1,0:T(8,128)(2,1)S(1)}, bf16[4,8,128,256]{3,2,1,0:T(8,128)(2,1)}, u32[]{:S(2)}) copy-start(bf16[4,8,128,256]{3,2,1,0:T(8,128)(2,1)} %copy-done) | copy-start | bytes 6291460
  40.8 1.3 copy-start.4
  40.8 2.0 %copy-start.8 = (bf16[4,8,128,256]{3,2,1,0:T(8,128)(2,1)}, bf16[4,8,128,256]{3,2,1,0:T(8,128)(2,1)S(1)}, u32[]{:S(2)}) copy-start(bf16[4,8,128,256]{3,2,1,0:T(8,128)(2,1)S(1)} %get-tuple-element.48) | copy-start | bytes 6291460
  40.8 2.0 %copy-start.12 = (s32[258]{0:T(512)S(1)}, s32[258]{0:T(512)}, u32[]{:S(2)}) copy-start(s32[258]{0:T(512)} %list_pairs.1.pairs_ref) | copy-start | bytes 3100
  40.8 2.0 %copy-start.13 = (f32[8,256]{1,0:T(8,128)S(1)}, f32[8,256]{1,0:T(8,128)}, u32[]{:S(2)}) copy-start(f32[8,256]{1,0:T(8,128)} %far_ref.6) | copy-start | bytes 24580
  42.8 1.6 %copy-start.5 = (bf16[4,8,256,128]{3,2,1,0:T(8,128)(2,1)S(1)}, bf16[4,8,256,128]{3,2,1,0:T(8,128)(2,1)}, u32[]{:S(2)}) copy-start(bf16[4,8,256,128]{3,2,1,0:T(8,128)(2,1)} %copy-done.4) | copy-start | bytes 6291460
  44.4 36.0 %copy-start.9 = (bf16[4,8,128,256]{3,2,1,0:T(8,128)(2,1)S(1)}, bf16[4,8,128,256]{3,2,1,0:T(8,128)(2,1)}, u32[]{:S(2)}) copy-start(bf16[4,8,128,256]{3,2,1,0:T(8,128)(2,1)} %copy-done.8) | copy-start | bytes 6291460
  44.4 36.0 %copy-start.14 = (f32[8,256]{1,0:T(8,128)S(1)}, f32[8,256]{1,0:T(8,128)}, u32[]{:S(2)}) copy-start(f32[8,256]{1,0:T(8,128)} %far_ref.7) | copy-start | bytes 24580
  73.1 6.0 %collective-permute-start.10 = (f32[2,32,256]{2,1,0:T(8,128)S(1)}, f32[2,32,256]{2,1,0:T(8,128)S(1)}, u32[]{:S(2)}, u32[]{:S(2)}) collective-permute-start(f32[2,32,256]{2,1,0:T(8,128)S(1)} %tiles.4), channel_id=1, source_target_pairs={{0,8},{1,9},{2,10},{3,11},{4,12},{5,13},{6,14},{7,15},{8,0},{9,1},... | collective-permute-start | bytes 196616 | tf_op jit(solution)/shard_map/ppermute | solution.py:249
  79.1 1.3 collective-permute-start.11
  95.1 3.9 %collective-permute-start.12 = (f32[32,256]{1,0:T(8,128)S(1)}, f32[32,256]{1,0:T(8,128)S(1)}, u32[]{:S(2)}, u32[]{:S(2)}) collective-permute-start(f32[32,256]{1,0:T(8,128)S(1)} %get-tuple-element.53), channel_id=1, source_target_pairs={{0,4},{1,5},{2,6},{3,7},{4,0},{5,1},{6,2},{7,3},{8,12},{9,13},{10,... | collective-permute-start | bytes 98312 | tf_op jit(solution)/shard_map/ppermute | solution.py:249
  99.0 4.0 %collective-permute-start.13 = (f32[32,256]{1,0:T(8,128)S(1)}, f32[32,256]{1,0:T(8,128)S(1)}, u32[]{:S(2)}, u32[]{:S(2)}) collective-permute-start(f32[32,256]{1,0:T(8,128)S(1)} %maximum_add_fusion.1.pot_ref), channel_id=1, source_target_pairs={{0,2},{1,3},{2,0},{3,1},{4,6},{5,7},{6,4},{7,5},{8,10},{9,11},{10,... | collective-permute-start | bytes 98312 | tf_op jit(solution)/shard_map/ppermute | solution.py:249
  117.1 4.9 %collective-permute-start.14 = (f32[32,256]{1,0:T(8,128)S(1)}, f32[32,256]{1,0:T(8,128)S(1)}, u32[]{:S(2)}, u32[]{:S(2)}) collective-permute-start(f32[32,256]{1,0:T(8,128)S(1)} %tiles.6), channel_id=1, source_target_pairs={{0,8},{1,9},{2,10},{3,11},{4,12},{5,13},{6,14},{7,15},{8,0},{9,1},... | collective-permute-start | bytes 98312 | tf_op jit(solution)/shard_map/ppermute | solution.py:249
  122.0 1.3 collective-permute-start.15
  137.9 3.9 %collective-permute-start.16 = (f32[32,256]{1,0:T(8,128)S(1)}, f32[32,256]{1,0:T(8,128)S(1)}, u32[]{:S(2)}, u32[]{:S(2)}) collective-permute-start(f32[32,256]{1,0:T(8,128)S(1)} %get-tuple-element.55), channel_id=1, source_target_pairs={{0,4},{1,5},{2,6},{3,7},{4,0},{5,1},{6,2},{7,3},{8,12},{9,13},{10,... | collective-permute-start | bytes 98312 | tf_op jit(solution)/shard_map/ppermute | solution.py:249
  141.8 4.0 %collective-permute-start.17 = (f32[32,256]{1,0:T(8,128)S(1)}, f32[32,256]{1,0:T(8,128)S(1)}, u32[]{:S(2)}, u32[]{:S(2)}) collective-permute-start(f32[32,256]{1,0:T(8,128)S(1)} %maximum_add_fusion.3), channel_id=1, source_target_pairs={{0,2},{1,3},{2,0},{3,1},{4,6},{5,7},{6,4},{7,5},{8,10},{9,11},{10,... | collective-permute-start | bytes 98312 | tf_op jit(solution)/shard_map/ppermute | solution.py:249
  (1 other events, 0.9 us)

commit v2 on v1

v2 whole, which is shorter than its diff:
```python
import functools
import math

import jax
import jax.numpy as jnp
from jax import lax
from jax.experimental import pallas as pl
from jax.experimental.pallas import tpu as pltpu
from jax.sharding import PartitionSpec as P

ITERS = 2
SCALE_EPS = 0.25
KEEP_TAU = 0.8
INV_EPS = 1.0 / SCALE_EPS

LOW_OFFSET = 60.0
LOW_TOP = 130.0
HIGH_OFFSET = 200.0
COLUMN_TOP = -KEEP_TAU * 10.0
LOG_LARGEST = 88.4

NOTHING = -1e30

DEPTH = 128
GROUP = 64
EXTRA = 32
VMEM = 12 * 1024 * 1024
SMALL = 1024 * 1024
LARGE = 60 * 1024 * 1024


def split3(value):
    high = value.astype(jnp.bfloat16).astype(jnp.float32)
    rest = value - high
    mid = rest.astype(jnp.bfloat16).astype(jnp.float32)
    return high, mid, rest - mid


def pack(points, *rows):
    clusters, dims, size = points[0].shape
    counts = [len(r) for r in rows]
    tall = clusters * dims

    flat = [p.reshape(tall, size) for p in points]
    few = [r for r in rows for r in r]

    def body(*refs):
        points_refs, refs = refs[:len(points)], refs[len(points):]
        few_refs, refs = refs[:len(few)], refs[len(few):]
        out_refs, refs = refs[:len(points)], refs[len(points):]
        held_refs, sems = refs[:-1], refs[-1]
        copies = [pltpu.make_async_copy(p, o.at[:tall], sems.at[i]) for i, (p, o) in enumerate(zip(points_refs, out_refs))]
        loads = [pltpu.make_async_copy(f, h, sems.at[len(copies) + i]) for i, (f, h) in enumerate(zip(few_refs, held_refs))]
        for copy in loads + copies:
            copy.start()
        for copy in loads:
            copy.wait()
        held = list(held_refs)
        for i, n in enumerate(counts):
            mine, held = held[:n], held[n:]
            if n > 1:
                values = [ref[...].astype(jnp.float32) for ref in mine]
                values = [jnp.concatenate([v, jnp.zeros((v.shape[0], size - v.shape[1]), jnp.float32)], axis=1) for v in values]
            else:
                values = list(split3(mine[0][...]))
            empty = EXTRA - sum(v.shape[0] for v in values)
            if empty:
                values.append(jnp.zeros((empty, size), jnp.float32))
            out_refs[i][tall:, :] = jnp.concatenate(values, axis=0).astype(jnp.bfloat16)
        for copy in copies:
            copy.wait()

    return pl.pallas_call(
        body,
        out_shape=[jax.ShapeDtypeStruct((tall + EXTRA, size), p.dtype) for p in points],
        in_specs=[pl.BlockSpec(memory_space=pltpu.HBM)] * (len(points) + len(few)),
        out_specs=[pl.BlockSpec(memory_space=pltpu.VMEM)] * len(points),
        scratch_shapes=[pltpu.VMEM(f.shape, f.dtype) for f in few] + [pltpu.SemaphoreType.DMA((len(points) + len(few),))],
        compiler_params=pltpu.CompilerParams(vmem_limit_bytes=LARGE),
        name="pack",
    )(*flat, *few)


def prepare(blocks, clusters, count, state):
    rows, size = blocks[0][0].shape
    tall = rows - EXTRA
    dims = tall // clusters
    places = [place for _, place in blocks]

    def body(*refs):
        points_refs = refs[:len(blocks)]
        lhs_ref, rhs_ref, half_ref, extra_ref = refs[-4:]
        row = lax.broadcasted_iota(jnp.int32, (DEPTH - dims, size), 0)
        ones = jnp.where(row < 3, 1.0, 0.0).astype(jnp.float32)

        def write(points_ref):
            extra = points_ref[tall:, :].astype(jnp.float32)
            extra_ref[0] = extra[:clusters] + extra[clusters:2 * clusters] + extra[2 * clusters:3 * clusters]

            def one(c, carry):
                raw = points_ref[pl.ds(pl.multiple_of(c * dims, dims), dims), :]
                wide = raw.astype(jnp.float32)
                half = 0.5 * jnp.sum(wide * wide, axis=0, keepdims=True)
                half_ref[0, pl.ds(c, 1), :] = half
                high, mid, low = split3(-INV_EPS * half)
                extra = jnp.where(row == 0, high, jnp.where(row == 1, mid, jnp.where(row == 2, low, 0.0)))
                rhs_ref[0, c, :dims, :] = raw
                rhs_ref[0, c, dims:, :] = extra.astype(jnp.bfloat16)
                lhs_ref[0, c] = jnp.concatenate([INV_EPS * wide, ones], axis=0).T.astype(jnp.bfloat16)
                return carry

            lax.fori_loop(0, clusters, one, 0, unroll=2)

        for i, points_ref in enumerate(points_refs):
            pl.when(pl.program_id(0) == i)(functools.partial(write, points_ref))

    def place_of(i):
        chosen = places[0]
        for j, place in enumerate(places[1:]):
            chosen = jnp.where(i > j, place, chosen)
        return chosen

    shapes = (
        jax.ShapeDtypeStruct((count, clusters, size, DEPTH), jnp.bfloat16),
        jax.ShapeDtypeStruct((count, clusters, DEPTH, size), jnp.bfloat16),
        jax.ShapeDtypeStruct((count, clusters, size), jnp.float32),
        jax.ShapeDtypeStruct((count, clusters, size), jnp.float32),
    )
    used = len(blocks)
    extra_specs = [] if state is None else [pl.BlockSpec(memory_space=pl.ANY)] * 4
    return pl.pallas_call(
        body,
        grid=(used,),
        out_shape=shapes,
        in_specs=[pl.BlockSpec((rows, size), lambda i: (0, 0))] * used + extra_specs,
        out_specs=(
            pl.BlockSpec((1, clusters, size, DEPTH), lambda i: (place_of(i), 0, 0, 0)),
            pl.BlockSpec((1, clusters, DEPTH, size), lambda i: (place_of(i), 0, 0, 0)),
            pl.BlockSpec((1, clusters, size), lambda i: (place_of(i), 0, 0)),
            pl.BlockSpec((1, clusters, size), lambda i: (place_of(i), 0, 0)),
        ),
        input_output_aliases={} if state is None else {used + i: i for i in range(4)},
        compiler_params=pltpu.CompilerParams(vmem_limit_bytes=VMEM),
        cost_estimate=pl.CostEstimate(
            flops=used * clusters * dims * size * 4, bytes_accessed=used * clusters * size * DEPTH * 8, transcendentals=0
        ),
        name="prepare",
    )(*[points for points, _ in blocks], *(() if state is None else state))


def list_pairs(entries):
    rows, width = entries.shape

    def body(entries_ref, out_ref):
        def one(r, filled):
            for k in range(width):
                entry = entries_ref[r, k]
                out_ref[filled] = entry
                filled = filled + jnp.where(entry >= 0, 1, 0).astype(jnp.int32)
            return filled

        filled = lax.fori_loop(0, rows - 1, one, jnp.int32(1))
        out_ref[0] = filled - 1
        last = entries_ref[rows - 1, 0]
        for extra in range(GROUP):
            out_ref[filled + extra] = last

    return pl.pallas_call(
        body,
        out_shape=jax.ShapeDtypeStruct((rows * width + 1 + GROUP,), jnp.int32),
        in_specs=[pl.BlockSpec(memory_space=pltpu.SMEM)],
        out_specs=pl.BlockSpec(memory_space=pltpu.SMEM),
        compiler_params=pltpu.CompilerParams(vmem_limit_bytes=SMALL),
        cost_estimate=pl.CostEstimate(flops=0, bytes_accessed=4 << 20, transcendentals=0),
        name="list_pairs",
    )(entries)


def padded_rows(rows):
    return -(-3 * rows // 128) * 128


def sum_pairs(pairs_ref, lhs_ref, rhs_ref, sources, values, extra_ref, acc_ref, by_source, adjust=lambda term: term):
    size = lhs_ref.shape[1]
    targets = lhs_ref.shape[0] - sources
    count, others = (targets, sources) if by_source else (sources, targets)
    lhs_base, rhs_base = (sources, 0) if by_source else (0, sources)
    wide = extra_ref.shape[1]
    parts = list(split3(values))
    if wide > 3 * count:
        parts.append(jnp.zeros((wide - 3 * count, size), jnp.float32))
    extra_ref[...] = jnp.concatenate(parts, axis=0).T.astype(jnp.bfloat16)
    acc_ref[...] = jnp.zeros_like(acc_ref)
    row = lax.broadcasted_iota(jnp.int32, (wide, size), 0)
    row = jnp.where(row < 3 * count, lax.rem(row, count), count)

    def step(g, carry):
        for u in range(GROUP):
            code = pairs_ref[g * GROUP + u + 1]
            s, t = lax.div(code, 2 * targets), lax.rem(code, 2 * targets)
            m, place = (t, s) if by_source else (s, t)
            m, n = jnp.minimum(m, count - 1), jnp.minimum(place, others - 1)
            chosen = jnp.where(row == m, 1.0, 0.0).astype(jnp.bfloat16)
            term = jnp.dot(
                jnp.concatenate([lhs_ref[lhs_base + m], extra_ref[...]], axis=1),
                jnp.concatenate([rhs_ref[rhs_base + n], chosen], axis=0),
                preferred_element_type=jnp.float32,
            )
            acc_ref[place] += jnp.sum(jnp.exp(adjust(term)).reshape(size // 8, 8, size), axis=0)
        return carry

    lax.fori_loop(0, lax.div(pairs_ref[0] + (GROUP - 1), GROUP), step, 0)
    return jnp.sum(acc_ref[:others], axis=1)


def moved(block, home, rows):
    return pl.ds(pl.multiple_of((block ^ home) * rows, rows), rows)


def store_sums(sums, home, out_ref, far):
    rows = far.shape[0]
    for block in range(sums.shape[0] // rows):
        part = sums[block * rows:(block + 1) * rows]
        out_ref[moved(block, home, rows), :] = part + far if block == 0 else part


def load_sums(sums_refs, home, rows):
    blocks = []
    for block in range(sums_refs[0].shape[-2] // rows):
        blocks.append(sum(ref[moved(block, home, rows), :] for ref in sums_refs))
    return jnp.concatenate(blocks, axis=0)


def row_kernel(terms, sources, first, pairs_ref, home_ref, lhs_ref, rhs_ref, half_ref, far_ref, *refs):
    pot_refs, (out_ref, extra_ref, acc_ref) = refs[:-3], refs[-3:]
    if first:
        pot = pot_refs[0][sources:, :]
    else:
        pot = -KEEP_TAU * SCALE_EPS * (jnp.log(load_sums(pot_refs, home_ref[1], far_ref.shape[0])) - column_offset(terms))
    values = INV_EPS * (pot - half_ref[sources:, :]) - LOW_OFFSET
    run = functools.partial(sum_pairs, pairs_ref, lhs_ref, rhs_ref, sources, values, extra_ref, acc_ref, True)
    far = jnp.exp(far_ref[...] - LOW_OFFSET)
    if not first:
        store_sums(run(), home_ref[0], out_ref, far)
        return
    own = far_ref.shape[0]

    def store_logs(low, high=None):
        low = jnp.concatenate([low[:own] + far, low[own:]], axis=0)
        logs = log_or_nothing(low) + LOW_OFFSET
        if high is not None:
            high = log_or_nothing(high) + HIGH_OFFSET
            top = jnp.maximum(logs, high)
            logs = top + jnp.log(jnp.exp(logs - top) + jnp.exp(high - top))
        store_sums(logs, home_ref[0], out_ref, jnp.zeros_like(far))

    narrow = jnp.max(pot) <= LOW_TOP * SCALE_EPS

    @pl.when(narrow)
    def _():
        store_logs(run())

    @pl.when(jnp.logical_not(narrow))
    def _():
        edge = LOW_TOP - LOW_OFFSET
        low = run(lambda term: jnp.where(term <= edge, term, NOTHING))
        store_logs(low, run(lambda term: jnp.where(term > edge, term - (HIGH_OFFSET - LOW_OFFSET), NOTHING)))


def log_or_nothing(value):
    return jnp.where(value > 0.0, jnp.log(jnp.where(value > 0.0, value, 1.0)), NOTHING)


def column_offset(terms):
    return LOG_LARGEST - COLUMN_TOP - math.log(terms)


def column_kernel(terms, sources, first, pairs_ref, home_ref, lhs_ref, rhs_ref, half_ref, far_ref, sums_ref, out_ref, pot_ref, extra_ref, acc_ref):
    parts, own = range(sums_ref.shape[0]), pot_ref.shape[0]
    if first:
        logs = [load_sums([sums_ref.at[i]], home_ref[0], own) for i in parts]
        top = functools.reduce(jnp.maximum, logs)
        log_sum = top + jnp.log(sum(jnp.exp(log - top) for log in logs))
    else:
        log_sum = jnp.log(load_sums([sums_ref.at[i] for i in parts], home_ref[0], own)) + LOW_OFFSET
    pot = -KEEP_TAU * SCALE_EPS * log_sum
    values = INV_EPS * (pot - half_ref[:sources, :]) + column_offset(terms)
    total = sum_pairs(pairs_ref, lhs_ref, rhs_ref, sources, values, extra_ref, acc_ref, False)
    store_sums(total, home_ref[1], out_ref, jnp.exp(far_ref[...] + column_offset(terms)))
    pot_ref[...] = pot[:own]


def run_pass(kernel, out_shapes, pairs, home, state, width, others, tiles, *rest):
    size = state[0].shape[1]
    space = pl.BlockSpec(memory_space=pltpu.VMEM)
    return pl.pallas_call(
        kernel,
        out_shape=out_shapes,
        in_specs=[pl.BlockSpec(memory_space=pltpu.SMEM)] * 2 + [space] * (3 + len(rest)),
        out_specs=jax.tree.map(lambda _: space, out_shapes),
        scratch_shapes=[
            pltpu.VMEM((size, padded_rows(width)), jnp.bfloat16),
            pltpu.VMEM((others + 1, 8, size), jnp.float32),
        ],
        compiler_params=pltpu.CompilerParams(vmem_limit_bytes=VMEM),
        cost_estimate=pl.CostEstimate(
            flops=2 * tiles * size * size * DEPTH, bytes_accessed=8 << 20, transcendentals=tiles * size * size
        ),
        name="tiles",
    )(pairs, home, *state, *rest)


def per_device(src_points, tgt_points, g_init, far_src, far_tgt, cand_owner, cand_local):
    src_count, _, size = src_points.shape
    tgt_count = tgt_points.shape[0]
    per_cluster = cand_owner.shape[1]
    shards = lax.axis_size("src")
    bits = shards.bit_length() - 1
    upper = max(bits // 2 - 1, 0)
    source_bits = [0] + [b for b in range(bits - upper, bits)]
    target_bits = [b for b in range(1, bits - upper)]
    nr, nc = 1 << len(source_bits), 1 << len(target_bits)
    capacity = max(2, min(src_count // 2, 2 * src_count * per_cluster // shards))
    terms = shards * capacity * size

    def across(array, *which):
        apart = sum(1 << bit for bit in which)
        return lax.ppermute(array, "src", [(i, i ^ apart) for i in range(shards)])

    def doubled(array, which):
        blocks = {0: array}
        for place, bit in reversed(list(enumerate(which))):
            blocks.update({at | 1 << place: across(block, bit) for at, block in list(blocks.items())})
        return [blocks[at] for at in range(1 << len(which))]

    def groups(which):
        masks = [sum(1 << bit for place, bit in enumerate(which) if i >> place & 1) for i in range(1 << len(which))]
        return [[base | m for m in masks] for base in range(shards) if not base & sum(1 << b for b in which)]

    def place_of(device, which):
        return sum(((device >> bit) & 1) << place for place, bit in enumerate(which))

    tall = src_count * src_points.shape[1]
    sources, targets = nr * src_count, nc * tgt_count
    me = lax.axis_index("src").astype(jnp.int32)
    home = jnp.stack([place_of(me, source_bits), place_of(me, target_bits)])
    src_message, tgt_message = pack((src_points, tgt_points), (cand_owner, cand_local), (g_init,))
    src_blocks = doubled(src_message, source_bits)
    tgt_blocks = doubled(tgt_message, target_bits)
    state = None
    order = lambda blocks: sorted(range(len(blocks)), key=lambda at: (at.bit_count(), at))
    src_order, tgt_order = order(src_blocks), order(tgt_blocks)
    for i in range(max(nr, nc)):
        blocks = [(src_blocks[at], at) for at in src_order[i:i + 1]] + [(tgt_blocks[at], nr + at) for at in tgt_order[i:i + 1]]
        state = prepare(blocks, src_count, nr + nc, state)
    *state, extra = [a.reshape((-1,) + a.shape[2:]) for a in state]

    owner = jnp.concatenate([b[tall:tall + src_count, :per_cluster] for b in src_blocks], axis=0).astype(jnp.int32)
    local = jnp.concatenate([b[tall + src_count:tall + 2 * src_count, :per_cluster] for b in src_blocks], axis=0).astype(jnp.int32)
    inside = ((owner ^ me) & ~sum(1 << b for b in target_bits)) == 0
    row = lax.broadcasted_iota(jnp.int32, (sources, per_cluster), 0)
    entries = jnp.where(inside, row * (2 * targets) + place_of(owner ^ me, target_bits) * tgt_count + local, -1)
    nobody = jnp.full((1, per_cluster), sources * (2 * targets) + targets, jnp.int32)
    pairs = list_pairs(jnp.concatenate([entries, nobody], axis=0))
    pots = [extra]

    f32 = jnp.float32
    tiles = src_count * per_cluster
    for iteration in range(ITERS):
        first = iteration == 0
        sums = run_pass(
            functools.partial(row_kernel, terms, sources, first),
            jax.ShapeDtypeStruct((sources, size), f32),
            pairs, home, state, targets, sources, tiles, far_src, *pots,
        )
        sums = lax.all_gather(sums, "src", axis_index_groups=groups(source_bits))
        column, src_pot = run_pass(
            functools.partial(column_kernel, terms, sources, first),
            (jax.ShapeDtypeStruct((targets, size), f32), jax.ShapeDtypeStruct((src_count, size), f32)),
            pairs, home, state, sources, targets, tiles, far_tgt, sums,
        )
        if iteration + 1 < ITERS:
            for bit in target_bits[:-1]:
                column = column + across(column, bit)
            pots = [column, across(column, target_bits[-1])]
    column = lax.all_to_all(
        column.reshape(nc, tgt_count, size), "src", 0, 0, tiled=True, axis_index_groups=groups(target_bits)
    )
    tgt_pot = -KEEP_TAU * SCALE_EPS * (jnp.log(jnp.sum(column, axis=0)) - column_offset(terms))
    return (src_pot, tgt_pot)


def solution(mesh):
    return jax.shard_map(
        per_device,
        mesh=mesh,
        in_specs=(
            P(("groups", "src"), None, None),
            P(("groups", "src"), None, None),
            P(("groups", "src"), None),
            P(("groups", "src"), None),
            P(("groups", "src"), None),
            P(("groups", "src"), None),
            P(("groups", "src"), None),
        ),
        out_specs=(P(("groups", "src"), None), P(("groups", "src"), None)),
        check_vma=False,
    )
```

time: 147 us -> 79.4 us (0.54)
  Pallas kernels: 80 us -> 27 us
  blocking collectives: 0 us -> 20.8 us
  waiting for transfers between devices: 34.9 us -> 15.9 us
  local copies, waits for them, and re-layouts: 15.6 us -> 2.62 us
  starting transfers between devices: 12.9 us -> 11.2 us
    pallas_call x4, Pallas kernels: 72 us -> 19.2 us  [run_pass(): pl.pallas_call(kernel, out_shape=out_shapes, in_specs=[pl.BlockSpec(memor...]
    ppermute x18 -> x8, waiting for transfers between devices: 34.9 us -> 15.9 us  [across(): return lax.ppermute(array, 'src', [(i, i ^ apart) for i in range(shards)])]
    all_gather x0 -> x2, blocking collectives: none -> 13.4 us  [per_device(): sums = lax.all_gather(sums, 'src', axis_index_groups=groups(source_bits))]
    unnamed x32 -> x8, local copies, waits for them, and re-layouts: 14.9 us -> 1.92 us
    all_to_all x0 -> x1, blocking collectives: none -> 7.47 us  [per_device(): lax.all_to_all(column.reshape(nc, tgt_count, size), 'src', 0, 0, tiled=Tr...]
    ppermute x18 -> x8, starting transfers between devices: 12.9 us -> 11.2 us  [across(): return lax.ppermute(array, 'src', [(i, i ^ apart) for i in range(shards)])]
    concatenate x4 -> x0, other arithmetic: 1.55 us -> none  [grown(): array = jnp.concatenate([array, across(array, bit)], axis=0)]
    pallas_call x9 -> x6, Pallas kernels: 7.99 us -> 7.77 us  [the longest x4 3.64 us: prepare(): pl.pallas_call(body, grid=(used,), out_shape=shapes, in_specs=[pl.BlockSp...]
  transfers between devices with their start and end apart: 18 -> 8, of which waited for: 11 -> 5; matrix products, arithmetic and copies ran while one was open for 3% -> 1% of each run, Pallas kernels for 5% -> 6%
where the time goes in v2:
time: 79.4 us; the launch traced here: 79.1 us
  Pallas kernels  27 us (34%)
  blocking collectives  20.8 us (26%)
  waiting for transfers between devices  15.9 us (20%)
  starting transfers between devices  11.2 us (14%)
  local copies, waits for them, and re-layouts  2.62 us (3%)
    pallas_call x4, Pallas kernels, run_pass(): pl.pallas_call(kernel, out_shape=out_shapes, in_specs=[pl.BlockSpec(memor...  19.2 us
    ppermute x8, waiting for transfers between devices, across(): return lax.ppermute(array, 'src', [(i, i ^ apart) for i in range(shards)])  15.9 us
    all_gather x2, blocking collectives, per_device(): sums = lax.all_gather(sums, 'src', axis_index_groups=groups(source_bits))  13.4 us
    ppermute x8, starting transfers between devices, across(): return lax.ppermute(array, 'src', [(i, i ^ apart) for i in range(shards)])  11.2 us
    all_to_all x1, blocking collectives, per_device(): lax.all_to_all(column.reshape(nc, tgt_count, size), 'src', 0, 0, tiled=Tr...  7.47 us
    pallas_call x4, Pallas kernels, prepare(): pl.pallas_call(body, grid=(used,), out_shape=shapes, in_specs=[pl.BlockSp...  3.64 us
    pallas_call x1, Pallas kernels, list_pairs(): pl.pallas_call(body, out_shape=jax.ShapeDtypeStruct((rows * width + 1 + G...  2.19 us
    pallas_call x1, Pallas kernels, pack(): pl.pallas_call(body, out_shape=[jax.ShapeDtypeStruct((tall + EXTRA, size)...  1.94 us
  transfers between devices with their start and end apart: 8, of which 5 were waited for; matrix products, arithmetic and copies ran while one was open for 1% of the time, Pallas kernels for 6%

profile of v2, /device:TPU:0, one launch (start us, length us, event | category | flops | bytes accessed | tf_op | source)
XLA Modules:
  0.0 79.1 jit_solution(11677265107140800300)
XLA Ops:
  0.6 1.9 %pack.1 = (bf16[544,256]{1,0:T(8,128)(2,1)}, bf16[544,256]{1,0:T(8,128)(2,1)}) custom-call(bf16[512,256]{1,0:T(8,128)(2,1)} %bitcast.27, bf16[512,256]{1,0:T(8,128)(2,1)} %bitcast.28, s32[8,8]{1,0:T(8,128)} %refs_2_.1, s32[8,8]{1,0:T(8,128)} %refs_3_.1, f32[8,256]{1,0:T(8,128)} %refs_4_.1), custom_call_target="tpu_custom_call" | custom-call | tf_op jit(solution)/shard_map/pack/pallas_call | solution.py:73
  2.6 0.5 collective-permute-start
  3.1 3.7 %collective-permute-start.1 = (bf16[544,256]{1,0:T(8,128)(2,1)}, bf16[544,256]{1,0:T(8,128)(2,1)S(1)}, u32[]{:S(2)}, u32[]{:S(2)}) collective-permute-start(bf16[544,256]{1,0:T(8,128)(2,1)} %get-tuple-element.23.refs_0_), channel_id=1, source_target_pairs={{0,8},{1,9},{2,10},{3,11},{4,12},{5,13},{6,14},{7,15},{8,0},{9,1},... | collective-permute-start | bytes 835592 | tf_op jit(solution)/shard_map/ppermute | solution.py:328
  6.8 1.5 %collective-permute-start.5 = (bf16[544,256]{1,0:T(8,128)(2,1)}, bf16[544,256]{1,0:T(8,128)(2,1)S(1)}, u32[]{:S(2)}, u32[]{:S(2)}) collective-permute-start(bf16[544,256]{1,0:T(8,128)(2,1)} %get-tuple-element.24.refs_1_), channel_id=1, source_target_pairs={{0,2},{1,3},{2,0},{3,1},{4,6},{5,7},{6,4},{7,5},{8,10},{9,11},{10,... | collective-permute-start | bytes 835592 | tf_op jit(solution)/shard_map/ppermute | solution.py:328
  8.2 1.6 %collective-permute-start.3 = (bf16[544,256]{1,0:T(8,128)(2,1)}, bf16[544,256]{1,0:T(8,128)(2,1)S(1)}, u32[]{:S(2)}, u32[]{:S(2)}) collective-permute-start(bf16[544,256]{1,0:T(8,128)(2,1)} %get-tuple-element.24.refs_1_), channel_id=1, source_target_pairs={{0,4},{1,5},{2,6},{3,7},{4,0},{5,1},{6,2},{7,3},{8,12},{9,13},{10,... | collective-permute-start | bytes 835592 | tf_op jit(solution)/shard_map/ppermute | solution.py:328
  9.8 0.7 fusion
  10.5 0.1 pad_add_fusion.home_ref
  10.6 1.0 %copy-done = bf16[544,256]{1,0:T(8,128)(2,1)S(1)} copy-done((bf16[544,256]{1,0:T(8,128)(2,1)S(1)}, bf16[544,256]{1,0:T(8,128)(2,1)}, u32[]{:S(2)}) %copy-start) | copy-done | bytes 278552
  11.5 1.0 %copy-done.1 = bf16[544,256]{1,0:T(8,128)(2,1)S(1)} copy-done((bf16[544,256]{1,0:T(8,128)(2,1)S(1)}, bf16[544,256]{1,0:T(8,128)(2,1)}, u32[]{:S(2)}) %copy-start.1) | copy-done | bytes 278552
  12.5 0.9 %prepare.4 = (bf16[8,8,256,128]{3,2,1,0:T(8,128)(2,1)S(1)}, bf16[8,8,128,256]{3,2,1,0:T(8,128)(2,1)S(1)}, f32[8,8,256]{2,1,0:T(8,128)S(1)}, f32[8,8,256]{2,1,0:T(8,128)S(1)}) custom-call(bf16[544,256]{1,0:T(8,128)(2,1)S(1)} %copy-done, bf16[544,256]{1,0:T(8,128)(2,1)S(1)} %copy-done.1), custom_call_target="tpu_custom_call" | custom-call | flops 1048576 | bytes 4194304 | tf_op jit(solution)/shard_map/prepare/pallas_call | solution.py:131
  13.4 6.9 %collective-permute-done.1.refs_0_ = bf16[544,256]{1,0:T(8,128)(2,1)S(1)} collective-permute-done((bf16[544,256]{1,0:T(8,128)(2,1)}, bf16[544,256]{1,0:T(8,128)(2,1)S(1)}, u32[]{:S(2)}, u32[]{:S(2)}) %collective-permute-start.1) | collective-permute-done | bytes 278560 | tf_op jit(solution)/shard_map/ppermute | solution.py:328
  20.3 1.4 %collective-permute-done.3.refs_1_ = bf16[544,256]{1,0:T(8,128)(2,1)S(1)} collective-permute-done((bf16[544,256]{1,0:T(8,128)(2,1)}, bf16[544,256]{1,0:T(8,128)(2,1)S(1)}, u32[]{:S(2)}, u32[]{:S(2)}) %collective-permute-start.3) | collective-permute-done | bytes 278560 | tf_op jit(solution)/shard_map/ppermute | solution.py:328
  21.7 0.6 collective-permute-start.4
  22.3 0.9 %prepare.5 = (bf16[8,8,256,128]{3,2,1,0:T(8,128)(2,1)S(1)}, bf16[8,8,128,256]{3,2,1,0:T(8,128)(2,1)S(1)}, f32[8,8,256]{2,1,0:T(8,128)S(1)}, f32[8,8,256]{2,1,0:T(8,128)S(1)}) custom-call(bf16[544,256]{1,0:T(8,128)(2,1)S(1)} %collective-permute-done.refs_0_, ...), custom_call_target="tpu_custom_call", output_to_operand_aliasing={{0}: (2, {}), {1}: (3, {}), {2}: (4, {}), {3}: (5, {})} | custom-call | flops 1048576 | bytes 4194304 | tf_op jit(solution)/shard_map/prepare/pallas_call | solution.py:131
  23.2 0.9 %prepare.6 = (bf16[8,8,256,128]{3,2,1,0:T(8,128)(2,1)S(1)}, bf16[8,8,128,256]{3,2,1,0:T(8,128)(2,1)S(1)}, f32[8,8,256]{2,1,0:T(8,128)S(1)}, f32[8,8,256]{2,1,0:T(8,128)S(1)}) custom-call(bf16[544,256]{1,0:T(8,128)(2,1)S(1)} %collective-permute-done.1.refs_0_, ...), custom_call_target="tpu_custom_call", output_to_operand_aliasing={{0}: (2, {}), {1}: (3, {}), {2}: (4, {}), {3}: (5, {})} | custom-call | flops 1048576 | bytes 4194304 | tf_op jit(solution)/shard_map/prepare/pallas_call | solution.py:131
  24.2 0.1 add_select_fusion
  24.3 2.2 %list_pairs.1.pairs_ref = s32[329]{0:T(512)S(1)} custom-call(s32[33,8]{1,0:T(8,128)S(1)} %concatenate.11.entries_ref), custom_call_target="tpu_custom_call" | custom-call | bytes 4194304 | tf_op jit(solution)/shard_map/list_pairs/pallas_call | solution.py:168
  26.5 2.9 %collective-permute-done.4.refs_1_ = bf16[544,256]{1,0:T(8,128)(2,1)S(1)} collective-permute-done((bf16[544,256]{1,0:T(8,128)(2,1)S(1)}, bf16[544,256]{1,0:T(8,128)(2,1)S(1)}, u32[]{:S(2)}, u32[]{:S(2)}) %collective-permute-start.4) | collective-permute-done | bytes 278560 | tf_op jit(solution)/shard_map/ppermute | solution.py:328
  29.4 0.9 %prepare.7 = (bf16[8,8,256,128]{3,2,1,0:T(8,128)(2,1)S(1)}, bf16[8,8,128,256]{3,2,1,0:T(8,128)(2,1)S(1)}, f32[8,8,256]{2,1,0:T(8,128)S(1)}, f32[8,8,256]{2,1,0:T(8,128)S(1)}) custom-call(bf16[544,256]{1,0:T(8,128)(2,1)S(1)} %collective-permute-done.2.refs_0_, ...), custom_call_target="tpu_custom_call", output_to_operand_aliasing={{0}: (2, {}), {1}: (3, {}), {2}: (4, {}), {3}: (5, {})} | custom-call | flops 1048576 | bytes 4194304 | tf_op jit(solution)/shard_map/prepare/pallas_call | solution.py:131
  30.3 0.0 copy-start.3
  30.3 8.6 %tiles.4 = f32[32,256]{1,0:T(8,128)S(1)} custom-call(s32[329]{0:T(512)S(1)} %list_pairs.1.pairs_ref, s32[2]{0:T(128)S(1)} %pad_add_fusion.home_ref, bf16[64,256,128]{2,1,0:T(8,128)(2,1)S(1)} %bitcast.11, bf16[64,128,256]{2,1,0:T(8,128)(2,1)S(1)} %bitcast.15, f32[64,256]{1,0:T(8,128)S(1)} %bitcast.19, f32[8,256]{1,0:T(8,128)S(1)} %copy-done.2, ...), custom_call_target="tpu_custom_call" | custom-call | flops 1073741824 | bytes 8388608 | tf_op jit(solution)/shard_map/tiles/pallas_call | solution.py:296
  38.9 6.3 %all-gather = f32[128,256]{1,0:T(8,128)S(1)} all-gather(f32[32,256]{1,0:T(8,128)S(1)} %tiles.4), channel_id=2, replica_groups={{0,1,8,9},{2,3,10,11},{4,5,12,13},{6,7,14,15},{16,17,24,25},{18,19,26,2..., dimensions={0}, use_global_device_ids=true | all-gather | bytes 163840 | tf_op jit(solution)/shard_map/all_gather | solution.py:376
  45.2 3.9 %tiles.5 = (f32[32,256]{1,0:T(8,128)S(1)}, f32[8,256]{1,0:T(8,128)}) custom-call(s32[329]{0:T(512)S(1)} %list_pairs.1.pairs_ref, s32[2]{0:T(128)S(1)} %pad_add_fusion.home_ref, bf16[64,256,128]{2,1,0:T(8,128)(2,1)S(1)} %bitcast.12, bf16[64,128,256]{2,1,0:T(8,128)(2,1)S(1)} %bitcast.16, f32[64,256]{1,0:T(8,128)S(1)} %bitcast.20, f32[8,256]{1,0:T(8,128)S(1)} %copy-done.3, ...), custom_call_target="tpu_custom_call" | custom-call | flops 1073741824 | bytes 8388608 | tf_op jit(solution)/shard_map/tiles/pallas_call | solution.py:296
  49.1 2.3 %collective-permute-start.6 = (f32[32,256]{1,0:T(8,128)S(1)}, f32[32,256]{1,0:T(8,128)S(1)}, u32[]{:S(2)}, u32[]{:S(2)}) collective-permute-start(f32[32,256]{1,0:T(8,128)S(1)} %get-tuple-element.41), channel_id=1, source_target_pairs={{0,2},{1,3},{2,0},{3,1},{4,6},{5,7},{6,4},{7,5},{8,10},{9,11},{10,... | collective-permute-start | bytes 98312 | tf_op jit(solution)/shard_map/ppermute | solution.py:328
  51.3 1.9 %collective-permute-done.6 = f32[32,256]{1,0:T(8,128)S(1)} collective-permute-done((f32[32,256]{1,0:T(8,128)S(1)}, f32[32,256]{1,0:T(8,128)S(1)}, u32[]{:S(2)}, u32[]{:S(2)}) %collective-permute-start.6) | collective-permute-done | bytes 32800 | tf_op jit(solution)/shard_map/ppermute | solution.py:328
  53.2 1.1 %collective-permute-start.7 = (f32[32,256]{1,0:T(8,128)S(1)}, f32[32,256]{1,0:T(8,128)S(1)}, u32[]{:S(2)}, u32[]{:S(2)}) collective-permute-start(f32[32,256]{1,0:T(8,128)S(1)} %add.26.refs_0_), channel_id=1, source_target_pairs={{0,4},{1,5},{2,6},{3,7},{4,0},{5,1},{6,2},{7,3},{8,12},{9,13},{10,... | collective-permute-start | bytes 98312 | tf_op jit(solution)/shard_map/ppermute | solution.py:328
  54.3 2.8 %collective-permute-done.7.refs_1_ = f32[32,256]{1,0:T(8,128)S(1)} collective-permute-done((f32[32,256]{1,0:T(8,128)S(1)}, f32[32,256]{1,0:T(8,128)S(1)}, u32[]{:S(2)}, u32[]{:S(2)}) %collective-permute-start.7) | collective-permute-done | bytes 32800 | tf_op jit(solution)/shard_map/ppermute | solution.py:328
  57.2 3.1 %tiles.6 = f32[32,256]{1,0:T(8,128)S(1)} custom-call(s32[329]{0:T(512)S(1)} %list_pairs.1.pairs_ref, s32[2]{0:T(128)S(1)} %pad_add_fusion.home_ref, bf16[64,256,128]{2,1,0:T(8,128)(2,1)S(1)} %bitcast.13, bf16[64,128,256]{2,1,0:T(8,128)(2,1)S(1)} %bitcast.17, f32[64,256]{1,0:T(8,128)S(1)} %bitcast.21, f32[8,256]{1,0:T(8,128)S(1)} %copy-done.2, ...), custom_call_target="tpu_custom_call" | custom-call | flops 1073741824 | bytes 8388608 | tf_op jit(solution)/shard_map/tiles/pallas_call | solution.py:296
  60.3 7.0 %all-gather.1 = f32[128,256]{1,0:T(8,128)S(1)} all-gather(f32[32,256]{1,0:T(8,128)S(1)} %tiles.6), channel_id=3, replica_groups={{0,1,8,9},{2,3,10,11},{4,5,12,13},{6,7,14,15},{16,17,24,25},{18,19,26,2..., dimensions={0}, use_global_device_ids=true | all-gather | bytes 163840 | tf_op jit(solution)/shard_map/all_gather | solution.py:376
  67.3 3.7 %tiles.7 = (f32[32,256]{1,0:T(8,128)S(1)}, f32[8,256]{1,0:T(8,128)}) custom-call(s32[329]{0:T(512)S(1)} %list_pairs.1.pairs_ref, s32[2]{0:T(128)S(1)} %pad_add_fusion.home_ref, bf16[64,256,128]{2,1,0:T(8,128)(2,1)S(1)} %bitcast.14, bf16[64,128,256]{2,1,0:T(8,128)(2,1)S(1)} %bitcast.18, f32[64,256]{1,0:T(8,128)S(1)} %bitcast.22, f32[8,256]{1,0:T(8,128)S(1)} %copy-done.3, ...), custom_call_target="tpu_custom_call" | custom-call | flops 1073741824 | bytes 8388608 | tf_op jit(solution)/shard_map/tiles/pallas_call | solution.py:296
  71.0 7.5 %all_to_all.5 = f32[4,8,256]{2,1,0:T(8,128)S(1)} all-to-all(f32[4,8,256]{2,1,0:T(8,128)S(1)} %bitcast.26), channel_id=1, replica_groups={{0,2,4,6},{1,3,5,7},{8,10,12,14},{9,11,13,15},{16,18,20,22},{17,19,21,2..., dimensions={0} | all-to-all | bytes 65536 | tf_op jit(solution)/shard_map/all_to_all | solution.py:386
  78.5 0.6 add_multiply_fusion
  (16 shorter events, 0.1 us)
Async XLA Ops:
  2.6 19.7 %collective-permute-start = (bf16[544,256]{1,0:T(8,128)(2,1)}, bf16[544,256]{1,0:T(8,128)(2,1)S(1)}, u32[]{:S(2)}, u32[]{:S(2)}) collective-permute-start(bf16[544,256]{1,0:T(8,128)(2,1)} %get-tuple-element.23.refs_0_), channel_id=1, source_target_pairs={{0,1},{1,0},{2,3},{3,2},{4,5},{5,4},{6,7},{7,6},{8,9},{9,8},{10,11... | collective-permute-start | bytes 835592 | tf_op jit(solution)/shard_map/ppermute | solution.py:328
  3.1 17.2 %collective-permute-start.1 = (bf16[544,256]{1,0:T(8,128)(2,1)}, bf16[544,256]{1,0:T(8,128)(2,1)S(1)}, u32[]{:S(2)}, u32[]{:S(2)}) collective-permute-start(bf16[544,256]{1,0:T(8,128)(2,1)} %get-tuple-element.23.refs_0_), channel_id=1, source_target_pairs={{0,8},{1,9},{2,10},{3,11},{4,12},{5,13},{6,14},{7,15},{8,0},{9,1},... | collective-permute-start | bytes 835592 | tf_op jit(solution)/shard_map/ppermute | solution.py:328
  6.8 15.5 %collective-permute-start.5 = (bf16[544,256]{1,0:T(8,128)(2,1)}, bf16[544,256]{1,0:T(8,128)(2,1)S(1)}, u32[]{:S(2)}, u32[]{:S(2)}) collective-permute-start(bf16[544,256]{1,0:T(8,128)(2,1)} %get-tuple-element.24.refs_1_), channel_id=1, source_target_pairs={{0,2},{1,3},{2,0},{3,1},{4,6},{5,7},{6,4},{7,5},{8,10},{9,11},{10,... | collective-permute-start | bytes 835592 | tf_op jit(solution)/shard_map/ppermute | solution.py:328
  8.2 13.4 %collective-permute-start.3 = (bf16[544,256]{1,0:T(8,128)(2,1)}, bf16[544,256]{1,0:T(8,128)(2,1)S(1)}, u32[]{:S(2)}, u32[]{:S(2)}) collective-permute-start(bf16[544,256]{1,0:T(8,128)(2,1)} %get-tuple-element.24.refs_1_), channel_id=1, source_target_pairs={{0,4},{1,5},{2,6},{3,7},{4,0},{5,1},{6,2},{7,3},{8,12},{9,13},{10,... | collective-permute-start | bytes 835592 | tf_op jit(solution)/shard_map/ppermute | solution.py:328
  10.6 1.0 %copy-start = (bf16[544,256]{1,0:T(8,128)(2,1)S(1)}, bf16[544,256]{1,0:T(8,128)(2,1)}, u32[]{:S(2)}) copy-start(bf16[544,256]{1,0:T(8,128)(2,1)} %get-tuple-element.23.refs_0_) | copy-start | bytes 835588
  11.5 1.0 %copy-start.1 = (bf16[544,256]{1,0:T(8,128)(2,1)S(1)}, bf16[544,256]{1,0:T(8,128)(2,1)}, u32[]{:S(2)}) copy-start(bf16[544,256]{1,0:T(8,128)(2,1)} %get-tuple-element.24.refs_1_) | copy-start | bytes 835588
  20.3 3.9 %collective-permute-start.2 = (bf16[544,256]{1,0:T(8,128)(2,1)S(1)}, bf16[544,256]{1,0:T(8,128)(2,1)S(1)}, u32[]{:S(2)}, u32[]{:S(2)}) collective-permute-start(bf16[544,256]{1,0:T(8,128)(2,1)S(1)} %collective-permute-done.1.refs_0_), channel_id=1, source_target_pairs={{0,1},{1,0},{2,3},{3,2},{4,5},{5,4},{6,7},{7,6},{8,9},{9,8},{10,11... | collective-permute-start | bytes 835592 | tf_op jit(solution)/shard_map/ppermute | solution.py:328
  21.7 7.7 %collective-permute-start.4 = (bf16[544,256]{1,0:T(8,128)(2,1)S(1)}, bf16[544,256]{1,0:T(8,128)(2,1)S(1)}, u32[]{:S(2)}, u32[]{:S(2)}) collective-permute-start(bf16[544,256]{1,0:T(8,128)(2,1)S(1)} %collective-permute-done.3.refs_1_), channel_id=1, source_target_pairs={{0,2},{1,3},{2,0},{3,1},{4,6},{5,7},{6,4},{7,5},{8,10},{9,11},{10,... | collective-permute-start | bytes 835592 | tf_op jit(solution)/shard_map/ppermute | solution.py:328
  29.4 0.9 %copy-start.2 = (f32[8,256]{1,0:T(8,128)S(1)}, f32[8,256]{1,0:T(8,128)}, u32[]{:S(2)}) copy-start(f32[8,256]{1,0:T(8,128)} %far_ref.6) | copy-start | bytes 24580
  30.3 14.9 %copy-start.3 = (f32[8,256]{1,0:T(8,128)S(1)}, f32[8,256]{1,0:T(8,128)}, u32[]{:S(2)}) copy-start(f32[8,256]{1,0:T(8,128)} %far_ref.7) | copy-start | bytes 24580
  49.1 4.2 %collective-permute-start.6 = (f32[32,256]{1,0:T(8,128)S(1)}, f32[32,256]{1,0:T(8,128)S(1)}, u32[]{:S(2)}, u32[]{:S(2)}) collective-permute-start(f32[32,256]{1,0:T(8,128)S(1)} %get-tuple-element.41), channel_id=1, source_target_pairs={{0,2},{1,3},{2,0},{3,1},{4,6},{5,7},{6,4},{7,5},{8,10},{9,11},{10,... | collective-permute-start | bytes 98312 | tf_op jit(solution)/shard_map/ppermute | solution.py:328
  53.2 3.9 %collective-permute-start.7 = (f32[32,256]{1,0:T(8,128)S(1)}, f32[32,256]{1,0:T(8,128)S(1)}, u32[]{:S(2)}, u32[]{:S(2)}) collective-permute-start(f32[32,256]{1,0:T(8,128)S(1)} %add.26.refs_0_), channel_id=1, source_target_pairs={{0,4},{1,5},{2,6},{3,7},{4,0},{5,1},{6,2},{7,3},{8,12},{9,13},{10,... | collective-permute-start | bytes 98312 | tf_op jit(solution)/shard_map/ppermute | solution.py:328

commit v3 on v2

--- a/solution.py
+++ b/solution.py
@@ -20,9 +20,11 @@
 LOG_LARGEST = 88.4
 
 NOTHING = -1e30
+ALL, EARLY, LATE = range(3)
 
 DEPTH = 128
 GROUP = 64
+PART = 16
 EXTRA = 32
 VMEM = 12 * 1024 * 1024
 SMALL = 1024 * 1024
@@ -81,21 +83,23 @@
     )(*flat, *few)
 
 
-def prepare(blocks, clusters, count, state):
-    rows, size = blocks[0][0].shape
-    tall = rows - EXTRA
-    dims = tall // clusters
+def prepare(blocks, clusters, dims, counts, state, after=()):
+    size = blocks[0][0].shape[1]
+    tall = clusters * dims
     places = [place for _, place in blocks]
+    used = len(blocks)
+    told = [place - counts[0] for place in places if place >= counts[0]]
 
     def body(*refs):
-        points_refs = refs[:len(blocks)]
-        lhs_ref, rhs_ref, half_ref, extra_ref = refs[-4:]
+        points_refs = refs[:used]
+        lhs_ref, rhs_ref, half_ref = refs[-4:-1] if told else refs[-3:]
         row = lax.broadcasted_iota(jnp.int32, (DEPTH - dims, size), 0)
         ones = jnp.where(row < 3, 1.0, 0.0).astype(jnp.float32)
 
-        def write(points_ref):
-            extra = points_ref[tall:, :].astype(jnp.float32)
-            extra_ref[0] = extra[:clusters] + extra[clusters:2 * clusters] + extra[2 * clusters:3 * clusters]
+        def write(points_ref, place):
+            if place >= counts[0]:
+                extra = points_ref[tall:, :].astype(jnp.float32)
+                refs[-1][0] = extra[:clusters] + extra[clusters:2 * clusters] + extra[2 * clusters:3 * clusters]
 
             def one(c, carry):
                 raw = points_ref[pl.ds(pl.multiple_of(c * dims, dims), dims), :]
@@ -112,7 +116,7 @@
             lax.fori_loop(0, clusters, one, 0, unroll=2)
 
         for i, points_ref in enumerate(points_refs):
-            pl.when(pl.program_id(0) == i)(functools.partial(write, points_ref))
+            pl.when(pl.program_id(0) == i)(functools.partial(write, points_ref, places[i]))
 
     def place_of(i):
         chosen = places[0]
@@ -120,67 +124,101 @@
             chosen = jnp.where(i > j, place, chosen)
         return chosen
 
-    shapes = (
+    count = sum(counts)
+    shapes = [
         jax.ShapeDtypeStruct((count, clusters, size, DEPTH), jnp.bfloat16),
         jax.ShapeDtypeStruct((count, clusters, DEPTH, size), jnp.bfloat16),
         jax.ShapeDtypeStruct((count, clusters, size), jnp.float32),
-        jax.ShapeDtypeStruct((count, clusters, size), jnp.float32),
-    )
-    used = len(blocks)
-    extra_specs = [] if state is None else [pl.BlockSpec(memory_space=pl.ANY)] * 4
-    return pl.pallas_call(
+        jax.ShapeDtypeStruct((counts[1], clusters, size), jnp.float32),
+    ]
+    out_specs = [
+        pl.BlockSpec((1, clusters, size, DEPTH), lambda i: (place_of(i), 0, 0, 0)),
+        pl.BlockSpec((1, clusters, DEPTH, size), lambda i: (place_of(i), 0, 0, 0)),
+        pl.BlockSpec((1, clusters, size), lambda i: (place_of(i), 0, 0)),
+        pl.BlockSpec((1, clusters, size), lambda i: (told[-1], 0, 0)),
+    ]
+    parts = 4 if told else 3
+    held = [] if state is None else list(state[:parts])
+    out = pl.pallas_call(
         body,
         grid=(used,),
-        out_shape=shapes,
-        in_specs=[pl.BlockSpec((rows, size), lambda i: (0, 0))] * used + extra_specs,
-        out_specs=(
-            pl.BlockSpec((1, clusters, size, DEPTH), lambda i: (place_of(i), 0, 0, 0)),
-            pl.BlockSpec((1, clusters, DEPTH, size), lambda i: (place_of(i), 0, 0, 0)),
-            pl.BlockSpec((1, clusters, size), lambda i: (place_of(i), 0, 0)),
-            pl.BlockSpec((1, clusters, size), lambda i: (place_of(i), 0, 0)),
-        ),
-        input_output_aliases={} if state is None else {used + i: i for i in range(4)},
+        out_shape=shapes[:parts],
+        in_specs=[pl.BlockSpec(points.shape, lambda i: (0, 0)) for points, _ in blocks]
+        + [pl.BlockSpec(memory_space=pl.ANY)] * (len(held) + len(after)),
+        out_specs=out_specs[:parts],
+        input_output_aliases={used + i: i for i in range(len(held))},
         compiler_params=pltpu.CompilerParams(vmem_limit_bytes=VMEM),
         cost_estimate=pl.CostEstimate(
             flops=used * clusters * dims * size * 4, bytes_accessed=used * clusters * size * DEPTH * 8, transcendentals=0
         ),
         name="prepare",
-    )(*[points for points, _ in blocks], *(() if state is None else state))
-
-
-def list_pairs(entries):
-    rows, width = entries.shape
-
-    def body(entries_ref, out_ref):
-        def one(r, filled):
-            for k in range(width):
-                entry = entries_ref[r, k]
-                out_ref[filled] = entry
-                filled = filled + jnp.where(entry >= 0, 1, 0).astype(jnp.int32)
-            return filled
-
-        filled = lax.fori_loop(0, rows - 1, one, jnp.int32(1))
-        out_ref[0] = filled - 1
-        last = entries_ref[rows - 1, 0]
+    )(*[points for points, _ in blocks], *held, *after)
+    return list(out) + ([] if told else [state[3]])
+
+
+def list_pairs(home, cand, target_bits, tgt_count, early, late):
+    sources, per_cluster = cand.shape
+    targets = tgt_count << len(target_bits)
+    mask = sum(1 << b for b in target_bits)
+    nobody = sources * (2 * targets) + targets
+
+    def body(home_ref, cand_ref, out_ref, table_ref, entries_ref, sem):
+        code = cand_ref[...]
+        apart = lax.div(code, tgt_count) ^ home_ref[2]
+        block = sum(((apart >> bit) & 1) << place for place, bit in enumerate(target_bits))
+        inside = (apart & ~mask) == 0
+        row = lax.broadcasted_iota(jnp.int32, code.shape, 0)
+        code = (row ^ (home_ref[0] * tgt_count)) * (2 * targets) + block * tgt_count + lax.rem(code, tgt_count)
+        lane = lax.broadcasted_iota(jnp.int32, table_ref.shape, 1)
+        table = jnp.full(table_ref.shape, -1, jnp.int32)
+        for at in early + late:
+            column = jnp.max(jnp.where(inside & (block == at), code, -1), axis=1, keepdims=True)
+            table = jnp.where(lane == at, column, table)
+        table_ref[...] = table
+        copy = pltpu.make_async_copy(table_ref, entries_ref, sem)
+        copy.start()
+        copy.wait()
+
+        def fill(columns, filled):
+            def one(r, filled):
+                for u in range(8):
+                    for k in columns:
+                        entry = entries_ref[r * 8 + u, k]
+                        out_ref[filled] = entry
+                        filled = filled + jnp.where(entry >= 0, 1, 0).astype(jnp.int32)
+                return filled
+
+            return lax.fori_loop(0, sources // 8, one, filled)
+
+        filled = fill(early, jnp.int32(2))
+        for extra in range(PART):
+            out_ref[filled + extra] = nobody
+        begin = lax.div(filled - 2 + (PART - 1), PART) * PART
+        filled = fill(late, begin + 2)
         for extra in range(GROUP):
-            out_ref[filled + extra] = last
+            out_ref[filled + extra] = nobody
+        out_ref[0] = begin
+        out_ref[1] = filled - 2
 
     return pl.pallas_call(
         body,
-        out_shape=jax.ShapeDtypeStruct((rows * width + 1 + GROUP,), jnp.int32),
-        in_specs=[pl.BlockSpec(memory_space=pltpu.SMEM)],
+        out_shape=jax.ShapeDtypeStruct((sources * per_cluster + 2 + PART + GROUP,), jnp.int32),
+        in_specs=[pl.BlockSpec(memory_space=pltpu.SMEM), pl.BlockSpec(memory_space=pltpu.VMEM)],
         out_specs=pl.BlockSpec(memory_space=pltpu.SMEM),
+        scratch_shapes=[
+            pltpu.VMEM((sources, 128), jnp.int32), pltpu.SMEM((sources, 128), jnp.int32), pltpu.SemaphoreType.DMA,
+        ],
         compiler_params=pltpu.CompilerParams(vmem_limit_bytes=SMALL),
         cost_estimate=pl.CostEstimate(flops=0, bytes_accessed=4 << 20, transcendentals=0),
         name="list_pairs",
-    )(entries)
+    )(home, cand)
 
 
 def padded_rows(rows):
     return -(-3 * rows // 128) * 128
 
 
-def sum_pairs(pairs_ref, lhs_ref, rhs_ref, sources, values, extra_ref, acc_ref, by_source, adjust=lambda term: term):
+def sum_pairs(pairs_ref, lhs_ref, rhs_ref, sources, values, extra_ref, acc_ref, by_source, part=ALL, adjust=lambda term: term):
     size = lhs_ref.shape[1]
     targets = lhs_ref.shape[0] - sources
     count, others = (targets, sources) if by_source else (sources, targets)
@@ -194,9 +232,11 @@
     row = lax.broadcasted_iota(jnp.int32, (wide, size), 0)
     row = jnp.where(row < 3 * count, lax.rem(row, count), count)
 
+    length = GROUP if part == ALL else PART
+
     def step(g, carry):
-        for u in range(GROUP):
-            code = pairs_ref[g * GROUP + u + 1]
+        for u in range(length):
+            code = pairs_ref[g * length + u + 2]
             s, t = lax.div(code, 2 * targets), lax.rem(code, 2 * targets)
             m, place = (t, s) if by_source else (s, t)
             m, n = jnp.minimum(m, count - 1), jnp.minimum(place, others - 1)
@@ -209,7 +249,9 @@
             acc_ref[place] += jnp.sum(jnp.exp(adjust(term)).reshape(size // 8, 8, size), axis=0)
         return carry
 
-    lax.fori_loop(0, lax.div(pairs_ref[0] + (GROUP - 1), GROUP), step, 0)
+    first = lax.div(pairs_ref[0], length) if part == LATE else 0
+    stop = lax.div(pairs_ref[0 if part == EARLY else 1] + (length - 1), length)
+    lax.fori_loop(first, stop, step, 0)
     return jnp.sum(acc_ref[:others], axis=1)
 
 
@@ -231,40 +273,52 @@
     return jnp.concatenate(blocks, axis=0)
 
 
-def row_kernel(terms, sources, first, pairs_ref, home_ref, lhs_ref, rhs_ref, half_ref, far_ref, *refs):
-    pot_refs, (out_ref, extra_ref, acc_ref) = refs[:-3], refs[-3:]
-    if first:
-        pot = pot_refs[0][sources:, :]
-    else:
-        pot = -KEEP_TAU * SCALE_EPS * (jnp.log(load_sums(pot_refs, home_ref[1], far_ref.shape[0])) - column_offset(terms))
-    values = INV_EPS * (pot - half_ref[sources:, :]) - LOW_OFFSET
-    run = functools.partial(sum_pairs, pairs_ref, lhs_ref, rhs_ref, sources, values, extra_ref, acc_ref, True)
+def first_row_kernel(sources, known, pairs_ref, home_ref, lhs_ref, rhs_ref, half_ref, far_ref, pot_ref, *refs):
+    before_ref, (out_ref, extra_ref, acc_ref) = refs[:-3], refs[-3:]
+    pot, half = pot_ref[...], half_ref[sources:, :]
+    if known is not None:
+        row = lax.broadcasted_iota(jnp.int32, pot.shape, 0)
+        is_known = functools.reduce(jnp.logical_or, [(row >= a) & (row < b) for a, b in known])
+        pot, half = jnp.where(is_known, pot, 0.0), jnp.where(is_known, half, 0.0)
+    values = INV_EPS * (pot - half) - LOW_OFFSET
+    run = functools.partial(
+        sum_pairs, pairs_ref, lhs_ref, rhs_ref, sources, values, extra_ref, acc_ref, True, LATE if before_ref else EARLY
+    )
     far = jnp.exp(far_ref[...] - LOW_OFFSET)
-    if not first:
-        store_sums(run(), home_ref[0], out_ref, far)
-        return
     own = far_ref.shape[0]
 
-    def store_logs(low, high=None):
+    def store(low, high):
+        if not before_ref:
+            out_ref[0] = low
+            out_ref[1] = jnp.zeros_like(low) if high is None else high
+            return
+        low = low + before_ref[0][0]
+        high = before_ref[0][1] if high is None else high + before_ref[0][1]
         low = jnp.concatenate([low[:own] + far, low[own:]], axis=0)
-        logs = log_or_nothing(low) + LOW_OFFSET
-        if high is not None:
-            high = log_or_nothing(high) + HIGH_OFFSET
-            top = jnp.maximum(logs, high)
-            logs = top + jnp.log(jnp.exp(logs - top) + jnp.exp(high - top))
+        low, high = log_or_nothing(low) + LOW_OFFSET, log_or_nothing(high) + HIGH_OFFSET
+        top = jnp.maximum(low, high)
+        logs = top + jnp.log(jnp.exp(low - top) + jnp.exp(high - top))
         store_sums(logs, home_ref[0], out_ref, jnp.zeros_like(far))
 
     narrow = jnp.max(pot) <= LOW_TOP * SCALE_EPS
 
     @pl.when(narrow)
     def _():
-        store_logs(run())
+        store(run(), None)
 
     @pl.when(jnp.logical_not(narrow))
     def _():
         edge = LOW_TOP - LOW_OFFSET
         low = run(lambda term: jnp.where(term <= edge, term, NOTHING))
-        store_logs(low, run(lambda term: jnp.where(term > edge, term - (HIGH_OFFSET - LOW_OFFSET), NOTHING)))
+        store(low, run(lambda term: jnp.where(term > edge, term - (HIGH_OFFSET - LOW_OFFSET), NOTHING)))
+
+
+def row_kernel(terms, sources, pairs_ref, home_ref, lhs_ref, rhs_ref, half_ref, far_ref, sums_ref, come_ref, out_ref, extra_ref, acc_ref):
+    sums = load_sums([sums_ref, come_ref], home_ref[1], far_ref.shape[0])
+    pot = -KEEP_TAU * SCALE_EPS * (jnp.log(sums) - column_offset(terms))
+    values = INV_EPS * (pot - half_ref[sources:, :]) - LOW_OFFSET
+    total = sum_pairs(pairs_ref, lhs_ref, rhs_ref, sources, values, extra_ref, acc_ref, True)
+    store_sums(total, home_ref[0], out_ref, jnp.exp(far_ref[...] - LOW_OFFSET))
 
 
 def log_or_nothing(value):
@@ -275,8 +329,9 @@
     return LOG_LARGEST - COLUMN_TOP - math.log(terms)
 
 
-def column_kernel(terms, sources, first, pairs_ref, home_ref, lhs_ref, rhs_ref, half_ref, far_ref, sums_ref, out_ref, pot_ref, extra_ref, acc_ref):
-    parts, own = range(sums_ref.shape[0]), pot_ref.shape[0]
+def column_kernel(terms, sources, first, pairs_ref, home_ref, lhs_ref, rhs_ref, half_ref, far_ref, sums_ref, out_ref, *refs):
+    pot_refs, (extra_ref, acc_ref) = refs[:-2], refs[-2:]
+    parts, own = range(sums_ref.shape[0]), far_ref.shape[0]
     if first:
         logs = [load_sums([sums_ref.at[i]], home_ref[0], own) for i in parts]
         top = functools.reduce(jnp.maximum, logs)
@@ -287,7 +342,8 @@
     values = INV_EPS * (pot - half_ref[:sources, :]) + column_offset(terms)
     total = sum_pairs(pairs_ref, lhs_ref, rhs_ref, sources, values, extra_ref, acc_ref, False)
     store_sums(total, home_ref[1], out_ref, jnp.exp(far_ref[...] + column_offset(terms)))
-    pot_ref[...] = pot[:own]
+    for pot_ref in pot_refs:
+        pot_ref[...] = pot[:own]
 
 
 def run_pass(kernel, out_shapes, pairs, home, state, width, others, tiles, *rest):
@@ -340,54 +396,87 @@
     def place_of(device, which):
         return sum(((device >> bit) & 1) << place for place, bit in enumerate(which))
 
-    tall = src_count * src_points.shape[1]
     sources, targets = nr * src_count, nc * tgt_count
+    dims = src_points.shape[1]
     me = lax.axis_index("src").astype(jnp.int32)
-    home = jnp.stack([place_of(me, source_bits), place_of(me, target_bits)])
-    src_message, tgt_message = pack((src_points, tgt_points), (cand_owner, cand_local), (g_init,))
-    src_blocks = doubled(src_message, source_bits)
-    tgt_blocks = doubled(tgt_message, target_bits)
-    state = None
-    order = lambda blocks: sorted(range(len(blocks)), key=lambda at: (at.bit_count(), at))
-    src_order, tgt_order = order(src_blocks), order(tgt_blocks)
-    for i in range(max(nr, nc)):
-        blocks = [(src_blocks[at], at) for at in src_order[i:i + 1]] + [(tgt_blocks[at], nr + at) for at in tgt_order[i:i + 1]]
-        state = prepare(blocks, src_count, nr + nc, state)
-    *state, extra = [a.reshape((-1,) + a.shape[2:]) for a in state]
-
-    owner = jnp.concatenate([b[tall:tall + src_count, :per_cluster] for b in src_blocks], axis=0).astype(jnp.int32)
-    local = jnp.concatenate([b[tall + src_count:tall + 2 * src_count, :per_cluster] for b in src_blocks], axis=0).astype(jnp.int32)
-    inside = ((owner ^ me) & ~sum(1 << b for b in target_bits)) == 0
-    row = lax.broadcasted_iota(jnp.int32, (sources, per_cluster), 0)
-    entries = jnp.where(inside, row * (2 * targets) + place_of(owner ^ me, target_bits) * tgt_count + local, -1)
-    nobody = jnp.full((1, per_cluster), sources * (2 * targets) + targets, jnp.int32)
-    pairs = list_pairs(jnp.concatenate([entries, nobody], axis=0))
-    pots = [extra]
+    home = jnp.stack([place_of(me, source_bits), place_of(me, target_bits), me])
+    src_points = src_points.reshape(-1, size)
+    tgt_message, = pack((tgt_points,), (g_init,))
+    late = [at for at in range(2, nc) if at & 1]
+    early = [at for at in range(nc) if at not in late]
+    ready = functools.partial(prepare, clusters=src_count, dims=dims, counts=(nr, nc))
+
+    src_far = doubled(src_points, source_bits[1:])
+    src_side = across(src_points, source_bits[0])
+    tgt_far = doubled(tgt_message, target_bits[1:])
+    held, home = lax.optimization_barrier((src_points, home))
+    state = ready([(held, 0), (tgt_message, nr)], state=None)
+    code = cand_owner * tgt_count + cand_local
+    code, state, tgt_held = lax.optimization_barrier((code, state, tgt_message))
+    tgt_side = across(tgt_held, target_bits[0])
+    cand = lax.all_gather(code, "src", axis_index_groups=groups(source_bits)).reshape(sources, per_cluster)
+    pairs = list_pairs(home, cand, target_bits, tgt_count, early, late)
+    src_far[1:], cand = lax.optimization_barrier((src_far[1:], cand))
+
+    def interleaved(far, side, bit):
+        return [b for pair in zip(far, [side] + [across(block, bit) for block in far[1:]]) for b in pair]
+
+    src_blocks = interleaved(src_far, src_side, source_bits[0])
+    tgt_blocks = interleaved(tgt_far, tgt_side, target_bits[0])
+
+    def pairs_of(sources_at, targets_at):
+        return [(src_blocks[at], at) for at in sources_at] + [(tgt_blocks[at], nr + at) for at in targets_at]
+
+    by_hops = lambda places: sorted(places, key=lambda at: (at.bit_count(), at))[1:]
+    src_order, tgt_order = by_hops(range(nr)), by_hops(early)
+    for i in range(max(len(src_order), len(tgt_order))):
+        state = ready(pairs_of(src_order[i:i + 1], tgt_order[i:i + 1]), state=state)
+
+    def flat(state):
+        return [a.reshape((-1,) + a.shape[2:]) for a in state]
 
     f32 = jnp.float32
     tiles = src_count * per_cluster
     for iteration in range(ITERS):
         first = iteration == 0
-        sums = run_pass(
-            functools.partial(row_kernel, terms, sources, first),
-            jax.ShapeDtypeStruct((sources, size), f32),
-            pairs, home, state, targets, sources, tiles, far_src, *pots,
-        )
+        if first:
+            known = [(at * tgt_count, (at + 1) * tgt_count) for at in early]
+            *operands, pot = flat(state)
+            before = run_pass(
+                functools.partial(first_row_kernel, sources, known),
+                jax.ShapeDtypeStruct((2, sources, size), f32),
+                pairs, home, operands, targets, sources, tiles, far_src, pot,
+            )
+            for at in late:
+                state = ready(pairs_of([], [at]), state=state, after=(before,))
+            *state, pot = flat(state)
+            sums = run_pass(
+                functools.partial(first_row_kernel, sources, None),
+                jax.ShapeDtypeStruct((sources, size), f32),
+                pairs, home, state, targets, sources, tiles, far_src, pot, before,
+            )
+        else:
+            sums = run_pass(
+                functools.partial(row_kernel, terms, sources),
+                jax.ShapeDtypeStruct((sources, size), f32),
+                pairs, home, state, targets, sources, tiles, far_src, *sums,
+            )
         sums = lax.all_gather(sums, "src", axis_index_groups=groups(source_bits))
-        column, src_pot = run_pass(
+        shapes = [jax.ShapeDtypeStruct((targets, size), f32), jax.ShapeDtypeStruct((src_count, size), f32)]
+        column, *src_pot = run_pass(
             functools.partial(column_kernel, terms, sources, first),
-            (jax.ShapeDtypeStruct((targets, size), f32), jax.ShapeDtypeStruct((src_count, size), f32)),
+            shapes if iteration + 1 == ITERS else shapes[:1],
             pairs, home, state, sources, targets, tiles, far_tgt, sums,
         )
         if iteration + 1 < ITERS:
             for bit in target_bits[:-1]:
                 column = column + across(column, bit)
-            pots = [column, across(column, target_bits[-1])]
+            sums = [column, across(column, target_bits[-1])]
     column = lax.all_to_all(
         column.reshape(nc, tgt_count, size), "src", 0, 0, tiled=True, axis_index_groups=groups(target_bits)
     )
     tgt_pot = -KEEP_TAU * SCALE_EPS * (jnp.log(jnp.sum(column, axis=0)) - column_offset(terms))
-    return (src_pot, tgt_pot)
+    return (src_pot[0], tgt_pot)
 
 
 def solution(mesh):

time: 79.4 us -> 76.7 us (0.966)
  waiting for transfers between devices: 15.9 us -> 6.61 us
  blocking collectives: 20.8 us -> 26.5 us
  Pallas kernels: 27 us -> 29.6 us
  local copies, waits for them, and re-layouts: 2.62 us -> 1.21 us
  starting transfers between devices: 11.2 us -> 10.2 us
    ppermute x8, waiting for transfers between devices: 15.9 us -> 6.61 us  [across(): return lax.ppermute(array, 'src', [(i, i ^ apart) for i in range(shards)])]
    all_gather x0 -> x1, blocking collectives: none -> 6.07 us  [per_device(): lax.all_gather(code, 'src', axis_index_groups=groups(source_bits))]
    pallas_call x4 -> x5, Pallas kernels: 19.2 us -> 20.9 us  [run_pass(): pl.pallas_call(kernel, out_shape=out_shapes, in_specs=[pl.BlockSpec(memor...]
    pallas_call x5 -> x6, Pallas kernels: 5.83 us -> 7.08 us  [the longest x5 4.58 us: prepare(): pl.pallas_call(body, grid=(used,), out_shape=shapes[:parts], in_specs=[pl...]
    ppermute x8, starting transfers between devices: 11.2 us -> 10.2 us  [across(): return lax.ppermute(array, 'src', [(i, i ^ apart) for i in range(shards)])]
    unnamed x8 -> x6, local copies, waits for them, and re-layouts: 1.92 us -> 1.21 us
  transfers between devices with their start and end apart: 8 -> 8, of which waited for: 5 -> 2; matrix products, arithmetic and copies ran while one was open for 1% -> 1% of each run, Pallas kernels for 6% -> 21%
where the time goes in v3:
time: 76.7 us; the launch traced here: 76.3 us
  Pallas kernels  29.6 us (39%)
  blocking collectives  26.5 us (35%)
  starting transfers between devices  10.2 us (13%)
  waiting for transfers between devices  6.61 us (9%)
  other arithmetic  1.41 us (2%)
  local copies, waits for them, and re-layouts  1.21 us (2%)
    pallas_call x5, Pallas kernels, run_pass(): pl.pallas_call(kernel, out_shape=out_shapes, in_specs=[pl.BlockSpec(memor...  20.9 us
    all_gather x2, blocking collectives, per_device(): sums = lax.all_gather(sums, 'src', axis_index_groups=groups(source_bits))  13.3 us
    ppermute x8, starting transfers between devices, across(): return lax.ppermute(array, 'src', [(i, i ^ apart) for i in range(shards)])  10.2 us
    all_to_all x1, blocking collectives, per_device(): lax.all_to_all(column.reshape(nc, tgt_count, size), 'src', 0, 0, tiled=Tr...  7.1 us
    ppermute x8, waiting for transfers between devices, across(): return lax.ppermute(array, 'src', [(i, i ^ apart) for i in range(shards)])  6.61 us
    all_gather x1, blocking collectives, per_device(): lax.all_gather(code, 'src', axis_index_groups=groups(source_bits))  6.07 us
    pallas_call x5, Pallas kernels, prepare(): pl.pallas_call(body, grid=(used,), out_shape=shapes[:parts], in_specs=[pl...  4.58 us
    pallas_call x1, Pallas kernels, list_pairs(): pl.pallas_call(body, out_shape=jax.ShapeDtypeStruct((sources * per_cluste...  2.5 us
  transfers between devices with their start and end apart: 8, of which 2 were waited for; matrix products, arithmetic and copies ran while one was open for 1% of the time, Pallas kernels for 21%

profile of v3, /device:TPU:0, one launch (start us, length us, event | category | flops | bytes accessed | tf_op | source)
XLA Modules:
  0.0 76.3 jit_solution(9742589231241293258)
XLA Ops:
  0.6 4.1 %collective-permute-start.2 = (bf16[512,256]{1,0:T(8,128)(2,1)}, bf16[512,256]{1,0:T(8,128)(2,1)S(1)}, u32[]{:S(2)}, u32[]{:S(2)}) collective-permute-start(bf16[512,256]{1,0:T(8,128)(2,1)} %bitcast.refs_0_), channel_id=1, source_target_pairs={{0,8},{1,9},{2,10},{3,11},{4,12},{5,13},{6,14},{7,15},{8,0},{9,1},... | collective-permute-start | bytes 786440 | tf_op jit(solution)/shard_map/ppermute | solution.py:384
  4.7 1.7 %pack.1.refs_1_ = bf16[544,256]{1,0:T(8,128)(2,1)} custom-call(bf16[512,256]{1,0:T(8,128)(2,1)} %bitcast.36, f32[8,256]{1,0:T(8,128)} %refs_1_.1), custom_call_target="tpu_custom_call" | custom-call | tf_op jit(solution)/shard_map/pack/pallas_call | solution.py:75
  6.4 1.6 %collective-permute-start = (bf16[544,256]{1,0:T(8,128)(2,1)}, bf16[544,256]{1,0:T(8,128)(2,1)S(1)}, u32[]{:S(2)}, u32[]{:S(2)}) collective-permute-start(bf16[544,256]{1,0:T(8,128)(2,1)} %pack.1.refs_1_), channel_id=1, source_target_pairs={{0,4},{1,5},{2,6},{3,7},{4,0},{5,1},{6,2},{7,3},{8,12},{9,13},{10,... | collective-permute-start | bytes 835592 | tf_op jit(solution)/shard_map/ppermute | solution.py:384
  8.1 0.1 pad_add_fusion.home_ref
  8.1 1.0 %copy-done = bf16[544,256]{1,0:T(8,128)(2,1)S(1)} copy-done((bf16[544,256]{1,0:T(8,128)(2,1)S(1)}, bf16[544,256]{1,0:T(8,128)(2,1)}, u32[]{:S(2)}) %copy-start) | copy-done | bytes 278552
  9.1 1.9 %prepare.5 = (bf16[8,8,256,128]{3,2,1,0:T(8,128)(2,1)S(1)}, bf16[8,8,128,256]{3,2,1,0:T(8,128)(2,1)S(1)}, f32[8,8,256]{2,1,0:T(8,128)S(1)}, f32[4,8,256]{2,1,0:T(8,128)S(1)}) custom-call(bf16[512,256]{1,0:T(8,128)(2,1)} %bitcast.refs_0_, bf16[544,256]{1,0:T(8,128)(2,1)S(1)} %copy-done), custom_call_target="tpu_custom_call" | custom-call | flops 1048576 | bytes 4194304 | tf_op jit(solution)/shard_map/prepare/pallas_call | solution.py:142
  11.0 0.7 multiply_add_fusion
  11.7 1.5 %collective-permute-start.5 = (bf16[544,256]{1,0:T(8,128)(2,1)S(1)}, bf16[544,256]{1,0:T(8,128)(2,1)S(1)}, u32[]{:S(2)}, u32[]{:S(2)}) collective-permute-start(bf16[544,256]{1,0:T(8,128)(2,1)S(1)} %copy-done), channel_id=1, source_target_pairs={{0,2},{1,3},{2,0},{3,1},{4,6},{5,7},{6,4},{7,5},{8,10},{9,11},{10,... | collective-permute-start | bytes 835592 | tf_op jit(solution)/shard_map/ppermute | solution.py:384
  13.2 6.1 %all-gather.cand_ref = s32[32,8]{1,0:T(8,128)S(1)} all-gather(s32[8,8]{1,0:T(8,128)S(1)} %multiply_add_fusion), channel_id=2, replica_groups={{0,1,8,9},{2,3,10,11},{4,5,12,13},{6,7,14,15},{16,17,24,25},{18,19,26,2..., dimensions={0}, use_global_device_ids=true | all-gather | bytes 1280 | tf_op jit(solution)/shard_map/all_gather | solution.py:417
  19.2 0.3 collective-permute-start.3
  19.6 1.3 %collective-permute-start.1 = (bf16[544,256]{1,0:T(8,128)(2,1)S(1)}, bf16[544,256]{1,0:T(8,128)(2,1)S(1)}, u32[]{:S(2)}, u32[]{:S(2)}) collective-permute-start(bf16[544,256]{1,0:T(8,128)(2,1)S(1)} %collective-permute-done.refs_1_), channel_id=1, source_target_pairs={{0,2},{1,3},{2,0},{3,1},{4,6},{5,7},{6,4},{7,5},{8,10},{9,11},{10,... | collective-permute-start | bytes 835592 | tf_op jit(solution)/shard_map/ppermute | solution.py:384
  20.9 2.5 %list_pairs.1.pairs_ref = s32[338]{0:T(512)S(1)} custom-call(s32[3]{0:T(128)S(1)} %pad_add_fusion.home_ref, s32[32,8]{1,0:T(8,128)S(1)} %all-gather.cand_ref), custom_call_target="tpu_custom_call" | custom-call | bytes 4194304 | tf_op jit(solution)/shard_map/list_pairs/pallas_call | solution.py:203
  23.4 0.9 %prepare.6 = (bf16[8,8,256,128]{3,2,1,0:T(8,128)(2,1)S(1)}, bf16[8,8,128,256]{3,2,1,0:T(8,128)(2,1)S(1)}, f32[8,8,256]{2,1,0:T(8,128)S(1)}, f32[4,8,256]{2,1,0:T(8,128)S(1)}) custom-call(bf16[512,256]{1,0:T(8,128)(2,1)S(1)} %collective-permute-done.4.refs_0_, ...), custom_call_target="tpu_custom_call", output_to_operand_aliasing={{0}: (2, {}), {1}: (3, {}), {2}: (4, {}), {3}: (5, {})} | custom-call | flops 1048576 | bytes 4194304 | tf_op jit(solution)/shard_map/prepare/pallas_call | solution.py:142
  24.4 0.9 %prepare.7 = (bf16[8,8,256,128]{3,2,1,0:T(8,128)(2,1)S(1)}, bf16[8,8,128,256]{3,2,1,0:T(8,128)(2,1)S(1)}, f32[8,8,256]{2,1,0:T(8,128)S(1)}, f32[4,8,256]{2,1,0:T(8,128)S(1)}) custom-call(bf16[512,256]{1,0:T(8,128)(2,1)S(1)} %collective-permute-done.2.refs_0_, ...), custom_call_target="tpu_custom_call", output_to_operand_aliasing={{0}: (2, {}), {1}: (3, {}), {2}: (4, {}), {3}: (5, {})} | custom-call | flops 1048576 | bytes 4194304 | tf_op jit(solution)/shard_map/prepare/pallas_call | solution.py:142
  25.3 0.0 copy-start.1
  25.3 0.4 prepare.8
  25.8 0.2 copy-done.1
  26.0 7.6 %tiles.5.refs_5_.refs_0_ = f32[2,32,256]{2,1,0:T(8,128)S(1)} custom-call(s32[338]{0:T(512)S(1)} %list_pairs.1.pairs_ref, s32[3]{0:T(128)S(1)} %pad_add_fusion.home_ref, bf16[64,256,128]{2,1,0:T(8,128)(2,1)S(1)} %bitcast.16, bf16[64,128,256]{2,1,0:T(8,128)(2,1)S(1)} %bitcast.21, f32[64,256]{1,0:T(8,128)S(1)} %bitcast.26, f32[8,256]{1,0:T(8,128)S(1)} %copy-done.1, ...), custom_call_target="tpu_custom_call" | custom-call | flops 1073741824 | bytes 8388608 | tf_op jit(solution)/shard_map/tiles/pallas_call | solution.py:352
  33.6 0.4 prepare.9
  34.0 0.0 copy-start.2
  34.0 3.2 %tiles.6 = f32[32,256]{1,0:T(8,128)S(1)} custom-call(s32[338]{0:T(512)S(1)} %list_pairs.1.pairs_ref, s32[3]{0:T(128)S(1)} %pad_add_fusion.home_ref, bf16[64,256,128]{2,1,0:T(8,128)(2,1)S(1)} %bitcast.17, bf16[64,128,256]{2,1,0:T(8,128)(2,1)S(1)} %bitcast.22, f32[64,256]{1,0:T(8,128)S(1)} %bitcast.27, f32[8,256]{1,0:T(8,128)S(1)} %copy-done.1, ...), custom_call_target="tpu_custom_call" | custom-call | flops 1073741824 | bytes 8388608 | tf_op jit(solution)/shard_map/tiles/pallas_call | solution.py:352
  37.2 6.7 %all-gather.1 = f32[128,256]{1,0:T(8,128)S(1)} all-gather(f32[32,256]{1,0:T(8,128)S(1)} %tiles.6), channel_id=3, replica_groups={{0,1,8,9},{2,3,10,11},{4,5,12,13},{6,7,14,15},{16,17,24,25},{18,19,26,2..., dimensions={0}, use_global_device_ids=true | all-gather | bytes 163840 | tf_op jit(solution)/shard_map/all_gather | solution.py:464
  43.9 3.1 %tiles.7 = f32[32,256]{1,0:T(8,128)S(1)} custom-call(s32[338]{0:T(512)S(1)} %list_pairs.1.pairs_ref, s32[3]{0:T(128)S(1)} %pad_add_fusion.home_ref, bf16[64,256,128]{2,1,0:T(8,128)(2,1)S(1)} %bitcast.18, bf16[64,128,256]{2,1,0:T(8,128)(2,1)S(1)} %bitcast.23, f32[64,256]{1,0:T(8,128)S(1)} %bitcast.28, f32[8,256]{1,0:T(8,128)S(1)} %copy-done.2, ...), custom_call_target="tpu_custom_call" | custom-call | flops 1073741824 | bytes 8388608 | tf_op jit(solution)/shard_map/tiles/pallas_call | solution.py:352
  47.0 0.8 collective-permute-start.6
  47.8 3.2 %collective-permute-done.6 = f32[32,256]{1,0:T(8,128)S(1)} collective-permute-done((f32[32,256]{1,0:T(8,128)S(1)}, f32[32,256]{1,0:T(8,128)S(1)}, u32[]{:S(2)}, u32[]{:S(2)}) %collective-permute-start.6) | collective-permute-done | bytes 32800 | tf_op jit(solution)/shard_map/ppermute | solution.py:384
  51.0 0.5 collective-permute-start.7
  51.6 3.4 %collective-permute-done.7.come_ref = f32[32,256]{1,0:T(8,128)S(1)} collective-permute-done((f32[32,256]{1,0:T(8,128)S(1)}, f32[32,256]{1,0:T(8,128)S(1)}, u32[]{:S(2)}, u32[]{:S(2)}) %collective-permute-start.7) | collective-permute-done | bytes 32800 | tf_op jit(solution)/shard_map/ppermute | solution.py:384
  54.9 3.3 %tiles.8 = f32[32,256]{1,0:T(8,128)S(1)} custom-call(s32[338]{0:T(512)S(1)} %list_pairs.1.pairs_ref, s32[3]{0:T(128)S(1)} %pad_add_fusion.home_ref, bf16[64,256,128]{2,1,0:T(8,128)(2,1)S(1)} %bitcast.19, bf16[64,128,256]{2,1,0:T(8,128)(2,1)S(1)} %bitcast.24, f32[64,256]{1,0:T(8,128)S(1)} %bitcast.29, f32[8,256]{1,0:T(8,128)S(1)} %copy-done.1, ...), custom_call_target="tpu_custom_call" | custom-call | flops 1073741824 | bytes 8388608 | tf_op jit(solution)/shard_map/tiles/pallas_call | solution.py:352
  58.3 6.7 %all-gather.2 = f32[128,256]{1,0:T(8,128)S(1)} all-gather(f32[32,256]{1,0:T(8,128)S(1)} %tiles.8), channel_id=4, replica_groups={{0,1,8,9},{2,3,10,11},{4,5,12,13},{6,7,14,15},{16,17,24,25},{18,19,26,2..., dimensions={0}, use_global_device_ids=true | all-gather | bytes 163840 | tf_op jit(solution)/shard_map/all_gather | solution.py:464
  64.9 3.7 %tiles.9 = (f32[32,256]{1,0:T(8,128)S(1)}, f32[8,256]{1,0:T(8,128)}) custom-call(s32[338]{0:T(512)S(1)} %list_pairs.1.pairs_ref, s32[3]{0:T(128)S(1)} %pad_add_fusion.home_ref, bf16[64,256,128]{2,1,0:T(8,128)(2,1)S(1)} %bitcast.20, bf16[64,128,256]{2,1,0:T(8,128)(2,1)S(1)} %bitcast.25, f32[64,256]{1,0:T(8,128)S(1)} %bitcast.30, f32[8,256]{1,0:T(8,128)S(1)} %copy-done.2, ...), custom_call_target="tpu_custom_call" | custom-call | flops 1073741824 | bytes 8388608 | tf_op jit(solution)/shard_map/tiles/pallas_call | solution.py:352
  68.6 7.1 %all_to_all.5 = f32[4,8,256]{2,1,0:T(8,128)S(1)} all-to-all(f32[4,8,256]{2,1,0:T(8,128)S(1)} %bitcast.35), channel_id=1, replica_groups={{0,2,4,6},{1,3,5,7},{8,10,12,14},{9,11,13,15},{16,18,20,22},{17,19,21,2..., dimensions={0} | all-to-all | bytes 65536 | tf_op jit(solution)/shard_map/all_to_all | solution.py:475
  75.7 0.6 add_multiply_fusion
  (11 shorter events, 0.0 us)
Async XLA Ops:
  0.6 18.6 %collective-permute-start.2 = (bf16[512,256]{1,0:T(8,128)(2,1)}, bf16[512,256]{1,0:T(8,128)(2,1)S(1)}, u32[]{:S(2)}, u32[]{:S(2)}) collective-permute-start(bf16[512,256]{1,0:T(8,128)(2,1)} %bitcast.refs_0_), channel_id=1, source_target_pairs={{0,8},{1,9},{2,10},{3,11},{4,12},{5,13},{6,14},{7,15},{8,0},{9,1},... | collective-permute-start | bytes 786440 | tf_op jit(solution)/shard_map/ppermute | solution.py:384
  6.4 13.2 %collective-permute-start = (bf16[544,256]{1,0:T(8,128)(2,1)}, bf16[544,256]{1,0:T(8,128)(2,1)S(1)}, u32[]{:S(2)}, u32[]{:S(2)}) collective-permute-start(bf16[544,256]{1,0:T(8,128)(2,1)} %pack.1.refs_1_), channel_id=1, source_target_pairs={{0,4},{1,5},{2,6},{3,7},{4,0},{5,1},{6,2},{7,3},{8,12},{9,13},{10,... | collective-permute-start | bytes 835592 | tf_op jit(solution)/shard_map/ppermute | solution.py:384
  8.1 1.0 %copy-start = (bf16[544,256]{1,0:T(8,128)(2,1)S(1)}, bf16[544,256]{1,0:T(8,128)(2,1)}, u32[]{:S(2)}) copy-start(bf16[544,256]{1,0:T(8,128)(2,1)} %pack.1.refs_1_) | copy-start | bytes 835588
  11.7 11.8 %collective-permute-start.5 = (bf16[544,256]{1,0:T(8,128)(2,1)S(1)}, bf16[544,256]{1,0:T(8,128)(2,1)S(1)}, u32[]{:S(2)}, u32[]{:S(2)}) collective-permute-start(bf16[544,256]{1,0:T(8,128)(2,1)S(1)} %copy-done), channel_id=1, source_target_pairs={{0,2},{1,3},{2,0},{3,1},{4,6},{5,7},{6,4},{7,5},{8,10},{9,11},{10,... | collective-permute-start | bytes 835592 | tf_op jit(solution)/shard_map/ppermute | solution.py:384
  13.2 10.2 %collective-permute-start.4 = (bf16[512,256]{1,0:T(8,128)(2,1)}, bf16[512,256]{1,0:T(8,128)(2,1)S(1)}, u32[]{:S(2)}, u32[]{:S(2)}) collective-permute-start(bf16[512,256]{1,0:T(8,128)(2,1)} %bitcast.refs_0_), channel_id=1, source_target_pairs={{0,1},{1,0},{2,3},{3,2},{4,5},{5,4},{6,7},{7,6},{8,9},{9,8},{10,11... | collective-permute-start | bytes 786440 | tf_op jit(solution)/shard_map/ppermute | solution.py:384
  19.2 6.0 %collective-permute-start.3 = (bf16[512,256]{1,0:T(8,128)(2,1)S(1)}, bf16[512,256]{1,0:T(8,128)(2,1)S(1)}, u32[]{:S(2)}, u32[]{:S(2)}) collective-permute-start(bf16[512,256]{1,0:T(8,128)(2,1)S(1)} %collective-permute-done.2.refs_0_), channel_id=1, source_target_pairs={{0,1},{1,0},{2,3},{3,2},{4,5},{5,4},{6,7},{7,6},{8,9},{9,8},{10,11... | collective-permute-start | bytes 786440 | tf_op jit(solution)/shard_map/ppermute | solution.py:384
  19.6 14.0 %collective-permute-start.1 = (bf16[544,256]{1,0:T(8,128)(2,1)S(1)}, bf16[544,256]{1,0:T(8,128)(2,1)S(1)}, u32[]{:S(2)}, u32[]{:S(2)}) collective-permute-start(bf16[544,256]{1,0:T(8,128)(2,1)S(1)} %collective-permute-done.refs_1_), channel_id=1, source_target_pairs={{0,2},{1,3},{2,0},{3,1},{4,6},{5,7},{6,4},{7,5},{8,10},{9,11},{10,... | collective-permute-start | bytes 835592 | tf_op jit(solution)/shard_map/ppermute | solution.py:384
  25.3 0.7 copy-start.1
  34.0 9.9 %copy-start.2 = (f32[8,256]{1,0:T(8,128)S(1)}, f32[8,256]{1,0:T(8,128)}, u32[]{:S(2)}) copy-start(f32[8,256]{1,0:T(8,128)} %far_ref.9) | copy-start | bytes 24580
  47.0 4.0 %collective-permute-start.6 = (f32[32,256]{1,0:T(8,128)S(1)}, f32[32,256]{1,0:T(8,128)S(1)}, u32[]{:S(2)}, u32[]{:S(2)}) collective-permute-start(f32[32,256]{1,0:T(8,128)S(1)} %tiles.7), channel_id=1, source_target_pairs={{0,2},{1,3},{2,0},{3,1},{4,6},{5,7},{6,4},{7,5},{8,10},{9,11},{10,... | collective-permute-start | bytes 98312 | tf_op jit(solution)/shard_map/ppermute | solution.py:384
  51.0 3.9 %collective-permute-start.7 = (f32[32,256]{1,0:T(8,128)S(1)}, f32[32,256]{1,0:T(8,128)S(1)}, u32[]{:S(2)}, u32[]{:S(2)}) collective-permute-start(f32[32,256]{1,0:T(8,128)S(1)} %add.16.sums_ref), channel_id=1, source_target_pairs={{0,4},{1,5},{2,6},{3,7},{4,0},{5,1},{6,2},{7,3},{8,12},{9,13},{10,... | collective-permute-start | bytes 98312 | tf_op jit(solution)/shard_map/ppermute | solution.py:384

commit v4 on v3

--- a/solution.py
+++ b/solution.py
@@ -89,12 +89,15 @@
     places = [place for _, place in blocks]
     used = len(blocks)
     told = [place - counts[0] for place in places if place >= counts[0]]
+    latest = []
+    for place in places:
+        latest.append(place - counts[0] if place >= counts[0] else latest[-1] if latest else told[0] if told else 0)
 
     def body(*refs):
         points_refs = refs[:used]
         lhs_ref, rhs_ref, half_ref = refs[-4:-1] if told else refs[-3:]
         row = lax.broadcasted_iota(jnp.int32, (DEPTH - dims, size), 0)
-        ones = jnp.where(row < 3, 1.0, 0.0).astype(jnp.float32)
+        ones = jnp.where(row < 3, 1.0, 0.0).astype(jnp.bfloat16)
 
         def write(points_ref, place):
             if place >= counts[0]:
@@ -110,19 +113,22 @@
                 extra = jnp.where(row == 0, high, jnp.where(row == 1, mid, jnp.where(row == 2, low, 0.0)))
                 rhs_ref[0, c, :dims, :] = raw
                 rhs_ref[0, c, dims:, :] = extra.astype(jnp.bfloat16)
-                lhs_ref[0, c] = jnp.concatenate([INV_EPS * wide, ones], axis=0).T.astype(jnp.bfloat16)
+                lhs_ref[0, c] = jnp.concatenate([raw * jnp.asarray(INV_EPS, raw.dtype), ones], axis=0).T
                 return carry
 
-            lax.fori_loop(0, clusters, one, 0, unroll=2)
+            lax.fori_loop(0, clusters, one, 0, unroll=True)
 
         for i, points_ref in enumerate(points_refs):
             pl.when(pl.program_id(0) == i)(functools.partial(write, points_ref, places[i]))
 
+    def at_step(i, values):
+        chosen = values[0]
+        for j, value in enumerate(values[1:]):
+            chosen = jnp.where(i > j, value, chosen)
+        return chosen
+
     def place_of(i):
-        chosen = places[0]
-        for j, place in enumerate(places[1:]):
-            chosen = jnp.where(i > j, place, chosen)
-        return chosen
+        return at_step(i, places)
 
     count = sum(counts)
     shapes = [
@@ -135,7 +141,7 @@
         pl.BlockSpec((1, clusters, size, DEPTH), lambda i: (place_of(i), 0, 0, 0)),
         pl.BlockSpec((1, clusters, DEPTH, size), lambda i: (place_of(i), 0, 0, 0)),
         pl.BlockSpec((1, clusters, size), lambda i: (place_of(i), 0, 0)),
-        pl.BlockSpec((1, clusters, size), lambda i: (told[-1], 0, 0)),
+        pl.BlockSpec((1, clusters, size), lambda i: (at_step(i, latest), 0, 0)),
     ]
     parts = 4 if told else 3
     held = [] if state is None else list(state[:parts])
@@ -191,12 +197,20 @@
             return lax.fori_loop(0, sources // 8, one, filled)
 
         filled = fill(early, jnp.int32(2))
-        for extra in range(PART):
-            out_ref[filled + extra] = nobody
+
+        @pl.when(lax.rem(filled - 2, PART) != 0)
+        def _():
+            for extra in range(PART):
+                out_ref[filled + extra] = nobody
+
         begin = lax.div(filled - 2 + (PART - 1), PART) * PART
         filled = fill(late, begin + 2)
-        for extra in range(GROUP):
-            out_ref[filled + extra] = nobody
+
+        @pl.when(lax.rem(filled - 2, GROUP) != 0)
+        def _():
+            for extra in range(GROUP):
+                out_ref[filled + extra] = nobody
+
         out_ref[0] = begin
         out_ref[1] = filled - 2
 
@@ -313,8 +327,8 @@
         store(low, run(lambda term: jnp.where(term > edge, term - (HIGH_OFFSET - LOW_OFFSET), NOTHING)))
 
 
-def row_kernel(terms, sources, pairs_ref, home_ref, lhs_ref, rhs_ref, half_ref, far_ref, sums_ref, come_ref, out_ref, extra_ref, acc_ref):
-    sums = load_sums([sums_ref, come_ref], home_ref[1], far_ref.shape[0])
+def row_kernel(terms, sources, pairs_ref, home_ref, lhs_ref, rhs_ref, half_ref, far_ref, sums_ref, out_ref, extra_ref, acc_ref):
+    sums = load_sums([sums_ref.at[i] for i in range(sums_ref.shape[0])], home_ref[1], far_ref.shape[0])
     pot = -KEEP_TAU * SCALE_EPS * (jnp.log(sums) - column_offset(terms))
     values = INV_EPS * (pot - half_ref[sources:, :]) - LOW_OFFSET
     total = sum_pairs(pairs_ref, lhs_ref, rhs_ref, sources, values, extra_ref, acc_ref, True)
@@ -329,8 +343,8 @@
     return LOG_LARGEST - COLUMN_TOP - math.log(terms)
 
 
-def column_kernel(terms, sources, first, pairs_ref, home_ref, lhs_ref, rhs_ref, half_ref, far_ref, sums_ref, out_ref, *refs):
-    pot_refs, (extra_ref, acc_ref) = refs[:-2], refs[-2:]
+def column_kernel(terms, sources, first, last, pairs_ref, home_ref, lhs_ref, rhs_ref, half_ref, far_ref, sums_ref, out_ref, *refs):
+    pot_refs, (extra_ref, acc_ref, own_ref, sem) = refs[:-4], refs[-4:]
     parts, own = range(sums_ref.shape[0]), far_ref.shape[0]
     if first:
         logs = [load_sums([sums_ref.at[i]], home_ref[0], own) for i in parts]
@@ -339,24 +353,31 @@
     else:
         log_sum = jnp.log(load_sums([sums_ref.at[i] for i in parts], home_ref[0], own)) + LOW_OFFSET
     pot = -KEEP_TAU * SCALE_EPS * log_sum
+    own_ref[...] = pot[:own]
+    copies = [pltpu.make_async_copy(own_ref, pot_ref, sem) for pot_ref in pot_refs]
+    for copy in copies:
+        copy.start()
     values = INV_EPS * (pot - half_ref[:sources, :]) + column_offset(terms)
     total = sum_pairs(pairs_ref, lhs_ref, rhs_ref, sources, values, extra_ref, acc_ref, False)
-    store_sums(total, home_ref[1], out_ref, jnp.exp(far_ref[...] + column_offset(terms)))
-    for pot_ref in pot_refs:
-        pot_ref[...] = pot[:own]
-
-
-def run_pass(kernel, out_shapes, pairs, home, state, width, others, tiles, *rest):
+    far = jnp.exp(far_ref[...] + column_offset(terms))
+    for out_at in [out_ref.at[i] for i in range(out_ref.shape[0])] if not last else [out_ref]:
+        store_sums(total, home_ref[1], out_at, far)
+    for copy in copies:
+        copy.wait()
+
+
+def run_pass(kernel, out_shapes, pairs, home, state, width, others, tiles, *rest, scratch=()):
     size = state[0].shape[1]
     space = pl.BlockSpec(memory_space=pltpu.VMEM)
     return pl.pallas_call(
         kernel,
         out_shape=out_shapes,
         in_specs=[pl.BlockSpec(memory_space=pltpu.SMEM)] * 2 + [space] * (3 + len(rest)),
-        out_specs=jax.tree.map(lambda _: space, out_shapes),
+        out_specs=[space] + [pl.BlockSpec(memory_space=pl.ANY)] * (len(out_shapes) - 1) if isinstance(out_shapes, list) else space,
         scratch_shapes=[
             pltpu.VMEM((size, padded_rows(width)), jnp.bfloat16),
             pltpu.VMEM((others + 1, 8, size), jnp.float32),
+            *scratch,
         ],
         compiler_params=pltpu.CompilerParams(vmem_limit_bytes=VMEM),
         cost_estimate=pl.CostEstimate(
@@ -427,10 +448,7 @@
     def pairs_of(sources_at, targets_at):
         return [(src_blocks[at], at) for at in sources_at] + [(tgt_blocks[at], nr + at) for at in targets_at]
 
-    by_hops = lambda places: sorted(places, key=lambda at: (at.bit_count(), at))[1:]
-    src_order, tgt_order = by_hops(range(nr)), by_hops(early)
-    for i in range(max(len(src_order), len(tgt_order))):
-        state = ready(pairs_of(src_order[i:i + 1], tgt_order[i:i + 1]), state=state)
+    state = ready(pairs_of([], early[1:2]) + pairs_of(range(1, 2), early[2:]) + pairs_of(range(2, nr), []), state=state)
 
     def flat(state):
         return [a.reshape((-1,) + a.shape[2:]) for a in state]
@@ -459,23 +477,24 @@
             sums = run_pass(
                 functools.partial(row_kernel, terms, sources),
                 jax.ShapeDtypeStruct((sources, size), f32),
-                pairs, home, state, targets, sources, tiles, far_src, *sums,
+                pairs, home, state, targets, sources, tiles, far_src, sums,
             )
         sums = lax.all_gather(sums, "src", axis_index_groups=groups(source_bits))
-        shapes = [jax.ShapeDtypeStruct((targets, size), f32), jax.ShapeDtypeStruct((src_count, size), f32)]
+        last = iteration + 1 == ITERS
+        shapes = [jax.ShapeDtypeStruct((targets, size) if last else (nc, targets, size), f32)]
+        shapes += [jax.ShapeDtypeStruct((src_count, size), f32)] if last else []
         column, *src_pot = run_pass(
-            functools.partial(column_kernel, terms, sources, first),
-            shapes if iteration + 1 == ITERS else shapes[:1],
+            functools.partial(column_kernel, terms, sources, first, last),
+            shapes,
             pairs, home, state, sources, targets, tiles, far_tgt, sums,
+            scratch=(pltpu.VMEM((src_count, size), f32), pltpu.SemaphoreType.DMA),
         )
-        if iteration + 1 < ITERS:
-            for bit in target_bits[:-1]:
-                column = column + across(column, bit)
-            sums = [column, across(column, target_bits[-1])]
+        if not last:
+            sums = lax.all_to_all(column, "src", 0, 0, tiled=True, axis_index_groups=groups(target_bits))
     column = lax.all_to_all(
         column.reshape(nc, tgt_count, size), "src", 0, 0, tiled=True, axis_index_groups=groups(target_bits)
     )
-    tgt_pot = -KEEP_TAU * SCALE_EPS * (jnp.log(jnp.sum(column, axis=0)) - column_offset(terms))
+    tgt_pot = -KEEP_TAU * SCALE_EPS * (jnp.log(sum(column[at] for at in range(nc))) - column_offset(terms))
     return (src_pot[0], tgt_pot)
 
 

time: 76.7 us -> 73.8 us (0.962)
  blocking collectives: 26.5 us -> 33.7 us
  waiting for transfers between devices: 6.61 us -> 0.26 us
  Pallas kernels: 29.6 us -> 26.3 us
  starting transfers between devices: 10.2 us -> 9.11 us
    all_to_all x0 -> x1, blocking collectives: none -> 7.48 us  [per_device(): lax.all_to_all(column, 'src', 0, 0, tiled=True, axis_index_groups=groups(...]
    ppermute x8 -> x6, waiting for transfers between devices: 6.61 us -> 0.26 us  [across(): return lax.ppermute(array, 'src', [(i, i ^ apart) for i in range(shards)])]
    pallas_call x5 -> x3, Pallas kernels: 4.58 us -> 1.83 us  [prepare(): pl.pallas_call(body, grid=(used,), out_shape=shapes[:parts], in_specs=[pl...]
    ppermute x8 -> x6, starting transfers between devices: 10.2 us -> 9.11 us  [across(): return lax.ppermute(array, 'src', [(i, i ^ apart) for i in range(shards)])]
    unnamed x6 -> x8, local copies, waits for them, and re-layouts: 1.21 us -> 1.92 us
  transfers between devices with their start and end apart: 8 -> 6, of which waited for: 2 -> 1; matrix products, arithmetic and copies ran while one was open for 1% -> 1% of each run, Pallas kernels for 21% -> 18%
where the time goes in v4:
time: 73.8 us; the launch traced here: 73.4 us
  blocking collectives  33.7 us (46%)
  Pallas kernels  26.3 us (36%)
  starting transfers between devices  9.11 us (12%)
  local copies, waits for them, and re-layouts  1.92 us (3%)
  other arithmetic  1.4 us (2%)
  between operations  0.77 us (1%)
    pallas_call x5, Pallas kernels, run_pass(): pl.pallas_call(kernel, out_shape=out_shapes, in_specs=[pl.BlockSpec(memor...  20.3 us
    all_gather x2, blocking collectives, per_device(): sums = lax.all_gather(sums, 'src', axis_index_groups=groups(source_bits))  13 us
    ppermute x6, starting transfers between devices, across(): return lax.ppermute(array, 'src', [(i, i ^ apart) for i in range(shards)])  9.11 us
    all_to_all x1, blocking collectives, per_device(): lax.all_to_all(column, 'src', 0, 0, tiled=True, axis_index_groups=groups(...  7.48 us
    all_to_all x1, blocking collectives, per_device(): lax.all_to_all(column.reshape(nc, tgt_count, size), 'src', 0, 0, tiled=Tr...  7.11 us
    all_gather x1, blocking collectives, per_device(): lax.all_gather(code, 'src', axis_index_groups=groups(source_bits))  6.07 us
    pallas_call x1, Pallas kernels, list_pairs(): pl.pallas_call(body, out_shape=jax.ShapeDtypeStruct((sources * per_cluste...  2.47 us
    unnamed x8, local copies, waits for them, and re-layouts  1.92 us
  transfers between devices with their start and end apart: 6, of which 1 were waited for; matrix products, arithmetic and copies ran while one was open for 1% of the time, Pallas kernels for 18%

profile of v4, /device:TPU:0, one launch (start us, length us, event | category | flops | bytes accessed | tf_op | source)
XLA Modules:
  0.0 73.4 jit_solution(7681211558251752593)
XLA Ops:
  0.6 4.1 %collective-permute-start.4 = (bf16[512,256]{1,0:T(8,128)(2,1)}, bf16[512,256]{1,0:T(8,128)(2,1)S(1)}, u32[]{:S(2)}, u32[]{:S(2)}) collective-permute-start(bf16[512,256]{1,0:T(8,128)(2,1)} %bitcast.37), channel_id=1, source_target_pairs={{0,8},{1,9},{2,10},{3,11},{4,12},{5,13},{6,14},{7,15},{8,0},{9,1},... | collective-permute-start | bytes 786440 | tf_op jit(solution)/shard_map/ppermute | solution.py:405
  4.7 1.7 %pack.1.refs_1_ = bf16[544,256]{1,0:T(8,128)(2,1)} custom-call(bf16[512,256]{1,0:T(8,128)(2,1)} %bitcast.41, f32[8,256]{1,0:T(8,128)} %refs_1_.1), custom_call_target="tpu_custom_call" | custom-call | tf_op jit(solution)/shard_map/pack/pallas_call | solution.py:75
  6.4 1.6 %collective-permute-start = (bf16[544,256]{1,0:T(8,128)(2,1)}, bf16[544,256]{1,0:T(8,128)(2,1)S(1)}, u32[]{:S(2)}, u32[]{:S(2)}) collective-permute-start(bf16[544,256]{1,0:T(8,128)(2,1)} %pack.1.refs_1_), channel_id=1, source_target_pairs={{0,4},{1,5},{2,6},{3,7},{4,0},{5,1},{6,2},{7,3},{8,12},{9,13},{10,... | collective-permute-start | bytes 835592 | tf_op jit(solution)/shard_map/ppermute | solution.py:405
  8.1 0.1 pad_add_fusion.home_ref
  8.2 1.0 %copy-done = bf16[544,256]{1,0:T(8,128)(2,1)S(1)} copy-done((bf16[544,256]{1,0:T(8,128)(2,1)S(1)}, bf16[544,256]{1,0:T(8,128)(2,1)}, u32[]{:S(2)}) %copy-start) | copy-done | bytes 278552
  9.1 0.9 %copy-done.1 = bf16[8,64,256]{2,1,0:T(8,128)(2,1)S(1)} copy-done((bf16[8,64,256]{2,1,0:T(8,128)(2,1)S(1)}, bf16[8,64,256]{2,1,0:T(8,128)(2,1)}, u32[]{:S(2)}) %copy-start.1) | copy-done | bytes 262168
  10.1 0.4 prepare.3
  10.5 0.7 multiply_add_fusion
  11.2 1.5 %collective-permute-start.2 = (bf16[544,256]{1,0:T(8,128)(2,1)S(1)}, bf16[544,256]{1,0:T(8,128)(2,1)S(1)}, u32[]{:S(2)}, u32[]{:S(2)}) collective-permute-start(bf16[544,256]{1,0:T(8,128)(2,1)S(1)} %copy-done), channel_id=1, source_target_pairs={{0,2},{1,3},{2,0},{3,1},{4,6},{5,7},{6,4},{7,5},{8,10},{9,11},{10,... | collective-permute-start | bytes 835592 | tf_op jit(solution)/shard_map/ppermute | solution.py:405
  12.7 6.1 %all-gather.cand_ref = s32[32,8]{1,0:T(8,128)S(1)} all-gather(s32[8,8]{1,0:T(8,128)S(1)} %multiply_add_fusion), channel_id=2, replica_groups={{0,1,8,9},{2,3,10,11},{4,5,12,13},{6,7,14,15},{16,17,24,25},{18,19,26,2..., dimensions={0}, use_global_device_ids=true | all-gather | bytes 1280 | tf_op jit(solution)/shard_map/all_gather | solution.py:438
  18.8 0.0 collective-permute-done.4.refs_3_
  18.8 0.3 collective-permute-start.5
  19.1 0.2 collective-permute-done.refs_2_
  19.4 1.5 %collective-permute-start.1 = (bf16[544,256]{1,0:T(8,128)(2,1)S(1)}, bf16[544,256]{1,0:T(8,128)(2,1)S(1)}, u32[]{:S(2)}, u32[]{:S(2)}) collective-permute-start(bf16[544,256]{1,0:T(8,128)(2,1)S(1)} %collective-permute-done.refs_2_), channel_id=1, source_target_pairs={{0,2},{1,3},{2,0},{3,1},{4,6},{5,7},{6,4},{7,5},{8,10},{9,11},{10,... | collective-permute-start | bytes 835592 | tf_op jit(solution)/shard_map/ppermute | solution.py:405
  20.9 2.5 %list_pairs.1.pairs_ref = s32[338]{0:T(512)S(1)} custom-call(s32[3]{0:T(128)S(1)} %pad_add_fusion.home_ref, s32[32,8]{1,0:T(8,128)S(1)} %all-gather.cand_ref), custom_call_target="tpu_custom_call" | custom-call | bytes 4194304 | tf_op jit(solution)/shard_map/list_pairs/pallas_call | solution.py:217
  23.4 0.0 copy-start.2
  23.4 0.0 collective-permute-done.3.refs_1_
  23.4 0.0 collective-permute-done.5.refs_4_
  23.4 1.2 %prepare.4 = (bf16[8,8,256,128]{3,2,1,0:T(8,128)(2,1)S(1)}, bf16[8,8,128,256]{3,2,1,0:T(8,128)(2,1)S(1)}, f32[8,8,256]{2,1,0:T(8,128)S(1)}, f32[4,8,256]{2,1,0:T(8,128)S(1)}) custom-call(bf16[544,256]{1,0:T(8,128)(2,1)S(1)} %collective-permute-done.2.refs_0_, ...), custom_call_target="tpu_custom_call", output_to_operand_aliasing={{0}: (5, {}), {1}: (6, {}), {2}: (7, {}), {3}: (8, {})} | custom-call | flops 2621440 | bytes 10485760 | tf_op jit(solution)/shard_map/prepare/pallas_call | solution.py:148
  24.6 7.6 %tiles.5.refs_5_.refs_0_ = f32[2,32,256]{2,1,0:T(8,128)S(1)} custom-call(s32[338]{0:T(512)S(1)} %list_pairs.1.pairs_ref, s32[3]{0:T(128)S(1)} %pad_add_fusion.home_ref, bf16[64,256,128]{2,1,0:T(8,128)(2,1)S(1)} %bitcast.18, bf16[64,128,256]{2,1,0:T(8,128)(2,1)S(1)} %bitcast.23, f32[64,256]{1,0:T(8,128)S(1)} %bitcast.28, f32[8,256]{1,0:T(8,128)S(1)} %copy-done.2, ...), custom_call_target="tpu_custom_call" | custom-call | flops 1073741824 | bytes 8388608 | tf_op jit(solution)/shard_map/tiles/pallas_call | solution.py:372
  32.2 0.0 collective-permute-done.1.refs_0_
  32.2 0.2 prepare.5
  32.4 0.0 copy-start.3
  32.4 3.1 %tiles.6 = f32[32,256]{1,0:T(8,128)S(1)} custom-call(s32[338]{0:T(512)S(1)} %list_pairs.1.pairs_ref, s32[3]{0:T(128)S(1)} %pad_add_fusion.home_ref, bf16[64,256,128]{2,1,0:T(8,128)(2,1)S(1)} %bitcast.19, bf16[64,128,256]{2,1,0:T(8,128)(2,1)S(1)} %bitcast.24, f32[64,256]{1,0:T(8,128)S(1)} %bitcast.29, f32[8,256]{1,0:T(8,128)S(1)} %copy-done.2, ...), custom_call_target="tpu_custom_call" | custom-call | flops 1073741824 | bytes 8388608 | tf_op jit(solution)/shard_map/tiles/pallas_call | solution.py:372
  35.6 6.7 %all-gather.1 = f32[128,256]{1,0:T(8,128)S(1)} all-gather(f32[32,256]{1,0:T(8,128)S(1)} %tiles.6), channel_id=3, replica_groups={{0,1,8,9},{2,3,10,11},{4,5,12,13},{6,7,14,15},{16,17,24,25},{18,19,26,2..., dimensions={0}, use_global_device_ids=true | all-gather | bytes 163840 | tf_op jit(solution)/shard_map/all_gather | solution.py:482
  42.3 3.2 %tiles.7 = f32[4,32,256]{2,1,0:T(8,128)S(1)} custom-call(s32[338]{0:T(512)S(1)} %list_pairs.1.pairs_ref, s32[3]{0:T(128)S(1)} %pad_add_fusion.home_ref, bf16[64,256,128]{2,1,0:T(8,128)(2,1)S(1)} %bitcast.20, bf16[64,128,256]{2,1,0:T(8,128)(2,1)S(1)} %bitcast.25, f32[64,256]{1,0:T(8,128)S(1)} %bitcast.30, f32[8,256]{1,0:T(8,128)S(1)} %copy-done.3, ...), custom_call_target="tpu_custom_call" | custom-call | flops 1073741824 | bytes 8388608 | tf_op jit(solution)/shard_map/tiles/pallas_call | solution.py:372
  45.4 7.5 %all_to_all.10.sums_ref = f32[4,32,256]{2,1,0:T(8,128)S(1)} all-to-all(f32[4,32,256]{2,1,0:T(8,128)S(1)} %tiles.7), channel_id=1, replica_groups={{0,2,4,6},{1,3,5,7},{8,10,12,14},{9,11,13,15},{16,18,20,22},{17,19,21,2..., dimensions={0} | all-to-all | bytes 262144 | tf_op jit(solution)/shard_map/all_to_all | solution.py:493
  52.9 3.3 %tiles.8 = f32[32,256]{1,0:T(8,128)S(1)} custom-call(s32[338]{0:T(512)S(1)} %list_pairs.1.pairs_ref, s32[3]{0:T(128)S(1)} %pad_add_fusion.home_ref, bf16[64,256,128]{2,1,0:T(8,128)(2,1)S(1)} %bitcast.21, bf16[64,128,256]{2,1,0:T(8,128)(2,1)S(1)} %bitcast.26, f32[64,256]{1,0:T(8,128)S(1)} %bitcast.31, f32[8,256]{1,0:T(8,128)S(1)} %copy-done.2, ...), custom_call_target="tpu_custom_call" | custom-call | flops 1073741824 | bytes 8388608 | tf_op jit(solution)/shard_map/tiles/pallas_call | solution.py:372
  56.2 6.3 %all-gather.2 = f32[128,256]{1,0:T(8,128)S(1)} all-gather(f32[32,256]{1,0:T(8,128)S(1)} %tiles.8), channel_id=4, replica_groups={{0,1,8,9},{2,3,10,11},{4,5,12,13},{6,7,14,15},{16,17,24,25},{18,19,26,2..., dimensions={0}, use_global_device_ids=true | all-gather | bytes 163840 | tf_op jit(solution)/shard_map/all_gather | solution.py:482
  62.6 3.1 %tiles.9 = (f32[32,256]{1,0:T(8,128)S(1)}, f32[8,256]{1,0:T(8,128)}) custom-call(s32[338]{0:T(512)S(1)} %list_pairs.1.pairs_ref, s32[3]{0:T(128)S(1)} %pad_add_fusion.home_ref, bf16[64,256,128]{2,1,0:T(8,128)(2,1)S(1)} %bitcast.22, bf16[64,128,256]{2,1,0:T(8,128)(2,1)S(1)} %bitcast.27, f32[64,256]{1,0:T(8,128)S(1)} %bitcast.32, f32[8,256]{1,0:T(8,128)S(1)} %copy-done.3, ...), custom_call_target="tpu_custom_call" | custom-call | flops 1073741824 | bytes 8388608 | tf_op jit(solution)/shard_map/tiles/pallas_call | solution.py:372
  65.7 7.1 %all_to_all.11 = f32[4,8,256]{2,1,0:T(8,128)S(1)} all-to-all(f32[4,8,256]{2,1,0:T(8,128)S(1)} %bitcast.40), channel_id=1, replica_groups={{0,2,4,6},{1,3,5,7},{8,10,12,14},{9,11,13,15},{16,18,20,22},{17,19,21,2..., dimensions={0} | all-to-all | bytes 65536 | tf_op jit(solution)/shard_map/all_to_all | solution.py:494
  72.8 0.6 fusion.3
  (6 shorter events, 0.0 us)
Async XLA Ops:
  0.6 18.2 %collective-permute-start.4 = (bf16[512,256]{1,0:T(8,128)(2,1)}, bf16[512,256]{1,0:T(8,128)(2,1)S(1)}, u32[]{:S(2)}, u32[]{:S(2)}) collective-permute-start(bf16[512,256]{1,0:T(8,128)(2,1)} %bitcast.37), channel_id=1, source_target_pairs={{0,8},{1,9},{2,10},{3,11},{4,12},{5,13},{6,14},{7,15},{8,0},{9,1},... | collective-permute-start | bytes 786440 | tf_op jit(solution)/shard_map/ppermute | solution.py:405
  6.4 12.9 %collective-permute-start = (bf16[544,256]{1,0:T(8,128)(2,1)}, bf16[544,256]{1,0:T(8,128)(2,1)S(1)}, u32[]{:S(2)}, u32[]{:S(2)}) collective-permute-start(bf16[544,256]{1,0:T(8,128)(2,1)} %pack.1.refs_1_), channel_id=1, source_target_pairs={{0,4},{1,5},{2,6},{3,7},{4,0},{5,1},{6,2},{7,3},{8,12},{9,13},{10,... | collective-permute-start | bytes 835592 | tf_op jit(solution)/shard_map/ppermute | solution.py:405
  8.2 1.0 %copy-start = (bf16[544,256]{1,0:T(8,128)(2,1)S(1)}, bf16[544,256]{1,0:T(8,128)(2,1)}, u32[]{:S(2)}) copy-start(bf16[544,256]{1,0:T(8,128)(2,1)} %pack.1.refs_1_) | copy-start | bytes 835588
  9.1 0.9 %copy-start.1 = (bf16[8,64,256]{2,1,0:T(8,128)(2,1)S(1)}, bf16[8,64,256]{2,1,0:T(8,128)(2,1)}, u32[]{:S(2)}) copy-start(bf16[8,64,256]{2,1,0:T(8,128)(2,1)} %param.7) | copy-start | bytes 786436
  11.2 12.2 %collective-permute-start.2 = (bf16[544,256]{1,0:T(8,128)(2,1)S(1)}, bf16[544,256]{1,0:T(8,128)(2,1)S(1)}, u32[]{:S(2)}, u32[]{:S(2)}) collective-permute-start(bf16[544,256]{1,0:T(8,128)(2,1)S(1)} %copy-done), channel_id=1, source_target_pairs={{0,2},{1,3},{2,0},{3,1},{4,6},{5,7},{6,4},{7,5},{8,10},{9,11},{10,... | collective-permute-start | bytes 835592 | tf_op jit(solution)/shard_map/ppermute | solution.py:405
  12.7 10.7 %collective-permute-start.3 = (bf16[512,256]{1,0:T(8,128)(2,1)}, bf16[512,256]{1,0:T(8,128)(2,1)S(1)}, u32[]{:S(2)}, u32[]{:S(2)}) collective-permute-start(bf16[512,256]{1,0:T(8,128)(2,1)} %bitcast.38), channel_id=1, source_target_pairs={{0,1},{1,0},{2,3},{3,2},{4,5},{5,4},{6,7},{7,6},{8,9},{9,8},{10,11... | collective-permute-start | bytes 786440 | tf_op jit(solution)/shard_map/ppermute | solution.py:405
  18.8 4.6 %collective-permute-start.5 = (bf16[512,256]{1,0:T(8,128)(2,1)S(1)}, bf16[512,256]{1,0:T(8,128)(2,1)S(1)}, u32[]{:S(2)}, u32[]{:S(2)}) collective-permute-start(bf16[512,256]{1,0:T(8,128)(2,1)S(1)} %collective-permute-done.4.refs_3_), channel_id=1, source_target_pairs={{0,1},{1,0},{2,3},{3,2},{4,5},{5,4},{6,7},{7,6},{8,9},{9,8},{10,11... | collective-permute-start | bytes 786440 | tf_op jit(solution)/shard_map/ppermute | solution.py:405
  19.4 12.8 %collective-permute-start.1 = (bf16[544,256]{1,0:T(8,128)(2,1)S(1)}, bf16[544,256]{1,0:T(8,128)(2,1)S(1)}, u32[]{:S(2)}, u32[]{:S(2)}) collective-permute-start(bf16[544,256]{1,0:T(8,128)(2,1)S(1)} %collective-permute-done.refs_2_), channel_id=1, source_target_pairs={{0,2},{1,3},{2,0},{3,1},{4,6},{5,7},{6,4},{7,5},{8,10},{9,11},{10,... | collective-permute-start | bytes 835592 | tf_op jit(solution)/shard_map/ppermute | solution.py:405
  23.4 1.2 %copy-start.2 = (f32[8,256]{1,0:T(8,128)S(1)}, f32[8,256]{1,0:T(8,128)}, u32[]{:S(2)}) copy-start(f32[8,256]{1,0:T(8,128)} %far_ref.8) | copy-start | bytes 24580
  32.4 9.8 %copy-start.3 = (f32[8,256]{1,0:T(8,128)S(1)}, f32[8,256]{1,0:T(8,128)}, u32[]{:S(2)}) copy-start(f32[8,256]{1,0:T(8,128)} %far_ref.9) | copy-start | bytes 24580

commit v5 on v4

--- a/solution.py
+++ b/solution.py
@@ -38,49 +38,26 @@
     return high, mid, rest - mid
 
 
-def pack(points, *rows):
-    clusters, dims, size = points[0].shape
-    counts = [len(r) for r in rows]
-    tall = clusters * dims
-
-    flat = [p.reshape(tall, size) for p in points]
-    few = [r for r in rows for r in r]
-
-    def body(*refs):
-        points_refs, refs = refs[:len(points)], refs[len(points):]
-        few_refs, refs = refs[:len(few)], refs[len(few):]
-        out_refs, refs = refs[:len(points)], refs[len(points):]
-        held_refs, sems = refs[:-1], refs[-1]
-        copies = [pltpu.make_async_copy(p, o.at[:tall], sems.at[i]) for i, (p, o) in enumerate(zip(points_refs, out_refs))]
-        loads = [pltpu.make_async_copy(f, h, sems.at[len(copies) + i]) for i, (f, h) in enumerate(zip(few_refs, held_refs))]
-        for copy in loads + copies:
-            copy.start()
-        for copy in loads:
-            copy.wait()
-        held = list(held_refs)
-        for i, n in enumerate(counts):
-            mine, held = held[:n], held[n:]
-            if n > 1:
-                values = [ref[...].astype(jnp.float32) for ref in mine]
-                values = [jnp.concatenate([v, jnp.zeros((v.shape[0], size - v.shape[1]), jnp.float32)], axis=1) for v in values]
-            else:
-                values = list(split3(mine[0][...]))
-            empty = EXTRA - sum(v.shape[0] for v in values)
-            if empty:
-                values.append(jnp.zeros((empty, size), jnp.float32))
-            out_refs[i][tall:, :] = jnp.concatenate(values, axis=0).astype(jnp.bfloat16)
-        for copy in copies:
-            copy.wait()
-
+def pack(points, potentials):
+    tall, size = points.shape
+
+    def body(points_ref, potentials_ref, out_ref):
+        out_ref[:tall, :] = points_ref[...]
+        terms = list(split3(potentials_ref[...]))
+        empty = EXTRA - sum(t.shape[0] for t in terms)
+        if empty:
+            terms.append(jnp.zeros((empty, size), jnp.float32))
+        out_ref[tall:, :] = jnp.concatenate(terms, axis=0).astype(jnp.bfloat16)
+
+    space = pl.BlockSpec(memory_space=pltpu.VMEM)
     return pl.pallas_call(
         body,
-        out_shape=[jax.ShapeDtypeStruct((tall + EXTRA, size), p.dtype) for p in points],
-        in_specs=[pl.BlockSpec(memory_space=pltpu.HBM)] * (len(points) + len(few)),
-        out_specs=[pl.BlockSpec(memory_space=pltpu.VMEM)] * len(points),
-        scratch_shapes=[pltpu.VMEM(f.shape, f.dtype) for f in few] + [pltpu.SemaphoreType.DMA((len(points) + len(few),))],
+        out_shape=jax.ShapeDtypeStruct((tall + EXTRA, size), points.dtype),
+        in_specs=[space] * 2,
+        out_specs=space,
         compiler_params=pltpu.CompilerParams(vmem_limit_bytes=LARGE),
         name="pack",
-    )(*flat, *few)
+    )(points, potentials)
 
 
 def prepare(blocks, clusters, dims, counts, state, after=()):
@@ -167,19 +144,22 @@
     targets = tgt_count << len(target_bits)
     mask = sum(1 << b for b in target_bits)
     nobody = sources * (2 * targets) + targets
+    count = len(early) + len(late)
+    tall, wide = -(-count // 8) * 8, -(-sources // 128) * 128
 
     def body(home_ref, cand_ref, out_ref, table_ref, entries_ref, sem):
-        code = cand_ref[...]
+        code = cand_ref[...].astype(jnp.float32)
+        code = jnp.concatenate([code, jnp.zeros((sources, 128 - per_cluster), jnp.float32)], axis=1)
+        if wide > sources:
+            code = jnp.concatenate([code, jnp.zeros((wide - sources, 128), jnp.float32)], axis=0)
+        code = code.T[:per_cluster].astype(jnp.int32)
         apart = lax.div(code, tgt_count) ^ home_ref[2]
         block = sum(((apart >> bit) & 1) << place for place, bit in enumerate(target_bits))
         inside = (apart & ~mask) == 0
-        row = lax.broadcasted_iota(jnp.int32, code.shape, 0)
-        code = (row ^ (home_ref[0] * tgt_count)) * (2 * targets) + block * tgt_count + lax.rem(code, tgt_count)
-        lane = lax.broadcasted_iota(jnp.int32, table_ref.shape, 1)
-        table = jnp.full(table_ref.shape, -1, jnp.int32)
-        for at in early + late:
-            column = jnp.max(jnp.where(inside & (block == at), code, -1), axis=1, keepdims=True)
-            table = jnp.where(lane == at, column, table)
+        source = lax.broadcasted_iota(jnp.int32, code.shape, 1) ^ (home_ref[0] * tgt_count)
+        code = source * (2 * targets) + block * tgt_count + lax.rem(code, tgt_count)
+        found = [jnp.max(jnp.where(inside & (block == at), code, -1), axis=0, keepdims=True) for at in range(count)]
+        table = jnp.concatenate(found + [jnp.full((tall - count, wide), -1, jnp.int32)] * (tall > count), axis=0)
         table_ref[...] = table
         copy = pltpu.make_async_copy(table_ref, entries_ref, sem)
         copy.start()
@@ -189,7 +169,7 @@
             def one(r, filled):
                 for u in range(8):
                     for k in columns:
-                        entry = entries_ref[r * 8 + u, k]
+                        entry = entries_ref[k, r * 8 + u]
                         out_ref[filled] = entry
                         filled = filled + jnp.where(entry >= 0, 1, 0).astype(jnp.int32)
                 return filled
@@ -220,7 +200,7 @@
         in_specs=[pl.BlockSpec(memory_space=pltpu.SMEM), pl.BlockSpec(memory_space=pltpu.VMEM)],
         out_specs=pl.BlockSpec(memory_space=pltpu.SMEM),
         scratch_shapes=[
-            pltpu.VMEM((sources, 128), jnp.int32), pltpu.SMEM((sources, 128), jnp.int32), pltpu.SemaphoreType.DMA,
+            pltpu.VMEM((tall, wide), jnp.int32), pltpu.SMEM((tall, wide), jnp.int32), pltpu.SemaphoreType.DMA,
         ],
         compiler_params=pltpu.CompilerParams(vmem_limit_bytes=SMALL),
         cost_estimate=pl.CostEstimate(flops=0, bytes_accessed=4 << 20, transcendentals=0),
@@ -422,7 +402,7 @@
     me = lax.axis_index("src").astype(jnp.int32)
     home = jnp.stack([place_of(me, source_bits), place_of(me, target_bits), me])
     src_points = src_points.reshape(-1, size)
-    tgt_message, = pack((tgt_points,), (g_init,))
+    tgt_message = pack(tgt_points.reshape(-1, size), g_init)
     late = [at for at in range(2, nc) if at & 1]
     early = [at for at in range(nc) if at not in late]
     ready = functools.partial(prepare, clusters=src_count, dims=dims, counts=(nr, nc))

time: 73.8 us -> 73.1 us (level)
  no operation moved by 1% of the time
where the time goes in v5:
time: 73.1 us; the launch traced here: 72.8 us
  blocking collectives  33.3 us (46%)
  Pallas kernels  26.1 us (36%)
  starting transfers between devices  9.05 us (12%)
  local copies, waits for them, and re-layouts  1.92 us (3%)
  other arithmetic  1.4 us (2%)
  between operations  0.76 us (1%)
    pallas_call x5, Pallas kernels, run_pass(): pl.pallas_call(kernel, out_shape=out_shapes, in_specs=[pl.BlockSpec(memor...  20.3 us
    all_gather x2, blocking collectives, per_device(): sums = lax.all_gather(sums, 'src', axis_index_groups=groups(source_bits))  12.7 us
    ppermute x6, starting transfers between devices, across(): return lax.ppermute(array, 'src', [(i, i ^ apart) for i in range(shards)])  9.05 us
    all_to_all x1, blocking collectives, per_device(): lax.all_to_all(column, 'src', 0, 0, tiled=True, axis_index_groups=groups(...  7.48 us
    all_to_all x1, blocking collectives, per_device(): lax.all_to_all(column.reshape(nc, tgt_count, size), 'src', 0, 0, tiled=Tr...  7.11 us
    all_gather x1, blocking collectives, per_device(): lax.all_gather(code, 'src', axis_index_groups=groups(source_bits))  6.07 us
    pallas_call x1, Pallas kernels, list_pairs(): pl.pallas_call(body, out_shape=jax.ShapeDtypeStruct((sources * per_cluste...  2.26 us
    unnamed x8, local copies, waits for them, and re-layouts  1.92 us
  transfers between devices with their start and end apart: 6, of which 1 were waited for; matrix products, arithmetic and copies ran while one was open for 1% of the time, Pallas kernels for 18%

profile of v5, /device:TPU:0, one launch (start us, length us, event | category | flops | bytes accessed | tf_op | source)
XLA Modules:
  0.0 72.8 jit_solution(3363169031278140028)
XLA Ops:
  0.6 4.1 %collective-permute-start.4 = (bf16[512,256]{1,0:T(8,128)(2,1)}, bf16[512,256]{1,0:T(8,128)(2,1)S(1)}, u32[]{:S(2)}, u32[]{:S(2)}) collective-permute-start(bf16[512,256]{1,0:T(8,128)(2,1)} %bitcast.37), channel_id=1, source_target_pairs={{0,8},{1,9},{2,10},{3,11},{4,12},{5,13},{6,14},{7,15},{8,0},{9,1},... | collective-permute-start | bytes 786440 | tf_op jit(solution)/shard_map/ppermute | solution.py:385
  4.7 1.7 %pack.1.refs_1_ = bf16[544,256]{1,0:T(8,128)(2,1)} custom-call(bf16[512,256]{1,0:T(8,128)(2,1)} %bitcast.41, f32[8,256]{1,0:T(8,128)} %potentials_ref.1), custom_call_target="tpu_custom_call" | custom-call | tf_op jit(solution)/shard_map/pack/pallas_call | solution.py:53
  6.4 1.6 %collective-permute-start = (bf16[544,256]{1,0:T(8,128)(2,1)}, bf16[544,256]{1,0:T(8,128)(2,1)S(1)}, u32[]{:S(2)}, u32[]{:S(2)}) collective-permute-start(bf16[544,256]{1,0:T(8,128)(2,1)} %pack.1.refs_1_), channel_id=1, source_target_pairs={{0,4},{1,5},{2,6},{3,7},{4,0},{5,1},{6,2},{7,3},{8,12},{9,13},{10,... | collective-permute-start | bytes 835592 | tf_op jit(solution)/shard_map/ppermute | solution.py:385
  8.0 0.1 pad_add_fusion.home_ref
  8.1 1.0 %copy-done = bf16[544,256]{1,0:T(8,128)(2,1)S(1)} copy-done((bf16[544,256]{1,0:T(8,128)(2,1)S(1)}, bf16[544,256]{1,0:T(8,128)(2,1)}, u32[]{:S(2)}) %copy-start) | copy-done | bytes 278552
  9.0 0.9 %copy-done.1 = bf16[8,64,256]{2,1,0:T(8,128)(2,1)S(1)} copy-done((bf16[8,64,256]{2,1,0:T(8,128)(2,1)S(1)}, bf16[8,64,256]{2,1,0:T(8,128)(2,1)}, u32[]{:S(2)}) %copy-start.1) | copy-done | bytes 262168
  10.0 0.4 prepare.3
  10.4 0.7 multiply_add_fusion
  11.1 1.5 %collective-permute-start.2 = (bf16[544,256]{1,0:T(8,128)(2,1)S(1)}, bf16[544,256]{1,0:T(8,128)(2,1)S(1)}, u32[]{:S(2)}, u32[]{:S(2)}) collective-permute-start(bf16[544,256]{1,0:T(8,128)(2,1)S(1)} %copy-done), channel_id=1, source_target_pairs={{0,2},{1,3},{2,0},{3,1},{4,6},{5,7},{6,4},{7,5},{8,10},{9,11},{10,... | collective-permute-start | bytes 835592 | tf_op jit(solution)/shard_map/ppermute | solution.py:385
  12.6 6.1 %all-gather.cand_ref = s32[32,8]{1,0:T(8,128)S(1)} all-gather(s32[8,8]{1,0:T(8,128)S(1)} %multiply_add_fusion), channel_id=2, replica_groups={{0,1,8,9},{2,3,10,11},{4,5,12,13},{6,7,14,15},{16,17,24,25},{18,19,26,2..., dimensions={0}, use_global_device_ids=true | all-gather | bytes 1280 | tf_op jit(solution)/shard_map/all_gather | solution.py:418
  18.7 0.0 collective-permute-done.4.refs_3_
  18.7 0.3 collective-permute-start.5
  19.0 0.2 collective-permute-done.refs_2_
  19.3 1.5 %collective-permute-start.1 = (bf16[544,256]{1,0:T(8,128)(2,1)S(1)}, bf16[544,256]{1,0:T(8,128)(2,1)S(1)}, u32[]{:S(2)}, u32[]{:S(2)}) collective-permute-start(bf16[544,256]{1,0:T(8,128)(2,1)S(1)} %collective-permute-done.refs_2_), channel_id=1, source_target_pairs={{0,2},{1,3},{2,0},{3,1},{4,6},{5,7},{6,4},{7,5},{8,10},{9,11},{10,... | collective-permute-start | bytes 835592 | tf_op jit(solution)/shard_map/ppermute | solution.py:385
  20.8 2.3 %list_pairs.1.pairs_ref = s32[338]{0:T(512)S(1)} custom-call(s32[3]{0:T(128)S(1)} %pad_add_fusion.home_ref, s32[32,8]{1,0:T(8,128)S(1)} %all-gather.cand_ref), custom_call_target="tpu_custom_call" | custom-call | bytes 4194304 | tf_op jit(solution)/shard_map/list_pairs/pallas_call | solution.py:197
  23.1 0.0 copy-start.2
  23.1 0.0 collective-permute-done.2.refs_0_
  23.1 0.0 collective-permute-done.5.refs_4_
  23.1 1.2 %prepare.4 = (bf16[8,8,256,128]{3,2,1,0:T(8,128)(2,1)S(1)}, bf16[8,8,128,256]{3,2,1,0:T(8,128)(2,1)S(1)}, f32[8,8,256]{2,1,0:T(8,128)S(1)}, f32[4,8,256]{2,1,0:T(8,128)S(1)}) custom-call(bf16[544,256]{1,0:T(8,128)(2,1)S(1)} %collective-permute-done.2.refs_0_, ...), custom_call_target="tpu_custom_call", output_to_operand_aliasing={{0}: (5, {}), {1}: (6, {}), {2}: (7, {}), {3}: (8, {})} | custom-call | flops 2621440 | bytes 10485760 | tf_op jit(solution)/shard_map/prepare/pallas_call | solution.py:125
  24.3 7.6 %tiles.5.refs_5_.refs_0_ = f32[2,32,256]{2,1,0:T(8,128)S(1)} custom-call(s32[338]{0:T(512)S(1)} %list_pairs.1.pairs_ref, s32[3]{0:T(128)S(1)} %pad_add_fusion.home_ref, bf16[64,256,128]{2,1,0:T(8,128)(2,1)S(1)} %bitcast.18, bf16[64,128,256]{2,1,0:T(8,128)(2,1)S(1)} %bitcast.23, f32[64,256]{1,0:T(8,128)S(1)} %bitcast.28, f32[8,256]{1,0:T(8,128)S(1)} %copy-done.2, ...), custom_call_target="tpu_custom_call" | custom-call | flops 1073741824 | bytes 8388608 | tf_op jit(solution)/shard_map/tiles/pallas_call | solution.py:352
  31.9 0.0 collective-permute-done.1.refs_0_
  31.9 0.2 prepare.5
  32.1 0.0 copy-start.3
  32.1 3.1 %tiles.6 = f32[32,256]{1,0:T(8,128)S(1)} custom-call(s32[338]{0:T(512)S(1)} %list_pairs.1.pairs_ref, s32[3]{0:T(128)S(1)} %pad_add_fusion.home_ref, bf16[64,256,128]{2,1,0:T(8,128)(2,1)S(1)} %bitcast.19, bf16[64,128,256]{2,1,0:T(8,128)(2,1)S(1)} %bitcast.24, f32[64,256]{1,0:T(8,128)S(1)} %bitcast.29, f32[8,256]{1,0:T(8,128)S(1)} %copy-done.2, ...), custom_call_target="tpu_custom_call" | custom-call | flops 1073741824 | bytes 8388608 | tf_op jit(solution)/shard_map/tiles/pallas_call | solution.py:352
  35.3 6.3 %all-gather.1 = f32[128,256]{1,0:T(8,128)S(1)} all-gather(f32[32,256]{1,0:T(8,128)S(1)} %tiles.6), channel_id=3, replica_groups={{0,1,8,9},{2,3,10,11},{4,5,12,13},{6,7,14,15},{16,17,24,25},{18,19,26,2..., dimensions={0}, use_global_device_ids=true | all-gather | bytes 163840 | tf_op jit(solution)/shard_map/all_gather | solution.py:462
  41.6 3.2 %tiles.7 = f32[4,32,256]{2,1,0:T(8,128)S(1)} custom-call(s32[338]{0:T(512)S(1)} %list_pairs.1.pairs_ref, s32[3]{0:T(128)S(1)} %pad_add_fusion.home_ref, bf16[64,256,128]{2,1,0:T(8,128)(2,1)S(1)} %bitcast.20, bf16[64,128,256]{2,1,0:T(8,128)(2,1)S(1)} %bitcast.25, f32[64,256]{1,0:T(8,128)S(1)} %bitcast.30, f32[8,256]{1,0:T(8,128)S(1)} %copy-done.3, ...), custom_call_target="tpu_custom_call" | custom-call | flops 1073741824 | bytes 8388608 | tf_op jit(solution)/shard_map/tiles/pallas_call | solution.py:352
  44.8 7.5 %all_to_all.10.sums_ref = f32[4,32,256]{2,1,0:T(8,128)S(1)} all-to-all(f32[4,32,256]{2,1,0:T(8,128)S(1)} %tiles.7), channel_id=1, replica_groups={{0,2,4,6},{1,3,5,7},{8,10,12,14},{9,11,13,15},{16,18,20,22},{17,19,21,2..., dimensions={0} | all-to-all | bytes 262144 | tf_op jit(solution)/shard_map/all_to_all | solution.py:473
  52.3 3.3 %tiles.8 = f32[32,256]{1,0:T(8,128)S(1)} custom-call(s32[338]{0:T(512)S(1)} %list_pairs.1.pairs_ref, s32[3]{0:T(128)S(1)} %pad_add_fusion.home_ref, bf16[64,256,128]{2,1,0:T(8,128)(2,1)S(1)} %bitcast.21, bf16[64,128,256]{2,1,0:T(8,128)(2,1)S(1)} %bitcast.26, f32[64,256]{1,0:T(8,128)S(1)} %bitcast.31, f32[8,256]{1,0:T(8,128)S(1)} %copy-done.2, ...), custom_call_target="tpu_custom_call" | custom-call | flops 1073741824 | bytes 8388608 | tf_op jit(solution)/shard_map/tiles/pallas_call | solution.py:352
  55.6 6.3 %all-gather.2 = f32[128,256]{1,0:T(8,128)S(1)} all-gather(f32[32,256]{1,0:T(8,128)S(1)} %tiles.8), channel_id=4, replica_groups={{0,1,8,9},{2,3,10,11},{4,5,12,13},{6,7,14,15},{16,17,24,25},{18,19,26,2..., dimensions={0}, use_global_device_ids=true | all-gather | bytes 163840 | tf_op jit(solution)/shard_map/all_gather | solution.py:462
  61.9 3.1 %tiles.9 = (f32[32,256]{1,0:T(8,128)S(1)}, f32[8,256]{1,0:T(8,128)}) custom-call(s32[338]{0:T(512)S(1)} %list_pairs.1.pairs_ref, s32[3]{0:T(128)S(1)} %pad_add_fusion.home_ref, bf16[64,256,128]{2,1,0:T(8,128)(2,1)S(1)} %bitcast.22, bf16[64,128,256]{2,1,0:T(8,128)(2,1)S(1)} %bitcast.27, f32[64,256]{1,0:T(8,128)S(1)} %bitcast.32, f32[8,256]{1,0:T(8,128)S(1)} %copy-done.3, ...), custom_call_target="tpu_custom_call" | custom-call | flops 1073741824 | bytes 8388608 | tf_op jit(solution)/shard_map/tiles/pallas_call | solution.py:352
  65.1 7.1 %all_to_all.11 = f32[4,8,256]{2,1,0:T(8,128)S(1)} all-to-all(f32[4,8,256]{2,1,0:T(8,128)S(1)} %bitcast.40), channel_id=1, replica_groups={{0,2,4,6},{1,3,5,7},{8,10,12,14},{9,11,13,15},{16,18,20,22},{17,19,21,2..., dimensions={0} | all-to-all | bytes 65536 | tf_op jit(solution)/shard_map/all_to_all | solution.py:474
  72.2 0.6 fusion.3
  (6 shorter events, 0.0 us)
Async XLA Ops:
  0.6 18.1 %collective-permute-start.4 = (bf16[512,256]{1,0:T(8,128)(2,1)}, bf16[512,256]{1,0:T(8,128)(2,1)S(1)}, u32[]{:S(2)}, u32[]{:S(2)}) collective-permute-start(bf16[512,256]{1,0:T(8,128)(2,1)} %bitcast.37), channel_id=1, source_target_pairs={{0,8},{1,9},{2,10},{3,11},{4,12},{5,13},{6,14},{7,15},{8,0},{9,1},... | collective-permute-start | bytes 786440 | tf_op jit(solution)/shard_map/ppermute | solution.py:385
  6.4 12.9 %collective-permute-start = (bf16[544,256]{1,0:T(8,128)(2,1)}, bf16[544,256]{1,0:T(8,128)(2,1)S(1)}, u32[]{:S(2)}, u32[]{:S(2)}) collective-permute-start(bf16[544,256]{1,0:T(8,128)(2,1)} %pack.1.refs_1_), channel_id=1, source_target_pairs={{0,4},{1,5},{2,6},{3,7},{4,0},{5,1},{6,2},{7,3},{8,12},{9,13},{10,... | collective-permute-start | bytes 835592 | tf_op jit(solution)/shard_map/ppermute | solution.py:385
  8.1 1.0 %copy-start = (bf16[544,256]{1,0:T(8,128)(2,1)S(1)}, bf16[544,256]{1,0:T(8,128)(2,1)}, u32[]{:S(2)}) copy-start(bf16[544,256]{1,0:T(8,128)(2,1)} %pack.1.refs_1_) | copy-start | bytes 835588
  9.0 0.9 %copy-start.1 = (bf16[8,64,256]{2,1,0:T(8,128)(2,1)S(1)}, bf16[8,64,256]{2,1,0:T(8,128)(2,1)}, u32[]{:S(2)}) copy-start(bf16[8,64,256]{2,1,0:T(8,128)(2,1)} %param.7) | copy-start | bytes 786436
  11.1 12.0 %collective-permute-start.2 = (bf16[544,256]{1,0:T(8,128)(2,1)S(1)}, bf16[544,256]{1,0:T(8,128)(2,1)S(1)}, u32[]{:S(2)}, u32[]{:S(2)}) collective-permute-start(bf16[544,256]{1,0:T(8,128)(2,1)S(1)} %copy-done), channel_id=1, source_target_pairs={{0,2},{1,3},{2,0},{3,1},{4,6},{5,7},{6,4},{7,5},{8,10},{9,11},{10,... | collective-permute-start | bytes 835592 | tf_op jit(solution)/shard_map/ppermute | solution.py:385
  12.6 10.5 %collective-permute-start.3 = (bf16[512,256]{1,0:T(8,128)(2,1)}, bf16[512,256]{1,0:T(8,128)(2,1)S(1)}, u32[]{:S(2)}, u32[]{:S(2)}) collective-permute-start(bf16[512,256]{1,0:T(8,128)(2,1)} %bitcast.38), channel_id=1, source_target_pairs={{0,1},{1,0},{2,3},{3,2},{4,5},{5,4},{6,7},{7,6},{8,9},{9,8},{10,11... | collective-permute-start | bytes 786440 | tf_op jit(solution)/shard_map/ppermute | solution.py:385
  18.7 4.4 %collective-permute-start.5 = (bf16[512,256]{1,0:T(8,128)(2,1)S(1)}, bf16[512,256]{1,0:T(8,128)(2,1)S(1)}, u32[]{:S(2)}, u32[]{:S(2)}) collective-permute-start(bf16[512,256]{1,0:T(8,128)(2,1)S(1)} %collective-permute-done.4.refs_3_), channel_id=1, source_target_pairs={{0,1},{1,0},{2,3},{3,2},{4,5},{5,4},{6,7},{7,6},{8,9},{9,8},{10,11... | collective-permute-start | bytes 786440 | tf_op jit(solution)/shard_map/ppermute | solution.py:385
  19.3 12.6 %collective-permute-start.1 = (bf16[544,256]{1,0:T(8,128)(2,1)S(1)}, bf16[544,256]{1,0:T(8,128)(2,1)S(1)}, u32[]{:S(2)}, u32[]{:S(2)}) collective-permute-start(bf16[544,256]{1,0:T(8,128)(2,1)S(1)} %collective-permute-done.refs_2_), channel_id=1, source_target_pairs={{0,2},{1,3},{2,0},{3,1},{4,6},{5,7},{6,4},{7,5},{8,10},{9,11},{10,... | collective-permute-start | bytes 835592 | tf_op jit(solution)/shard_map/ppermute | solution.py:385
  23.1 1.2 %copy-start.2 = (f32[8,256]{1,0:T(8,128)S(1)}, f32[8,256]{1,0:T(8,128)}, u32[]{:S(2)}) copy-start(f32[8,256]{1,0:T(8,128)} %far_ref.8) | copy-start | bytes 24580
  32.1 9.5 %copy-start.3 = (f32[8,256]{1,0:T(8,128)S(1)}, f32[8,256]{1,0:T(8,128)}, u32[]{:S(2)}) copy-start(f32[8,256]{1,0:T(8,128)} %far_ref.9) | copy-start | bytes 24580

commit v6 on v5

--- a/solution.py
+++ b/solution.py
@@ -25,6 +25,8 @@
 DEPTH = 128
 GROUP = 64
 PART = 16
+FIRST = 48
+HEAD = 4
 EXTRA = 32
 VMEM = 12 * 1024 * 1024
 SMALL = 1024 * 1024
@@ -176,27 +178,29 @@
 
             return lax.fori_loop(0, sources // 8, one, filled)
 
-        filled = fill(early, jnp.int32(2))
-
-        @pl.when(lax.rem(filled - 2, PART) != 0)
+        filled = fill(early, jnp.int32(HEAD))
+
+        @pl.when(lax.rem(filled - HEAD, FIRST) != 0)
         def _():
-            for extra in range(PART):
+            for extra in range(FIRST):
                 out_ref[filled + extra] = nobody
 
-        begin = lax.div(filled - 2 + (PART - 1), PART) * PART
-        filled = fill(late, begin + 2)
-
-        @pl.when(lax.rem(filled - 2, GROUP) != 0)
+        begin = lax.div(filled - HEAD + (FIRST - 1), FIRST) * FIRST
+        filled = fill(late, begin + HEAD)
+
+        @pl.when(lax.rem(filled - HEAD, GROUP) != 0)
         def _():
             for extra in range(GROUP):
                 out_ref[filled + extra] = nobody
 
         out_ref[0] = begin
-        out_ref[1] = filled - 2
+        out_ref[1] = filled - HEAD
+        out_ref[2] = home_ref[0]
+        out_ref[3] = home_ref[1]
 
     return pl.pallas_call(
         body,
-        out_shape=jax.ShapeDtypeStruct((sources * per_cluster + 2 + PART + GROUP,), jnp.int32),
+        out_shape=jax.ShapeDtypeStruct((sources * per_cluster + HEAD + FIRST + GROUP,), jnp.int32),
         in_specs=[pl.BlockSpec(memory_space=pltpu.SMEM), pl.BlockSpec(memory_space=pltpu.VMEM)],
         out_specs=pl.BlockSpec(memory_space=pltpu.SMEM),
         scratch_shapes=[
@@ -226,11 +230,11 @@
     row = lax.broadcasted_iota(jnp.int32, (wide, size), 0)
     row = jnp.where(row < 3 * count, lax.rem(row, count), count)
 
-    length = GROUP if part == ALL else PART
+    length = {ALL: GROUP, EARLY: FIRST, LATE: PART}[part]
 
     def step(g, carry):
         for u in range(length):
-            code = pairs_ref[g * length + u + 2]
+            code = pairs_ref[g * length + u + HEAD]
             s, t = lax.div(code, 2 * targets), lax.rem(code, 2 * targets)
             m, place = (t, s) if by_source else (s, t)
             m, n = jnp.minimum(m, count - 1), jnp.minimum(place, others - 1)
@@ -267,7 +271,7 @@
     return jnp.concatenate(blocks, axis=0)
 
 
-def first_row_kernel(sources, known, pairs_ref, home_ref, lhs_ref, rhs_ref, half_ref, far_ref, pot_ref, *refs):
+def first_row_kernel(sources, known, pairs_ref, lhs_ref, rhs_ref, half_ref, far_ref, pot_ref, *refs):
     before_ref, (out_ref, extra_ref, acc_ref) = refs[:-3], refs[-3:]
     pot, half = pot_ref[...], half_ref[sources:, :]
     if known is not None:
@@ -292,7 +296,7 @@
         low, high = log_or_nothing(low) + LOW_OFFSET, log_or_nothing(high) + HIGH_OFFSET
         top = jnp.maximum(low, high)
         logs = top + jnp.log(jnp.exp(low - top) + jnp.exp(high - top))
-        store_sums(logs, home_ref[0], out_ref, jnp.zeros_like(far))
+        store_sums(logs, pairs_ref[2], out_ref, jnp.zeros_like(far))
 
     narrow = jnp.max(pot) <= LOW_TOP * SCALE_EPS
 
@@ -307,12 +311,12 @@
         store(low, run(lambda term: jnp.where(term > edge, term - (HIGH_OFFSET - LOW_OFFSET), NOTHING)))
 
 
-def row_kernel(terms, sources, pairs_ref, home_ref, lhs_ref, rhs_ref, half_ref, far_ref, sums_ref, out_ref, extra_ref, acc_ref):
-    sums = load_sums([sums_ref.at[i] for i in range(sums_ref.shape[0])], home_ref[1], far_ref.shape[0])
+def row_kernel(terms, sources, pairs_ref, lhs_ref, rhs_ref, half_ref, far_ref, sums_ref, out_ref, extra_ref, acc_ref):
+    sums = load_sums([sums_ref.at[i] for i in range(sums_ref.shape[0])], pairs_ref[3], far_ref.shape[0])
     pot = -KEEP_TAU * SCALE_EPS * (jnp.log(sums) - column_offset(terms))
     values = INV_EPS * (pot - half_ref[sources:, :]) - LOW_OFFSET
     total = sum_pairs(pairs_ref, lhs_ref, rhs_ref, sources, values, extra_ref, acc_ref, True)
-    store_sums(total, home_ref[0], out_ref, jnp.exp(far_ref[...] - LOW_OFFSET))
+    store_sums(total, pairs_ref[2], out_ref, jnp.exp(far_ref[...] - LOW_OFFSET))
 
 
 def log_or_nothing(value):
@@ -323,15 +327,15 @@
     return LOG_LARGEST - COLUMN_TOP - math.log(terms)
 
 
-def column_kernel(terms, sources, first, last, pairs_ref, home_ref, lhs_ref, rhs_ref, half_ref, far_ref, sums_ref, out_ref, *refs):
+def column_kernel(terms, sources, first, last, pairs_ref, lhs_ref, rhs_ref, half_ref, far_ref, sums_ref, out_ref, *refs):
     pot_refs, (extra_ref, acc_ref, own_ref, sem) = refs[:-4], refs[-4:]
     parts, own = range(sums_ref.shape[0]), far_ref.shape[0]
     if first:
-        logs = [load_sums([sums_ref.at[i]], home_ref[0], own) for i in parts]
+        logs = [load_sums([sums_ref.at[i]], pairs_ref[2], own) for i in parts]
         top = functools.reduce(jnp.maximum, logs)
         log_sum = top + jnp.log(sum(jnp.exp(log - top) for log in logs))
     else:
-        log_sum = jnp.log(load_sums([sums_ref.at[i] for i in parts], home_ref[0], own)) + LOW_OFFSET
+        log_sum = jnp.log(load_sums([sums_ref.at[i] for i in parts], pairs_ref[2], own)) + LOW_OFFSET
     pot = -KEEP_TAU * SCALE_EPS * log_sum
     own_ref[...] = pot[:own]
     copies = [pltpu.make_async_copy(own_ref, pot_ref, sem) for pot_ref in pot_refs]
@@ -341,18 +345,18 @@
     total = sum_pairs(pairs_ref, lhs_ref, rhs_ref, sources, values, extra_ref, acc_ref, False)
     far = jnp.exp(far_ref[...] + column_offset(terms))
     for out_at in [out_ref.at[i] for i in range(out_ref.shape[0])] if not last else [out_ref]:
-        store_sums(total, home_ref[1], out_at, far)
+        store_sums(total, pairs_ref[3], out_at, far)
     for copy in copies:
         copy.wait()
 
 
-def run_pass(kernel, out_shapes, pairs, home, state, width, others, tiles, *rest, scratch=()):
+def run_pass(kernel, out_shapes, pairs, state, width, others, tiles, *rest, scratch=()):
     size = state[0].shape[1]
     space = pl.BlockSpec(memory_space=pltpu.VMEM)
     return pl.pallas_call(
         kernel,
         out_shape=out_shapes,
-        in_specs=[pl.BlockSpec(memory_space=pltpu.SMEM)] * 2 + [space] * (3 + len(rest)),
+        in_specs=[pl.BlockSpec(memory_space=pltpu.SMEM)] + [space] * (3 + len(rest)),
         out_specs=[space] + [pl.BlockSpec(memory_space=pl.ANY)] * (len(out_shapes) - 1) if isinstance(out_shapes, list) else space,
         scratch_shapes=[
             pltpu.VMEM((size, padded_rows(width)), jnp.bfloat16),
@@ -364,7 +368,7 @@
             flops=2 * tiles * size * size * DEPTH, bytes_accessed=8 << 20, transcendentals=tiles * size * size
         ),
         name="tiles",
-    )(pairs, home, *state, *rest)
+    )(pairs, *state, *rest)
 
 
 def per_device(src_points, tgt_points, g_init, far_src, far_tgt, cand_owner, cand_local):
@@ -443,7 +447,7 @@
             before = run_pass(
                 functools.partial(first_row_kernel, sources, known),
                 jax.ShapeDtypeStruct((2, sources, size), f32),
-                pairs, home, operands, targets, sources, tiles, far_src, pot,
+                pairs, operands, targets, sources, tiles, far_src, pot,
             )
             for at in late:
                 state = ready(pairs_of([], [at]), state=state, after=(before,))
@@ -451,13 +455,13 @@
             sums = run_pass(
                 functools.partial(first_row_kernel, sources, None),
                 jax.ShapeDtypeStruct((sources, size), f32),
-                pairs, home, state, targets, sources, tiles, far_src, pot, before,
+                pairs, state, targets, sources, tiles, far_src, pot, before,
             )
         else:
             sums = run_pass(
                 functools.partial(row_kernel, terms, sources),
                 jax.ShapeDtypeStruct((sources, size), f32),
-                pairs, home, state, targets, sources, tiles, far_src, sums,
+                pairs, state, targets, sources, tiles, far_src, sums,
             )
         sums = lax.all_gather(sums, "src", axis_index_groups=groups(source_bits))
         last = iteration + 1 == ITERS
@@ -466,7 +470,7 @@
         column, *src_pot = run_pass(
             functools.partial(column_kernel, terms, sources, first, last),
             shapes,
-            pairs, home, state, sources, targets, tiles, far_tgt, sums,
+            pairs, state, sources, targets, tiles, far_tgt, sums,
             scratch=(pltpu.VMEM((src_count, size), f32), pltpu.SemaphoreType.DMA),
         )
         if not last:

time: 73.1 us -> 72.4 us (level)
  Pallas kernels: 26.1 us -> 25.3 us
    pallas_call x5, Pallas kernels: 20.3 us -> 19.5 us  [run_pass(): pl.pallas_call(kernel, out_shape=out_shapes, in_specs=[pl.BlockSpec(memor...]
  transfers between devices with their start and end apart: 6 -> 6, of which waited for: 1 -> 1; matrix products, arithmetic and copies ran while one was open for 1% -> 1% of each run, Pallas kernels for 18% -> 17%
where the time goes in v6:
time: 72.4 us; the launch traced here: 72.1 us
  blocking collectives  33.3 us (46%)
  Pallas kernels  25.3 us (35%)
  starting transfers between devices  9.05 us (12%)
  local copies, waits for them, and re-layouts  1.92 us (3%)
  other arithmetic  1.4 us (2%)
  between operations  0.76 us (1%)
    pallas_call x5, Pallas kernels, run_pass(): pl.pallas_call(kernel, out_shape=out_shapes, in_specs=[pl.BlockSpec(memor...  19.5 us
    all_gather x2, blocking collectives, per_device(): sums = lax.all_gather(sums, 'src', axis_index_groups=groups(source_bits))  12.7 us
    ppermute x6, starting transfers between devices, across(): return lax.ppermute(array, 'src', [(i, i ^ apart) for i in range(shards)])  9.05 us
    all_to_all x1, blocking collectives, per_device(): lax.all_to_all(column, 'src', 0, 0, tiled=True, axis_index_groups=groups(...  7.49 us
    all_to_all x1, blocking collectives, per_device(): lax.all_to_all(column.reshape(nc, tgt_count, size), 'src', 0, 0, tiled=Tr...  7.11 us
    all_gather x1, blocking collectives, per_device(): lax.all_gather(code, 'src', axis_index_groups=groups(source_bits))  6.07 us
    pallas_call x1, Pallas kernels, list_pairs(): pl.pallas_call(body, out_shape=jax.ShapeDtypeStruct((sources * per_cluste...  2.28 us
    unnamed x8, local copies, waits for them, and re-layouts  1.92 us
  transfers between devices with their start and end apart: 6, of which 1 were waited for; matrix products, arithmetic and copies ran while one was open for 1% of the time, Pallas kernels for 17%

profile of v6, /device:TPU:0, one launch (start us, length us, event | category | flops | bytes accessed | tf_op | source)
XLA Modules:
  0.0 72.1 jit_solution(6999096863592047496)
XLA Ops:
  0.6 4.1 %collective-permute-start.4 = (bf16[512,256]{1,0:T(8,128)(2,1)}, bf16[512,256]{1,0:T(8,128)(2,1)S(1)}, u32[]{:S(2)}, u32[]{:S(2)}) collective-permute-start(bf16[512,256]{1,0:T(8,128)(2,1)} %bitcast.37), channel_id=1, source_target_pairs={{0,8},{1,9},{2,10},{3,11},{4,12},{5,13},{6,14},{7,15},{8,0},{9,1},... | collective-permute-start | bytes 786440 | tf_op jit(solution)/shard_map/ppermute | solution.py:389
  4.7 1.7 %pack.1.refs_1_ = bf16[544,256]{1,0:T(8,128)(2,1)} custom-call(bf16[512,256]{1,0:T(8,128)(2,1)} %bitcast.41, f32[8,256]{1,0:T(8,128)} %potentials_ref.1), custom_call_target="tpu_custom_call" | custom-call | tf_op jit(solution)/shard_map/pack/pallas_call | solution.py:55
  6.4 1.6 %collective-permute-start = (bf16[544,256]{1,0:T(8,128)(2,1)}, bf16[544,256]{1,0:T(8,128)(2,1)S(1)}, u32[]{:S(2)}, u32[]{:S(2)}) collective-permute-start(bf16[544,256]{1,0:T(8,128)(2,1)} %pack.1.refs_1_), channel_id=1, source_target_pairs={{0,4},{1,5},{2,6},{3,7},{4,0},{5,1},{6,2},{7,3},{8,12},{9,13},{10,... | collective-permute-start | bytes 835592 | tf_op jit(solution)/shard_map/ppermute | solution.py:389
  8.0 0.1 pad_add_fusion.home_ref
  8.1 1.0 %copy-done = bf16[544,256]{1,0:T(8,128)(2,1)S(1)} copy-done((bf16[544,256]{1,0:T(8,128)(2,1)S(1)}, bf16[544,256]{1,0:T(8,128)(2,1)}, u32[]{:S(2)}) %copy-start) | copy-done | bytes 278552
  9.0 0.9 %copy-done.1 = bf16[8,64,256]{2,1,0:T(8,128)(2,1)S(1)} copy-done((bf16[8,64,256]{2,1,0:T(8,128)(2,1)S(1)}, bf16[8,64,256]{2,1,0:T(8,128)(2,1)}, u32[]{:S(2)}) %copy-start.1) | copy-done | bytes 262168
  10.0 0.4 prepare.3
  10.4 0.7 multiply_add_fusion
  11.1 1.5 %collective-permute-start.2 = (bf16[544,256]{1,0:T(8,128)(2,1)S(1)}, bf16[544,256]{1,0:T(8,128)(2,1)S(1)}, u32[]{:S(2)}, u32[]{:S(2)}) collective-permute-start(bf16[544,256]{1,0:T(8,128)(2,1)S(1)} %copy-done), channel_id=1, source_target_pairs={{0,2},{1,3},{2,0},{3,1},{4,6},{5,7},{6,4},{7,5},{8,10},{9,11},{10,... | collective-permute-start | bytes 835592 | tf_op jit(solution)/shard_map/ppermute | solution.py:389
  12.6 0.0 collective-permute-start.3
  12.6 6.1 %all-gather.cand_ref = s32[32,8]{1,0:T(8,128)S(1)} all-gather(s32[8,8]{1,0:T(8,128)S(1)} %multiply_add_fusion), channel_id=2, replica_groups={{0,1,8,9},{2,3,10,11},{4,5,12,13},{6,7,14,15},{16,17,24,25},{18,19,26,2..., dimensions={0}, use_global_device_ids=true | all-gather | bytes 1280 | tf_op jit(solution)/shard_map/all_gather | solution.py:422
  18.7 0.0 collective-permute-done.4.refs_3_
  18.7 0.3 collective-permute-start.5
  19.0 0.2 collective-permute-done.refs_2_
  19.3 1.5 %collective-permute-start.1 = (bf16[544,256]{1,0:T(8,128)(2,1)S(1)}, bf16[544,256]{1,0:T(8,128)(2,1)S(1)}, u32[]{:S(2)}, u32[]{:S(2)}) collective-permute-start(bf16[544,256]{1,0:T(8,128)(2,1)S(1)} %collective-permute-done.refs_2_), channel_id=1, source_target_pairs={{0,2},{1,3},{2,0},{3,1},{4,6},{5,7},{6,4},{7,5},{8,10},{9,11},{10,... | collective-permute-start | bytes 835592 | tf_op jit(solution)/shard_map/ppermute | solution.py:389
  20.8 2.3 %list_pairs.1.pairs_ref = s32[372]{0:T(512)S(1)} custom-call(s32[3]{0:T(128)S(1)} %pad_add_fusion.home_ref, s32[32,8]{1,0:T(8,128)S(1)} %all-gather.cand_ref), custom_call_target="tpu_custom_call" | custom-call | bytes 4194304 | tf_op jit(solution)/shard_map/list_pairs/pallas_call | solution.py:201
  23.1 0.0 copy-start.2
  23.1 0.0 collective-permute-done.3.refs_1_
  23.2 0.0 collective-permute-done.5.refs_4_
  23.2 1.2 %prepare.4 = (bf16[8,8,256,128]{3,2,1,0:T(8,128)(2,1)S(1)}, bf16[8,8,128,256]{3,2,1,0:T(8,128)(2,1)S(1)}, f32[8,8,256]{2,1,0:T(8,128)S(1)}, f32[4,8,256]{2,1,0:T(8,128)S(1)}) custom-call(bf16[544,256]{1,0:T(8,128)(2,1)S(1)} %collective-permute-done.2.refs_0_, ...), custom_call_target="tpu_custom_call", output_to_operand_aliasing={{0}: (5, {}), {1}: (6, {}), {2}: (7, {}), {3}: (8, {})} | custom-call | flops 2621440 | bytes 10485760 | tf_op jit(solution)/shard_map/prepare/pallas_call | solution.py:127
  24.4 6.8 %tiles.5.refs_5_.refs_0_ = f32[2,32,256]{2,1,0:T(8,128)S(1)} custom-call(s32[372]{0:T(512)S(1)} %list_pairs.1.pairs_ref, bf16[64,256,128]{2,1,0:T(8,128)(2,1)S(1)} %bitcast.18, bf16[64,128,256]{2,1,0:T(8,128)(2,1)S(1)} %bitcast.23, f32[64,256]{1,0:T(8,128)S(1)} %bitcast.28, f32[8,256]{1,0:T(8,128)S(1)} %copy-done.2, f32[32,256]{1,0:T(8,128)S(1)} %bitcast.33), custom_call_target="tpu_custom_call" | custom-call | flops 1073741824 | bytes 8388608 | tf_op jit(solution)/shard_map/tiles/pallas_call | solution.py:356
  31.2 0.2 prepare.5
  31.4 0.0 copy-start.3
  31.4 3.3 %tiles.6 = f32[32,256]{1,0:T(8,128)S(1)} custom-call(s32[372]{0:T(512)S(1)} %list_pairs.1.pairs_ref, bf16[64,256,128]{2,1,0:T(8,128)(2,1)S(1)} %bitcast.19, bf16[64,128,256]{2,1,0:T(8,128)(2,1)S(1)} %bitcast.24, f32[64,256]{1,0:T(8,128)S(1)} %bitcast.29, f32[8,256]{1,0:T(8,128)S(1)} %copy-done.2, f32[32,256]{1,0:T(8,128)S(1)} %bitcast.34, ...), custom_call_target="tpu_custom_call" | custom-call | flops 1073741824 | bytes 8388608 | tf_op jit(solution)/shard_map/tiles/pallas_call | solution.py:356
  34.7 6.3 %all-gather.1 = f32[128,256]{1,0:T(8,128)S(1)} all-gather(f32[32,256]{1,0:T(8,128)S(1)} %tiles.6), channel_id=3, replica_groups={{0,1,8,9},{2,3,10,11},{4,5,12,13},{6,7,14,15},{16,17,24,25},{18,19,26,2..., dimensions={0}, use_global_device_ids=true | all-gather | bytes 163840 | tf_op jit(solution)/shard_map/all_gather | solution.py:466
  41.1 3.2 %tiles.7 = f32[4,32,256]{2,1,0:T(8,128)S(1)} custom-call(s32[372]{0:T(512)S(1)} %list_pairs.1.pairs_ref, bf16[64,256,128]{2,1,0:T(8,128)(2,1)S(1)} %bitcast.20, bf16[64,128,256]{2,1,0:T(8,128)(2,1)S(1)} %bitcast.25, f32[64,256]{1,0:T(8,128)S(1)} %bitcast.30, f32[8,256]{1,0:T(8,128)S(1)} %copy-done.3, f32[4,32,256]{2,1,0:T(8,128)S(1)} %bitcast.36), custom_call_target="tpu_custom_call" | custom-call | flops 1073741824 | bytes 8388608 | tf_op jit(solution)/shard_map/tiles/pallas_call | solution.py:356
  44.2 7.5 %all_to_all.10.sums_ref = f32[4,32,256]{2,1,0:T(8,128)S(1)} all-to-all(f32[4,32,256]{2,1,0:T(8,128)S(1)} %tiles.7), channel_id=1, replica_groups={{0,2,4,6},{1,3,5,7},{8,10,12,14},{9,11,13,15},{16,18,20,22},{17,19,21,2..., dimensions={0} | all-to-all | bytes 262144 | tf_op jit(solution)/shard_map/all_to_all | solution.py:477
  51.7 3.1 %tiles.8 = f32[32,256]{1,0:T(8,128)S(1)} custom-call(s32[372]{0:T(512)S(1)} %list_pairs.1.pairs_ref, bf16[64,256,128]{2,1,0:T(8,128)(2,1)S(1)} %bitcast.21, bf16[64,128,256]{2,1,0:T(8,128)(2,1)S(1)} %bitcast.26, f32[64,256]{1,0:T(8,128)S(1)} %bitcast.31, f32[8,256]{1,0:T(8,128)S(1)} %copy-done.2, f32[4,32,256]{2,1,0:T(8,128)S(1)} %all_to_all.10.sums_ref), custom_call_target="tpu_custom_call" | custom-call | flops 1073741824 | bytes 8388608 | tf_op jit(solution)/shard_map/tiles/pallas_call | solution.py:356
  54.9 6.3 %all-gather.2 = f32[128,256]{1,0:T(8,128)S(1)} all-gather(f32[32,256]{1,0:T(8,128)S(1)} %tiles.8), channel_id=4, replica_groups={{0,1,8,9},{2,3,10,11},{4,5,12,13},{6,7,14,15},{16,17,24,25},{18,19,26,2..., dimensions={0}, use_global_device_ids=true | all-gather | bytes 163840 | tf_op jit(solution)/shard_map/all_gather | solution.py:466
  61.2 3.1 %tiles.9 = (f32[32,256]{1,0:T(8,128)S(1)}, f32[8,256]{1,0:T(8,128)}) custom-call(s32[372]{0:T(512)S(1)} %list_pairs.1.pairs_ref, bf16[64,256,128]{2,1,0:T(8,128)(2,1)S(1)} %bitcast.22, bf16[64,128,256]{2,1,0:T(8,128)(2,1)S(1)} %bitcast.27, f32[64,256]{1,0:T(8,128)S(1)} %bitcast.32, f32[8,256]{1,0:T(8,128)S(1)} %copy-done.3, f32[4,32,256]{2,1,0:T(8,128)S(1)} %bitcast.35), custom_call_target="tpu_custom_call" | custom-call | flops 1073741824 | bytes 8388608 | tf_op jit(solution)/shard_map/tiles/pallas_call | solution.py:356
  64.3 7.1 %all_to_all.11 = f32[4,8,256]{2,1,0:T(8,128)S(1)} all-to-all(f32[4,8,256]{2,1,0:T(8,128)S(1)} %bitcast.40), channel_id=1, replica_groups={{0,2,4,6},{1,3,5,7},{8,10,12,14},{9,11,13,15},{16,18,20,22},{17,19,21,2..., dimensions={0} | all-to-all | bytes 65536 | tf_op jit(solution)/shard_map/all_to_all | solution.py:478
  71.4 0.6 fusion.3
  (6 shorter events, 0.0 us)
Async XLA Ops:
  0.6 18.1 %collective-permute-start.4 = (bf16[512,256]{1,0:T(8,128)(2,1)}, bf16[512,256]{1,0:T(8,128)(2,1)S(1)}, u32[]{:S(2)}, u32[]{:S(2)}) collective-permute-start(bf16[512,256]{1,0:T(8,128)(2,1)} %bitcast.37), channel_id=1, source_target_pairs={{0,8},{1,9},{2,10},{3,11},{4,12},{5,13},{6,14},{7,15},{8,0},{9,1},... | collective-permute-start | bytes 786440 | tf_op jit(solution)/shard_map/ppermute | solution.py:389
  6.4 12.9 %collective-permute-start = (bf16[544,256]{1,0:T(8,128)(2,1)}, bf16[544,256]{1,0:T(8,128)(2,1)S(1)}, u32[]{:S(2)}, u32[]{:S(2)}) collective-permute-start(bf16[544,256]{1,0:T(8,128)(2,1)} %pack.1.refs_1_), channel_id=1, source_target_pairs={{0,4},{1,5},{2,6},{3,7},{4,0},{5,1},{6,2},{7,3},{8,12},{9,13},{10,... | collective-permute-start | bytes 835592 | tf_op jit(solution)/shard_map/ppermute | solution.py:389
  8.1 1.0 %copy-start = (bf16[544,256]{1,0:T(8,128)(2,1)S(1)}, bf16[544,256]{1,0:T(8,128)(2,1)}, u32[]{:S(2)}) copy-start(bf16[544,256]{1,0:T(8,128)(2,1)} %pack.1.refs_1_) | copy-start | bytes 835588
  9.0 0.9 %copy-start.1 = (bf16[8,64,256]{2,1,0:T(8,128)(2,1)S(1)}, bf16[8,64,256]{2,1,0:T(8,128)(2,1)}, u32[]{:S(2)}) copy-start(bf16[8,64,256]{2,1,0:T(8,128)(2,1)} %param.7) | copy-start | bytes 786436
  11.1 12.0 %collective-permute-start.2 = (bf16[544,256]{1,0:T(8,128)(2,1)S(1)}, bf16[544,256]{1,0:T(8,128)(2,1)S(1)}, u32[]{:S(2)}, u32[]{:S(2)}) collective-permute-start(bf16[544,256]{1,0:T(8,128)(2,1)S(1)} %copy-done), channel_id=1, source_target_pairs={{0,2},{1,3},{2,0},{3,1},{4,6},{5,7},{6,4},{7,5},{8,10},{9,11},{10,... | collective-permute-start | bytes 835592 | tf_op jit(solution)/shard_map/ppermute | solution.py:389
  12.6 10.5 %collective-permute-start.3 = (bf16[512,256]{1,0:T(8,128)(2,1)}, bf16[512,256]{1,0:T(8,128)(2,1)S(1)}, u32[]{:S(2)}, u32[]{:S(2)}) collective-permute-start(bf16[512,256]{1,0:T(8,128)(2,1)} %bitcast.38), channel_id=1, source_target_pairs={{0,1},{1,0},{2,3},{3,2},{4,5},{5,4},{6,7},{7,6},{8,9},{9,8},{10,11... | collective-permute-start | bytes 786440 | tf_op jit(solution)/shard_map/ppermute | solution.py:389
  18.7 4.4 %collective-permute-start.5 = (bf16[512,256]{1,0:T(8,128)(2,1)S(1)}, bf16[512,256]{1,0:T(8,128)(2,1)S(1)}, u32[]{:S(2)}, u32[]{:S(2)}) collective-permute-start(bf16[512,256]{1,0:T(8,128)(2,1)S(1)} %collective-permute-done.4.refs_3_), channel_id=1, source_target_pairs={{0,1},{1,0},{2,3},{3,2},{4,5},{5,4},{6,7},{7,6},{8,9},{9,8},{10,11... | collective-permute-start | bytes 786440 | tf_op jit(solution)/shard_map/ppermute | solution.py:389
  19.3 11.9 %collective-permute-start.1 = (bf16[544,256]{1,0:T(8,128)(2,1)S(1)}, bf16[544,256]{1,0:T(8,128)(2,1)S(1)}, u32[]{:S(2)}, u32[]{:S(2)}) collective-permute-start(bf16[544,256]{1,0:T(8,128)(2,1)S(1)} %collective-permute-done.refs_2_), channel_id=1, source_target_pairs={{0,2},{1,3},{2,0},{3,1},{4,6},{5,7},{6,4},{7,5},{8,10},{9,11},{10,... | collective-permute-start | bytes 835592 | tf_op jit(solution)/shard_map/ppermute | solution.py:389
  23.1 1.2 %copy-start.2 = (f32[8,256]{1,0:T(8,128)S(1)}, f32[8,256]{1,0:T(8,128)}, u32[]{:S(2)}) copy-start(f32[8,256]{1,0:T(8,128)} %far_ref.8) | copy-start | bytes 24580
  31.4 9.7 %copy-start.3 = (f32[8,256]{1,0:T(8,128)S(1)}, f32[8,256]{1,0:T(8,128)}, u32[]{:S(2)}) copy-start(f32[8,256]{1,0:T(8,128)} %far_ref.9) | copy-start | bytes 24580
